TPU v7x, 128 devices: a whole 4x4x4 slice. The times are simulated.
128 devices in a mesh: dp: 8 (over x_hi, y), vocab: 16 (over x_lo, z, core).
Axes of the slice: x: 4 (x_hi: 2, x_lo: 2; x = x_hi * 2 + x_lo), y: 4, z: 4, core: 2. Of those that a mesh axis runs over, the one named last changes fastest.
Arguments:
- hidden: bfloat16 [8192, 4096], P('dp', 'vocab'), may hold values from -6 to 6
- norm_gain: float32 [4096], replicated, may hold values from 0.5 to 3
- head_weight: bfloat16 [4096, 16000], P(None, 'vocab')
- lengths: int32 [64], P('dp'), may hold values from 16 to 128
- positives: int32 [16], P('dp'), may hold values from 0 to 47
- negatives: int32 [16, 2], P('dp'), may hold values from 0 to 47
Outputs:
- losses: float32 [3], replicated
- hidden_grad: bfloat16 [8192, 4096], P('dp', 'vocab')
- head_grad: bfloat16 [4096, 16000], P('dp', 'vocab')
- gain_grad: float32 [4096], P('vocab')
All inputs are finite; a program needn't handle non-finite values.
Results may differ from a plain program's by a relative error of at most 0.025.
Values may be sent and summed in bfloat16 or wider, within the bound.
No kernel may reach another device: no remote copies, remote signals or barrier semaphores. Data moves between devices by JAX's collectives and lax.ppermute only.
A program may use at most 128 MiB of HBM per device.

v0:
```python
import functools
import math

import jax
import jax.numpy as jnp
from jax import lax
from jax.experimental import pallas as pl
from jax.experimental.pallas import tpu as pltpu
from jax.sharding import Mesh, PartitionSpec as P

VOCAB = 16000
D = 4096
epsilon = 1e-05
sharpness = 80.0
flops_weight = 0.01

TOK = 1024
SEQ = 8
LEN = 128
TERMS = 1000
BLK = 256
ROWS_A = 560
ROWS_B = TERMS - ROWS_A
HALF = TOK // 2
PER = 2
SCORE_SCALE = 4.0 / math.sqrt(VOCAB)
COLS = ((0, 256), (256, 512), (512, 768), (768, 1000))
SIZES = {"xh": 2, "y": 4, "xl": 2, "z": 4, "c": 2}
VMEM_LIMIT = 67_000_000
HIGHEST = lax.Precision.HIGHEST

f32, bf16 = jnp.float32, jnp.bfloat16


def shift(x, axis, step):
    n = SIZES[axis]
    return lax.ppermute(x, axis, [(i, (i + step) % n) for i in range(n)])


def swap(x, axis, bits=1):
    return lax.ppermute(x, axis, [(i, i ^ bits) for i in range(SIZES[axis])])


def params(**more):
    return pltpu.CompilerParams(vmem_limit_bytes=VMEM_LIMIT, **more)


def cost(flops, moved, weight=0.02):
    return pl.CostEstimate(flops=int(flops * weight), bytes_accessed=int(moved * weight), transcendentals=0)


def tag(ids, pooled_ref):
    lane = lax.broadcasted_iota(jnp.int32, (1, 24), 1)
    for k in range(SEQ):
        tags = jnp.zeros((1, 24), f32)
        if k < 2:
            tags = jnp.where(lane == 0, ids[8 + k].astype(f32), tags)
            tags = jnp.where(lane == 1, ids[10 + 2 * k].astype(f32), tags)
            tags = jnp.where(lane == 2, ids[11 + 2 * k].astype(f32), tags)
        pooled_ref[k : k + 1, TERMS:] = tags


def pool(lengths, first, acc, ssq, inv_ref, weight_ref, pooled_ref):
    for s in range(acc.shape[0] // LEN):
        k = first + s
        rows = slice(s * LEN, (s + 1) * LEN)
        total = jnp.sum(ssq[rows, :], axis=1, keepdims=True)
        inverse = lax.rsqrt(total / D + epsilon)
        inv_ref[rows, :] = inverse
        count = lengths[k]
        for a, b in COLS:
            logits = acc[rows, a:b] * inverse
            valid = lax.broadcasted_iota(jnp.int32, (LEN, b - a), 0) < count
            held = jnp.where(valid, 1.0 + jnp.maximum(logits, 0.0), 1.0)
            top = jnp.max(held, axis=0, keepdims=True)
            down = 1.0 / top
            r1 = held * down
            r2 = r1 * r1
            r4 = r2 * r2
            r8 = r4 * r4
            r16 = r8 * r8
            r32 = r16 * r16
            r79 = (r32 * r32 * r8) * (r4 * (r2 * r1))
            summed = jnp.sum(jnp.where(valid, r79 * r1, 0.0), axis=0, keepdims=True)
            pooled_ref[pl.ds(k, 1), a:b] = jnp.log(top) + jnp.log(summed) / sharpness
            slope = r79 * (down / summed) * inverse
            weight_ref[rows, a:b] = jnp.where(valid & (logits > 0.0), slope, 0.0).astype(bf16)


def chip_of(ids, far_x, step):
    return (ids[2] ^ far_x) * 4 + ((ids[3] + step) & 3)


def block_at(ids, chip, side):
    return pl.ds(pl.multiple_of((chip * 2 + (ids[4] ^ side)) * BLK, BLK), BLK)


def scaled(weights, gain, ids, chip):
    row = jnp.concatenate([gain[:, block_at(ids, chip, side)] for side in range(2)], axis=1)
    return (weights.astype(f32) * row).astype(bf16)


def folded_squares(lefts):
    squares = 0.0
    for left in lefts:
        value = left.astype(f32)
        square = value * value
        squares = squares + square[:, :128] + square[:, 128:]
    return squares


def forward_kernel(places, first, ids, *refs):
    nb = len(places)
    arrays, (weights, gain), refs = refs[: 2 * nb], refs[2 * nb : 2 * nb + 2], refs[2 * nb + 2 :]
    if not first:
        (acc_in, ssq_in, _), refs = refs[:3], refs[3:]
    acc, ssq, kept, held, w_sem, x_sem = refs
    chips = [chip_of(ids, *place) for place in places]
    loads, saves = [], []
    for j in range(nb):
        for side in range(2):
            at = held.at[j, :, side * BLK : (side + 1) * BLK]
            loads.append(pltpu.make_async_copy(weights.at[:, block_at(ids, chips[j], side)], at, w_sem.at[j, side]))
            loads[-1].start()
    for j in range(nb):
        for side in range(2):
            saves.append(pltpu.make_async_copy(arrays[2 * j + side], kept.at[chips[j], side], x_sem.at[j, side]))
            saves[-1].start()
    for j in range(nb):
        loads[2 * j].wait()
        loads[2 * j + 1].wait()
        right = scaled(held[j], gain, ids, chips[j])
        for half in range(2):
            rows = slice(half * HALF, (half + 1) * HALF)
            lefts = [arrays[2 * j + side][rows, :] for side in range(2)]
            squares = folded_squares(lefts)
            product = lax.dot_general(
                jnp.concatenate(lefts, axis=1), right, (((1,), (1,)), ((), ())), preferred_element_type=f32
            )
            if j == 0 and first:
                acc[rows, :] = product
                ssq[rows, :] = squares
            elif j == 0:
                acc[rows, :] = acc_in[rows, :] + product
                ssq[rows, :] = ssq_in[rows, :] + squares
            else:
                acc[rows, :] += product
                ssq[rows, :] += squares
    for copy in saves:
        copy.wait()


SMEM = pl.BlockSpec(memory_space=pltpu.SMEM)
VMEM = pl.BlockSpec(memory_space=pltpu.VMEM)
ANY = pl.BlockSpec(memory_space=pl.ANY)


STATE = [
    jax.ShapeDtypeStruct((TOK, TERMS), f32),
    jax.ShapeDtypeStruct((TOK, 128), f32),
    jax.ShapeDtypeStruct((8, 2, TOK, BLK), bf16),
]


def forward(ids, places, arrays, weights, gain, state=()):
    nb = len(places)
    base = 3 + len(arrays)
    return pl.pallas_call(
        functools.partial(forward_kernel, places, not state),
        out_shape=STATE,
        in_specs=[SMEM] + [VMEM] * len(arrays) + [ANY, VMEM] + [VMEM, VMEM, ANY][: len(state)],
        out_specs=[VMEM, VMEM, ANY],
        scratch_shapes=[
            pltpu.VMEM((nb, TERMS, 2 * BLK), bf16),
            pltpu.SemaphoreType.DMA((nb, 2)),
            pltpu.SemaphoreType.DMA((nb, 2)),
        ],
        input_output_aliases={base + i: i for i in range(len(state))},
        compiler_params=params(),
        cost_estimate=cost(2 * nb * TOK * 512 * TERMS, nb * 3_000_000 + 8_000_000),
        name="forward_part",
    )(ids, *arrays, weights, gain, *state)


STEP = 256


def forward_last_kernel(place, ids, lengths, a0, a1, w0, w1, gain, acc_in, ssq_in, _, *refs):
    product, kept, inv_ref, weight_ref, pooled_ref, acc, right, ssq, sem = refs
    k = pl.program_id(0)
    chip = chip_of(ids, *place)

    @pl.when(k == 0)
    def _():
        right[...] = scaled(jnp.concatenate([w0[...], w1[...]], axis=1), gain, ids, chip)
        tag(ids, pooled_ref)

    rows = pl.ds(pl.multiple_of(k * STEP, STEP), STEP)
    saves = []
    for side, source in enumerate((a0, a1)):
        saves.append(pltpu.make_async_copy(source, kept.at[chip, side, rows, :], sem.at[side]))
        saves[-1].start()
    lefts = [a0[...], a1[...]]
    ssq[...] = ssq_in[...] + folded_squares(lefts)
    acc[...] = acc_in[...] + lax.dot_general(
        jnp.concatenate(lefts, axis=1), right[...], (((1,), (1,)), ((), ())), preferred_element_type=f32
    )
    product[...] = acc[...].astype(bf16)
    pool(lengths, k * (STEP // LEN), acc, ssq, inv_ref, weight_ref, pooled_ref)
    for copy in saves:
        copy.wait()


def forward_last(ids, lengths, place, arrays, weights, gain, state):
    whole = lambda k, *s: (0, 0)
    rows = lambda k, *s: (k, 0)
    sides = [
        pl.BlockSpec((TERMS, BLK), lambda k, s, n, side=side: (0, chip_of(s, *place) * 2 + (s[4] ^ side)))
        for side in range(2)
    ]
    return pl.pallas_call(
        functools.partial(forward_last_kernel, place),
        out_shape=[
            jax.ShapeDtypeStruct((TOK, TERMS), bf16),
            STATE[2],
            jax.ShapeDtypeStruct((TOK, 1), f32),
            jax.ShapeDtypeStruct((TOK, TERMS), bf16),
            jax.ShapeDtypeStruct((SEQ, 1024), f32),
        ],
        grid_spec=pltpu.PrefetchScalarGridSpec(
            num_scalar_prefetch=2,
            grid=(TOK // STEP,),
            in_specs=[pl.BlockSpec((STEP, BLK), rows)] * 2
            + [*sides, pl.BlockSpec((1, D), whole)]
            + [pl.BlockSpec((STEP, TERMS), rows), pl.BlockSpec((STEP, 128), rows), ANY],
            out_specs=[
                pl.BlockSpec((STEP, TERMS), rows),
                ANY,
                pl.BlockSpec((STEP, 1), rows),
                pl.BlockSpec((STEP, TERMS), rows),
                pl.BlockSpec((SEQ, 1024), whole),
            ],
            scratch_shapes=[
                pltpu.VMEM((STEP, TERMS), f32),
                pltpu.VMEM((TERMS, 2 * BLK), bf16),
                pltpu.VMEM((STEP, 128), f32),
                pltpu.SemaphoreType.DMA((2,)),
            ],
        ),
        input_output_aliases={9: 1},
        compiler_params=params(),
        cost_estimate=cost(2 * TOK * 512 * TERMS, 20_000_000),
        name="forward_last",
    )(ids, lengths, *arrays, weights, weights, gain, *state)


def touch_kernel(*refs):
    pass


def touch(after, *arrays):
    n = len(arrays)
    return pl.pallas_call(
        touch_kernel,
        out_shape=[jax.ShapeDtypeStruct(a.shape, a.dtype) for a in arrays],
        in_specs=[ANY] * (n + 1),
        out_specs=[ANY] * n,
        input_output_aliases={i + 1: i for i in range(n)},
        compiler_params=params(has_side_effects=True),
        cost_estimate=cost(1000, 1000),
        name="touch",
    )(after, *arrays)


def gram_kernel(ids, *refs):
    all_ref, part_ref = refs[4:]
    for bits, ref in enumerate(refs[:4]):
        for m in range(2):
            at = (ids[0] * 4 + ids[1]) ^ (4 * m + bits)
            all_ref[pl.ds(pl.multiple_of(at * SEQ, SEQ), SEQ), :] = ref[m]
    every = all_ref[:, :TERMS]
    part = lax.dot_general(every, every, (((1,), (1,)), ((), ())), precision=HIGHEST, preferred_element_type=f32)
    mean = jnp.sum(every, axis=0, keepdims=True) / 64.0
    flops = jnp.sum(mean * mean, axis=1, keepdims=True)
    part_ref[...] = jnp.zeros_like(part_ref)
    part_ref[0:64, 0:64] = part
    part_ref[64:72, :] = jnp.broadcast_to(flops, (8, 128))


def gram(ids, groups):
    return pl.pallas_call(
        gram_kernel,
        out_shape=[jax.ShapeDtypeStruct((64, 1024), f32), jax.ShapeDtypeStruct((72, 128), f32)],
        grid_spec=pltpu.PrefetchScalarGridSpec(
            num_scalar_prefetch=1,
            grid=(),
            in_specs=[VMEM] * 4,
            out_specs=[VMEM] * 2,
        ),
        compiler_params=params(),
        name="gram",
    )(ids, *groups)


def contrast(every, parts, scaled_ref, losses_ref):
    sums = (parts[0][...] + parts[1][...]) + (parts[2][...] + parts[3][...])
    scores = sums[0:64, :] * SCORE_SCALE
    row = lax.broadcasted_iota(jnp.int32, (64, 128), 0)
    col = lax.broadcasted_iota(jnp.int32, (64, 128), 1)
    is_query = (row & 7) < 2
    is_passage = ((col & 7) >= 2) & (col < 64)
    tags = every[:, TERMS:]

    def hot(at):
        index = tags[:, at : at + 1]
        group = jnp.floor((index + 0.5) * (1.0 / 6.0))
        place = group * 8.0 + 2.0 + (index - 6.0 * group)
        return (col.astype(f32) == place).astype(f32)

    positive, negatives = hot(0), (hot(1), hot(2))
    highest = jnp.max(jnp.where(is_passage, scores, -3e38), axis=1, keepdims=True)
    shifted = jnp.where(is_passage, jnp.exp(jnp.minimum(scores - highest, 0.0)), 0.0)
    denominator = jnp.sum(shifted, axis=1, keepdims=True)
    log_total = highest + jnp.log(denominator)
    positive_score = jnp.sum(scores * positive, axis=1, keepdims=True)
    query_row = is_query[:, 0:1]
    cross = jnp.sum(jnp.where(query_row, log_total - positive_score, 0.0), axis=0, keepdims=True) / 16.0
    grad = (shifted / denominator - positive) / 16.0
    margin = jnp.zeros((1, 1), f32)
    for negative in negatives:
        gap = jnp.sum(scores * negative, axis=1, keepdims=True) - positive_score
        small = jnp.exp(-jnp.abs(gap))
        soft = jnp.maximum(gap, 0.0) + jnp.log(1.0 + small)
        slope = jnp.where(gap >= 0.0, 1.0, small) / (1.0 + small) / 32.0
        margin = margin + jnp.sum(jnp.where(query_row, soft, 0.0), axis=0, keepdims=True) / 32.0
        grad = grad + slope * negative - slope * positive
    grad = jnp.where(is_query, grad, 0.0)
    square = jnp.concatenate([grad, jnp.zeros((64, 128), f32)], axis=0)
    scaled_ref[...] = (square + square.T) * SCORE_SCALE
    flops = sums[64:65, 0:1] * flops_weight
    lane = lax.broadcasted_iota(jnp.int32, (8, 128), 1)
    losses_ref[...] = jnp.where(lane == 0, cross, jnp.where(lane == 1, margin, flops))


def grad_kernel(
    ids, every, p0, p1, p2, p3, weight, acc, h_ref, ht_ref, dots, losses_ref, rep, scaled, padded
):
    k = pl.program_id(0)

    @pl.when(k == 0)
    def _():
        contrast(every, (p0, p1, p2, p3), scaled, losses_ref)
        dots[...] = jnp.zeros_like(dots)
        padded[0:64, :] = every[:, :TERMS]
        padded[64:128, :] = jnp.zeros((64, TERMS), f32)
        at = pl.multiple_of((ids[0] * 4 + ids[1]) * SEQ, SEQ)
        own = scaled[pl.ds(at, SEQ), :]
        mean = jnp.sum(padded[...], axis=0, keepdims=True) / 64.0
        rep[...] = jnp.dot(own, padded[...], precision=HIGHEST, preferred_element_type=f32) + (
            2.0 * flops_weight / 64.0
        ) * mean

    lines = []
    for s in range(PER):
        rows = slice(s * LEN, (s + 1) * LEN)
        folded = jnp.zeros((LEN, 128), f32)
        for a, b in COLS:
            grad = weight[rows, a:b].astype(f32) * rep[pl.ds(k * PER + s, 1), a:b]
            rounded = grad.astype(bf16)
            h_ref[rows, a:b] = rounded
            turned = grad.T.astype(bf16)
            ht_ref[a:b, rows] = turned
            product = rounded.astype(f32) * acc[rows, a:b].astype(f32)
            wide = b - a
            folded = folded + product[:, :128]
            if wide == 256:
                folded = folded + product[:, 128:]
            else:
                folded = folded + jnp.concatenate([product[:, 128:], jnp.zeros((LEN, 256 - wide), f32)], axis=1)
        lines.append(jnp.sum(folded.T, axis=0, keepdims=True))
    dots[pl.ds((k >> 1) * 8 + (k & 1), 1), :] = jnp.concatenate(lines, axis=1)


def grads(ids, every, parts, weight, acc):
    whole = lambda k, s: (0, 0)
    rows = lambda k, s: (k, 0)
    cols = lambda k, s: (0, k)
    return pl.pallas_call(
        grad_kernel,
        out_shape=[
            jax.ShapeDtypeStruct((TOK, TERMS), bf16),
            jax.ShapeDtypeStruct((TERMS, TOK), bf16),
            jax.ShapeDtypeStruct((16, BLK), f32),
            jax.ShapeDtypeStruct((8, 128), f32),
        ],
        grid_spec=pltpu.PrefetchScalarGridSpec(
            num_scalar_prefetch=1,
            grid=(SEQ // PER,),
            in_specs=[
                pl.BlockSpec((64, 1024), whole),
                *[pl.BlockSpec((72, 128), whole)] * 4,
                pl.BlockSpec((PER * LEN, TERMS), rows),
                pl.BlockSpec((PER * LEN, TERMS), rows),
            ],
            out_specs=[
                pl.BlockSpec((PER * LEN, TERMS), rows),
                pl.BlockSpec((TERMS, PER * LEN), cols),
                pl.BlockSpec((16, BLK), whole),
                pl.BlockSpec((8, 128), whole),
            ],
            scratch_shapes=[pltpu.VMEM((SEQ, TERMS), f32), pltpu.VMEM((128, 128), f32), pltpu.VMEM((128, TERMS), f32)],
        ),
        compiler_params=params(),
        cost_estimate=cost(20 * TOK * TERMS, 12_000_000),
        name="logit_grad",
    )(ids, every, *parts, weight, acc)


def later(count, kernel):
    return lambda ids, *refs: kernel(ids, *refs[count:])


def place_of(steps, n):
    step = steps[0]
    for i in range(1, len(steps)):
        step = jnp.where(n < 2 * i, step, steps[i])
    return step, n & 1


def head_chip(steps, ids, n):
    step, j = place_of(steps, n)
    return (ids[0] ^ j) * 4 + ((ids[1] + step) & 3)


def head_kernel(steps, split, n_add, ids, ht, x, gain, *refs):
    n = pl.program_id(0)
    adds, outs, (keep, send) = refs[:n_add], refs[n_add:-2], refs[-2:]
    block = jnp.concatenate([x[0, 0], x[0, 1]], axis=1)
    chip = head_chip(steps, ids, n)
    row = jnp.concatenate([gain[:, block_at(ids, chip, side)] for side in range(2)], axis=1)
    total = jnp.dot(ht[...], block, preferred_element_type=f32) * row
    sides = [total[:, :BLK], total[:, BLK:]]
    for i in range(len(steps)):

        @pl.when((n >> 1) == i)
        def _(i=i):
            for side in range(2):
                share = sides[side][:ROWS_A]
                if n_add and side == i:
                    share = share + adds[i][0].astype(f32)
                if split:
                    outs[side][0] = share.astype(bf16)
                else:
                    outs[i][0, side] = share.astype(bf16)

    for j, out in enumerate((keep, send)):

        @pl.when((n & 1) == j)
        def _(out=out):
            for side in range(2):
                out[0, side] = sides[side][ROWS_A:].astype(bf16)


def head_part(ids, steps, ht, x, gain, after, split=False, adds=(), weight=0.02):
    count = len(steps)
    at = lambda i: lambda n, s: (jnp.clip(n - 2 * i, 0, 1), 0, 0)
    at4 = lambda i: lambda n, s: (jnp.clip(n - 2 * i, 0, 1), 0, 0, 0)
    one = pl.BlockSpec((1, ROWS_A, BLK), at(0))
    low = pl.BlockSpec((1, 2, ROWS_B, BLK), lambda n, s: (n // 2, 0, 0, 0))
    if split:
        high, specs = [jax.ShapeDtypeStruct((2, ROWS_A, BLK), bf16)] * 2, [one, one]
    else:
        high = [jax.ShapeDtypeStruct((2, 2, ROWS_A, BLK), bf16)] * count
        specs = [pl.BlockSpec((1, 2, ROWS_A, BLK), at4(i)) for i in range(count)]
    return pl.pallas_call(
        later(len(after), functools.partial(head_kernel, steps, split, len(adds))),
        out_shape=high + [jax.ShapeDtypeStruct((count, 2, ROWS_B, BLK), bf16)] * 2,
        grid_spec=pltpu.PrefetchScalarGridSpec(
            num_scalar_prefetch=1,
            grid=(2 * count,),
            in_specs=[ANY] * len(after)
            + [
                pl.BlockSpec((TERMS, TOK), lambda n, s: (0, 0)),
                pl.BlockSpec((1, 2, TOK, BLK), lambda n, s: (head_chip(steps, s, n), 0, 0, 0)),
                pl.BlockSpec((1, D), lambda n, s: (0, 0)),
            ]
            + [pl.BlockSpec((1, ROWS_A, BLK), at(i)) for i in range(len(adds))],
            out_specs=specs + [low, low],
        ),
        compiler_params=params(),
        cost_estimate=cost(2 * TERMS * TOK * 1024 * count, 2 * TERMS * TOK + 2048 * count * (TOK + TERMS), weight),
        name="head_part",
    )(ids, *after, ht, x, gain, *adds)


def low_sum_kernel(_, a, b, *outs):
    for i, out in enumerate(outs):
        out[...] = (a[i].astype(f32) + b[i].astype(f32)).astype(bf16)


def low_sum(after, a, b):
    return pl.pallas_call(
        low_sum_kernel,
        out_shape=[jax.ShapeDtypeStruct((2, ROWS_B, BLK), bf16)] * a.shape[0],
        in_specs=[ANY, VMEM, VMEM],
        out_specs=[VMEM] * a.shape[0],
        compiler_params=params(),
        cost_estimate=cost(1000, 3_000_000),
        name="low_sum",
    )(after, a, b)


def join_kernel(ids, _, a0, ra, rb, got, keep, swapped, b1, b2, b3, out):
    for side in range(2):
        cols = pl.ds(pl.multiple_of((ids[4] ^ side) * BLK, BLK), BLK)
        total = a0[0, side].astype(f32) + ra[0, side].astype(f32) + rb[0, side].astype(f32) + got[side].astype(f32)
        out[0:ROWS_A, cols] = total.astype(bf16)
        total = keep[0, side].astype(f32) + swapped[0, side].astype(f32)
        for b in (b1, b2, b3):
            total = total + b[side].astype(f32)
        out[ROWS_A:TERMS, cols] = total.astype(bf16)


def join(ids, after, *parts):
    return pl.pallas_call(
        join_kernel,
        out_shape=jax.ShapeDtypeStruct((TERMS, 2 * BLK), bf16),
        in_specs=[SMEM, ANY] + [VMEM] * len(parts),
        out_specs=VMEM,
        compiler_params=params(),
        cost_estimate=cost(1000, 8_000_000),
        name="join",
    )(ids, after, *parts)


ROWS_T = HALF + 16


def term_step(steps, n):
    step = steps[0]
    for i in range(1, len(steps)):
        step = jnp.where(n < i, step, steps[i])
    return step


def term_kernel(n_steps, split, n_adds, ids, h, w0, w1, dots, *refs):
    n = pl.program_id(0)
    crossed, adds, outs = refs[: n_adds[0]], refs[n_adds[0] : sum(n_adds)], refs[sum(n_adds) :]
    weights = jnp.concatenate([w0[...], w1[...]], axis=1)
    for half in range(2):
        total = jnp.dot(h[half * HALF : (half + 1) * HALF, :], weights, preferred_element_type=f32)
        tail = jnp.concatenate([dots[half * 8 : half * 8 + 8, :], jnp.zeros((8, BLK), f32)], axis=0)
        for m in range(2):
            share = jnp.concatenate([total[:, m * BLK : (m + 1) * BLK], tail], axis=0)
            for ref in crossed:
                share = share + ref[0, half, m].astype(f32)
            if adds:
                got = adds[half][m].astype(f32)
                share = share + jnp.where(n == half, got, 0.0)
            if split:
                outs[half][m] = share.astype(bf16)
            elif len(outs) == 1:
                outs[0][0, half, m] = share.astype(bf16)
            else:
                for i in range(n_steps):

                    @pl.when(n == i)
                    def _(i=i, half=half, m=m, share=share):
                        outs[i][half, m] = share.astype(bf16)


def term_part(ids, steps, side, h, wt, dots, after, split=False, apart=False, crossed=(), adds=(), weight=0.02):
    block = pl.BlockSpec((1, 2, 2, ROWS_T, BLK), lambda n, s: (n, 0, 0, 0, 0))
    part = pl.BlockSpec((2, ROWS_T, BLK), lambda n, s: (0, 0, 0))
    sides = [
        pl.BlockSpec(
            (TERMS, BLK), lambda n, s, m=m: (0, ((s[2] ^ m) * 4 + ((s[3] + term_step(steps, n)) & 3)) * 2 + (s[4] ^ side))
        )
        for m in range(2)
    ]
    count = len(steps)
    outs, specs = [jax.ShapeDtypeStruct((count, 2, 2, ROWS_T, BLK), bf16)], [block]
    if split:
        outs, specs = [jax.ShapeDtypeStruct((2, ROWS_T, BLK), bf16)] * 2, [part] * 2
    elif apart:
        outs = [jax.ShapeDtypeStruct((2, 2, ROWS_T, BLK), bf16)] * count
        specs = [pl.BlockSpec((2, 2, ROWS_T, BLK), lambda n, s: (0, 0, 0, 0))] * count
    return pl.pallas_call(
        later(len(after), functools.partial(term_kernel, count, split, (len(crossed), len(adds)))),
        out_shape=outs,
        grid_spec=pltpu.PrefetchScalarGridSpec(
            num_scalar_prefetch=1,
            grid=(count,),
            in_specs=[ANY] * len(after)
            + [pl.BlockSpec((TOK, TERMS), lambda n, s: (0, 0)), *sides]
            + [pl.BlockSpec((16, BLK), lambda n, s: (0, 0))]
            + [block] * len(crossed)
            + [part] * len(adds),
            out_specs=specs,
        ),
        compiler_params=params(),
        cost_estimate=cost(
            4 * count * TOK * BLK * TERMS, 2 * TOK * TERMS + 2 * count * BLK * (2 * TERMS + 4 * TOK), weight
        ),
        name="term_part",
    )(ids, *after, h, wt, wt, dots, *crossed, *adds)


def term_sum_kernel(own, ra, rb, x, x_p, keep, send, dots, gain):
    sums = [jnp.zeros((8, BLK), f32) for _ in range(2)]
    for half in range(2):
        for m, values in ((0, x), (1, x_p)):
            for first in range(0, ROWS_T, 128):
                rows = slice(first, min(first + 128, ROWS_T))
                total = own[half, m, rows, :].astype(f32)
                for ref in (ra, rb):
                    total = total + ref[half, m, rows, :].astype(f32)
                if m:
                    send[half, rows, :] = total.astype(bf16)
                elif first < HALF:
                    keep[half * HALF + first : half * HALF + first + 128, :] = total.astype(bf16)
                else:
                    dots[half * 8 : half * 8 + 8, :] = total[:8]
                if first < HALF:
                    at = half * HALF + first
                    product = total * values[at : at + 128, :].astype(f32)
                    sums[m] = sums[m] + jnp.sum(product.reshape(16, 8, BLK), axis=0)
    gain[...] = jnp.sum(sums[0], axis=0, keepdims=True)
    other = jnp.sum(sums[1], axis=0, keepdims=True)
    high = other.astype(bf16).astype(f32)
    row = lax.broadcasted_iota(jnp.int32, (16, 1), 0)
    tail = send[0, HALF:, :].astype(f32)
    tail = jnp.where(row == 2, high, jnp.where(row == 3, other - high, tail))
    send[0, HALF:, :] = tail.astype(bf16)


def term_sum(after, own, ra, rb, x, x_p):
    count = len(after)
    return pl.pallas_call(
        lambda *refs: term_sum_kernel(*refs[count:]),
        out_shape=[
            jax.ShapeDtypeStruct((TOK, BLK), bf16),
            jax.ShapeDtypeStruct((2, ROWS_T, BLK), bf16),
            jax.ShapeDtypeStruct((16, BLK), f32),
            jax.ShapeDtypeStruct((1, BLK), f32),
        ],
        in_specs=[ANY] * count + [VMEM] * 5,
        out_specs=[VMEM] * 4,
        compiler_params=params(),
        cost_estimate=cost(1_000_000, 5_000_000),
        name="term_sum",
    )(*after, own, ra, rb, x, x_p)


def final_kernel(ids, n_ref, got, x_ref, gain, inv_ref, dots, sums, out, sums_out):
    tail = got[0, HALF:, :].astype(f32)
    sums_out[...] = sums[...] + tail[2:3] + tail[3:4]
    g = gain[:, block_at(ids, ids[2] * 4 + ids[3], 0)]
    for half in range(2):
        lines = (dots[half * 8 : half * 8 + 8, :] + got[half, HALF:, :].astype(f32)[:8]) / D
        for k in range(4):
            local = slice(k * LEN, (k + 1) * LEN)
            rows = slice(half * HALF + k * LEN, half * HALF + (k + 1) * LEN)
            grad = n_ref[rows, :].astype(f32) + got[half, local, :].astype(f32)
            values = x_ref[rows, :].astype(f32)
            line = lines[k // 2 : k // 2 + 1, (k % 2) * LEN : (k % 2 + 1) * LEN]
            column = jnp.broadcast_to(line, (LEN, LEN)).T[:, 0:1]
            inverse = inv_ref[rows, :]
            out[rows, :] = (grad * g - values * (inverse * inverse * column)).astype(bf16)


def final(ids, after, n, got, x, gain, inv, dots, sums):
    return pl.pallas_call(
        later(len(after), final_kernel),
        out_shape=[jax.ShapeDtypeStruct((TOK, BLK), bf16), jax.ShapeDtypeStruct((1, BLK), f32)],
        in_specs=[SMEM] + [ANY] * len(after) + [VMEM] * 7,
        out_specs=[VMEM] * 2,
        compiler_params=params(),
        cost_estimate=cost(1_000_000, 2_000_000),
        name="hidden_grad",
    )(ids, *after, n, got, x, gain, inv, dots, sums)


def gain_sum_kernel(_, a, b, out):
    out[...] = a[...] + b[...]


def gain_sum(after, a, b):
    return pl.pallas_call(
        gain_sum_kernel,
        out_shape=jax.ShapeDtypeStruct((1, BLK), f32),
        in_specs=[ANY] + [VMEM] * 2,
        out_specs=VMEM,
        compiler_params=params(),
        cost_estimate=cost(1000, 5000),
        name="gain_sum",
    )(after, a, b)


def shards(hidden, norm_gain, head_weight, lengths, positives, negatives):
    xh, y, xl, z, c = (lax.axis_index(a).astype(jnp.int32) for a in ("xh", "y", "xl", "z", "c"))
    nil = jnp.int32(0)
    ids = jnp.concatenate([jnp.stack([xh, y, xl, z, c, nil, nil, nil]), positives, negatives.reshape(-1)])
    wt = head_weight.T
    gain = norm_gain.reshape(1, D)

    z_m, z_p, x_p = shift(hidden, "z", 1), shift(hidden, "z", -1), swap(hidden, "xl")
    own_c = swap(hidden, "c")
    z_m_c, z_p_c, x_p_c = (swap(a, "c") for a in (z_m, z_p, x_p))
    far, xz_p, xz_m = shift(z_m, "z", 1), shift(x_p, "z", -1), swap(z_m, "xl")
    state = forward(ids, [(0, 0), (0, -1), (1, 0)], [hidden, own_c, z_m, z_m_c, x_p, x_p_c], wt, gain)
    far, xz_p, xz_m = touch(state[1], far, xz_p, xz_m)
    last = swap(far, "xl")
    far_c, xz_p_c, xz_m_c = (swap(a, "c") for a in (far, xz_p, xz_m))
    state = forward(
        ids,
        [(0, 1), (0, 2), (1, 1), (1, -1)],
        [z_p, z_p_c, far, far_c, xz_p, xz_p_c, xz_m, xz_m_c],
        wt,
        gain,
        state,
    )
    (last,) = touch(state[1], last)
    last_c = swap(last, "c")
    acc, x, inv, weight, pooled = forward_last(ids, lengths, (1, 2), (last, last_c), wt, gain, state)

    pair = jnp.stack([pooled, swap(pooled, "xh")])
    every, part = gram(ids, [pair] + [swap(pair, "y", bits) for bits in (1, 2, 3)])
    part = (part + swap(part, "z", 1)) + (swap(part, "z", 2) + swap(part, "z", 3))
    both = lax.ppermute(part, ("xl", "c"), [(i, i ^ 3) for i in range(4)])
    parts = (part, swap(part, "c"), swap(part, "xl"), both)
    h, ht, dots, losses = grads(ids, every, parts, weight, acc)

    (crossing_2,) = term_part(ids, (2,), 1, h, wt, dots, ())
    (crossing,) = term_part(ids, (1, 3, 0), 1, h, wt, dots, (crossing_2,), weight=20)
    crossed_2, crossed = swap(crossing_2, "c"), swap(crossing, "c")
    term_0, term_1 = term_part(ids, (2,), 0, h, wt, dots, (crossing,), split=True, crossed=(crossed_2,))
    far_0, far_1, keep_2, send_2 = head_part(ids, (2,), ht, x, gain, (term_0,), split=True, weight=20)
    swap_2 = swap(send_2, "xh")
    adds = (shift(term_0, "z", 1), shift(term_1, "z", -1))
    t_1, t_3, t_0 = term_part(
        ids, (1, 3, 0), 0, h, wt, dots, (far_0,), apart=True, crossed=(crossed,), adds=adds, weight=20
    )
    adds = (shift(far_0, "y", 1), shift(far_1, "y", -1))
    a_1, a_3, keep_13, send_13 = head_part(ids, (1, 3), ht, x, gain, (t_0, swap_2), adds=adds, weight=20)
    swap_13 = swap(send_13, "xh")
    ra, rb = shift(a_1, "y", 1), shift(a_3, "y", -1)
    a_0, keep_0, send_0 = head_part(ids, (0,), ht, x, gain, (a_1,))
    keep, send, dots, partial = term_sum((keep_0,), t_0, shift(t_1, "z", 1), shift(t_3, "z", -1), hidden, x_p)
    swap_0 = swap(send_0, "xh")
    got = swap(a_0[1] + ra[1] + rb[1], "xh")
    low_1, low_3 = low_sum(keep, keep_13, swap_13)
    low = [shift(low_1, "y", 1), shift(keep_2[0] + swap_2[0], "y", 2), shift(low_3, "y", 3)]
    hidden_grad, gain_grad = final(ids, low, keep, swap(send, "xl"), hidden, gain, inv, dots, partial)
    gain_grad = (gain_grad + swap(gain_grad, "y", 1)) + (swap(gain_grad, "y", 2) + swap(gain_grad, "y", 3))
    head_t = join(ids, hidden_grad, a_0, ra, rb, got, keep_0, swap_0, *low)
    return losses[0, :3], hidden_grad, head_t.T, gain_sum(head_t, gain_grad, swap(gain_grad, "xh"))[0]


def solution(mesh):
    fine = Mesh(mesh.devices.reshape(2, 4, 2, 4, 2), ("xh", "y", "xl", "z", "c"))
    dp, vocab = ("xh", "y"), ("xl", "z", "c")
    in_specs = (P(dp, vocab), P(), P(None, vocab), P(dp), P(dp), P(dp, None))
    out_specs = (P(), P(dp, vocab), P(dp, vocab), P(vocab))
    return jax.shard_map(shards, mesh=fine, in_specs=in_specs, out_specs=out_specs, check_vma=False)
```

profile of v0, /device:TPU:0, one launch (start us, length us, event | category | flops | bytes accessed | tf_op | source)
XLA Modules:
  0.0 234.2 jit_solution(4271569276027330542)
XLA Ops:
  0.6 2.1 collective-permute-start.3
  2.7 1.5 collective-permute-start.5
  4.2 2.2 collective-permute-start
  6.4 10.7 %collective-permute-done.3.refs_2_ = bf16[1024,256]{1,0:T(8,128)(2,1)} collective-permute-done((bf16[1024,256]{1,0:T(8,128)(2,1)}, bf16[1024,256]{1,0:T(8,128)(2,1)}, u32[]{:S(2)}, u32[]{:S(2)}) %collective-permute-start.3) | collective-permute-done | bytes 524320 | tf_op jit(solution)/shard_map/ppermute | solution.py:37
  18.3 2.5 %collective-permute-start.8 = (bf16[1024,256]{1,0:T(8,128)(2,1)}, bf16[1024,256]{1,0:T(8,128)(2,1)}, u32[]{:S(2)}, u32[]{:S(2)}) collective-permute-start(bf16[1024,256]{1,0:T(8,128)(2,1)} %collective-permute-done.5.refs_4_.refs_5_), channel_id=1, source_target_pairs={{0,6},{2,0},{4,2},{6,4},{1,7},{3,1},{5,3},{7,5},{8,14},{10,8},{12,... | collective-permute-start | bytes 1572872 | tf_op jit(solution)/shard_map/ppermute | solution.py:37
  20.8 1.5 collective-permute-start.9
  24.4 10.0 %forward_part.2 = (f32[1024,1000]{1,0:T(8,128)}, f32[1024,128]{1,0:T(8,128)}, bf16[8,2,1024,256]{3,2,1,0:T(8,128)(2,1)}) custom-call(s32[14]{0:T(128)} %concatenate.3.ids, bf16[1024,256]{1,0:T(8,128)(2,1)} %refs_5_.1, bf16[1024,256]{1,0:T(8,128)(2,1)} %collective-permute-done.2.refs_1_, bf16[1024,256]{1,0:T(8,128)(2,1)} %collective-permute-done.3.refs_2_, ...), custom_call_target="tpu_custom_call" | custom-call | flops 62914560 | bytes 340000 | tf_op jit(solution)/shard_map/forward_part/pallas_call | solution.py:168
  38.4 13.1 %forward_part.3 = (f32[1024,1000]{1,0:T(8,128)}, f32[1024,128]{1,0:T(8,128)}, bf16[8,2,1024,256]{3,2,1,0:T(8,128)(2,1)}) custom-call(s32[14]{0:T(128)} %concatenate.3.ids, bf16[1024,256]{1,0:T(8,128)(2,1)} %collective-permute-done.refs_0_, ...), custom_call_target="tpu_custom_call", output_to_operand_aliasing={{0}: (11, {}), {1}: (12, {}), {2}: (13, {})} | custom-call | flops 83886080 | bytes 400000 | tf_op jit(solution)/shard_map/forward_part/pallas_call | solution.py:168
  52.0 1.9 collective-permute-done.14.a1
  53.9 12.2 %forward_last.1 = (bf16[1024,1000]{1,0:T(8,128)(2,1)}, bf16[8,2,1024,256]{3,2,1,0:T(8,128)(2,1)}, f32[1024,1]{1,0:T(8,128)}, bf16[1024,1000]{1,0:T(8,128)(2,1)}, f32[8,1024]{1,0:T(8,128)}) custom-call(s32[14]{0:T(128)} %concatenate.3.ids, s32[8]{0:T(128)} %lengths.1, bf16[1024,256]{1,0:T(8,128)(2,1)} %touch.3.a0, ...), custom_call_target="tpu_custom_call", output_to_operand_aliasing={{1}: (9, {})} | custom-call | flops 20971520 | bytes 400000 | tf_op jit(solution)/shard_map/forward_last/pallas_call | solution.py:221
  66.1 2.8 %collective-permute-start.15 = (f32[8,1024]{1,0:T(8,128)}, f32[8,1024]{1,0:T(8,128)S(1)}, u32[]{:S(2)}, u32[]{:S(2)}) collective-permute-start(f32[8,1024]{1,0:T(8,128)} %get-tuple-element.57), channel_id=1, source_target_pairs={{0,64},{64,0},{1,65},{65,1},{2,66},{66,2},{3,67},{67,3},{4,68},{68... | collective-permute-start | bytes 98312 | tf_op jit(solution)/shard_map/ppermute | solution.py:41
  68.9 2.9 %collective-permute-done.15 = f32[8,1024]{1,0:T(8,128)S(1)} collective-permute-done((f32[8,1024]{1,0:T(8,128)}, f32[8,1024]{1,0:T(8,128)S(1)}, u32[]{:S(2)}, u32[]{:S(2)}) %collective-permute-start.15) | collective-permute-done | bytes 32800 | tf_op jit(solution)/shard_map/ppermute | solution.py:41
  72.6 1.6 collective-permute-start.16
  74.2 2.9 %collective-permute-start.17 = (f32[2,8,1024]{2,1,0:T(8,128)S(1)}, f32[2,8,1024]{2,1,0:T(8,128)S(1)}, u32[]{:S(2)}, u32[]{:S(2)}) collective-permute-start(f32[2,8,1024]{2,1,0:T(8,128)S(1)} %pad_maximum_fusion.refs_0_), channel_id=1, source_target_pairs={{0,32},{16,48},{32,0},{48,16},{1,33},{17,49},{33,1},{49,17},{2,34}... | collective-permute-start | bytes 196616 | tf_op jit(solution)/shard_map/ppermute | solution.py:41
  77.3 2.8 %collective-permute-done.17.refs_2_ = f32[2,8,1024]{2,1,0:T(8,128)S(1)} collective-permute-done((f32[2,8,1024]{2,1,0:T(8,128)S(1)}, f32[2,8,1024]{2,1,0:T(8,128)S(1)}, u32[]{:S(2)}, u32[]{:S(2)}) %collective-permute-start.17) | collective-permute-done | bytes 65568 | tf_op jit(solution)/shard_map/ppermute | solution.py:41
  80.7 2.0 collective-permute-done.18.refs_3_
  82.6 2.6 %gram.1 = (f32[64,1024]{1,0:T(8,128)}, f32[72,128]{1,0:T(8,128)}) custom-call(s32[14]{0:T(128)} %concatenate.3.ids, f32[2,8,1024]{2,1,0:T(8,128)} %copy-done, f32[2,8,1024]{2,1,0:T(8,128)} %copy-done.2, f32[2,8,1024]{2,1,0:T(8,128)} %copy-done.3, f32[2,8,1024]{2,1,0:T(8,128)} %collective-permute-done.18.refs_3_), custom_call_target="tpu_custom_call" | custom-call | tf_op jit(solution)/shard_map/gram/pallas_call | solution.py:291
  85.2 2.9 %collective-permute-start.20 = (f32[72,128]{1,0:T(8,128)}, f32[72,128]{1,0:T(8,128)S(1)}, u32[]{:S(2)}, u32[]{:S(2)}) collective-permute-start(f32[72,128]{1,0:T(8,128)} %get-tuple-element.59), channel_id=1, source_target_pairs={{0,4},{2,6},{4,0},{6,2},{1,5},{3,7},{5,1},{7,3},{8,12},{10,14},{12... | collective-permute-start | bytes 110600 | tf_op jit(solution)/shard_map/ppermute | solution.py:41
  88.1 1.8 collective-permute-start.21
  90.9 2.6 %collective-permute-done.21 = f32[72,128]{1,0:T(8,128)S(1)} collective-permute-done((f32[72,128]{1,0:T(8,128)}, f32[72,128]{1,0:T(8,128)S(1)}, u32[]{:S(2)}, u32[]{:S(2)}) %collective-permute-start.21) | collective-permute-done | bytes 36896 | tf_op jit(solution)/shard_map/ppermute | solution.py:41
  96.3 2.2 collective-permute-done.23.p2
  99.8 6.6 %logit_grad.1 = (bf16[1024,1000]{1,0:T(8,128)(2,1)}, bf16[1000,1024]{1,0:T(8,128)(2,1)}, f32[16,256]{1,0:T(8,128)}, f32[8,128]{1,0:T(8,128)}) custom-call(s32[14]{0:T(128)} %concatenate.3.ids, f32[64,1024]{1,0:T(8,128)} %get-tuple-element.58.every, f32[72,128]{1,0:T(8,128)} %copy-done.1, f32[72,128]{1,0:T(8,128)} %copy-done.4, f32[72,128]{1,0:T(8,128)} %copy-done.5, ...), custom_call_target="tpu_custom_call" | custom-call | flops 409600 | bytes 240000 | tf_op jit(solution)/shard_map/logit_grad/pallas_call | solution.py:388
  106.3 4.8 %term_part.4.refs_0_ = bf16[1,2,2,528,256]{4,3,2,1,0:T(8,128)(2,1)} custom-call(s32[14]{0:T(128)} %concatenate.3.ids, bf16[1024,1000]{1,0:T(8,128)(2,1)} %get-tuple-element.63.refs_0_.refs_1_, bf16[1000,4096]{1,0:T(8,128)(2,1)} %bitcast.21, bf16[1000,4096]{1,0:T(8,128)(2,1)} %bitcast.22, f32[16,256]{1,0:T(8,128)} %get-tuple-element.64.refs_3_.refs_4_), custom_call_target="tpu_custom_call" | custom-call | flops 20971520 | bytes 103383 | tf_op jit(solution)/shard_map/term_part/pallas_call | solution.py:588
  111.3 7.8 %term_part.5.refs_0_ = bf16[3,2,2,528,256]{4,3,2,1,0:T(8,128)(2,1)} custom-call(s32[14]{0:T(128)} %concatenate.3.ids, bf16[1,2,2,528,256]{4,3,2,1,0:T(8,128)(2,1)} %term_part.4.refs_0_, bf16[1024,1000]{1,0:T(8,128)(2,1)} %get-tuple-element.63.refs_0_.refs_1_, bf16[1000,4096]{1,0:T(8,128)(2,1)} %bitcast.23, bf16[1000,4096]{1,0:T(8,128)(2,1)} %bitcast.24, ...), custom_call_target="tpu_custom_call" | custom-call | flops 62914560000 | bytes 228229120 | tf_op jit(solution)/shard_map/term_part/pallas_call | solution.py:588
  119.4 5.1 %term_part.6 = (bf16[2,528,256]{2,1,0:T(8,128)(2,1)}, bf16[2,528,256]{2,1,0:T(8,128)(2,1)}) custom-call(s32[14]{0:T(128)} %concatenate.3.ids, bf16[3,2,2,528,256]{4,3,2,1,0:T(8,128)(2,1)} %term_part.5.refs_0_, bf16[1024,1000]{1,0:T(8,128)(2,1)} %get-tuple-element.63.refs_0_.refs_1_, bf16[1000,4096]{1,0:T(8,128)(2,1)} %bitcast.25, ...), custom_call_target="tpu_custom_call" | custom-call | flops 20971520 | bytes 103383 | tf_op jit(solution)/shard_map/term_part/pallas_call | solution.py:588
  124.5 3.2 %collective-permute-start.28 = (bf16[2,528,256]{2,1,0:T(8,128)(2,1)}, bf16[2,528,256]{2,1,0:T(8,128)(2,1)}, u32[]{:S(2)}, u32[]{:S(2)}) collective-permute-start(bf16[2,528,256]{2,1,0:T(8,128)(2,1)} %get-tuple-element.69), channel_id=1, source_target_pairs={{0,6},{2,0},{4,2},{6,4},{1,7},{3,1},{5,3},{7,5},{8,14},{10,8},{12,... | collective-permute-start | bytes 1622024 | tf_op jit(solution)/shard_map/ppermute | solution.py:37
  127.8 6.5 %head_part.3 = (bf16[2,560,256]{2,1,0:T(8,128)(2,1)}, bf16[2,560,256]{2,1,0:T(8,128)(2,1)}, bf16[1,2,440,256]{3,2,1,0:T(8,128)(2,1)}, bf16[1,2,440,256]{3,2,1,0:T(8,128)(2,1)}) custom-call(s32[14]{0:T(128)} %concatenate.3.ids, bf16[2,528,256]{2,1,0:T(8,128)(2,1)} %get-tuple-element.65.refs_0_, bf16[1000,1024]{1,0:T(8,128)(2,1)} %get-tuple-element.66.refs_1_.refs_2_, ...), custom_call_target="tpu_custom_call" | custom-call | flops 41943040000 | bytes 123863040 | tf_op jit(solution)/shard_map/head_part/pallas_call | solution.py:475
  134.2 2.7 %collective-permute-start.29 = (bf16[1,2,440,256]{3,2,1,0:T(8,128)(2,1)}, bf16[1,2,440,256]{3,2,1,0:T(8,128)(2,1)}, u32[]{:S(2)}, u32[]{:S(2)}) collective-permute-start(bf16[1,2,440,256]{3,2,1,0:T(8,128)(2,1)} %get-tuple-element.71), channel_id=1, source_target_pairs={{0,64},{64,0},{1,65},{65,1},{2,66},{66,2},{3,67},{67,3},{4,68},{68... | collective-permute-start | bytes 1351688 | tf_op jit(solution)/shard_map/ppermute | solution.py:41
  137.0 3.4 %collective-permute-done.27.refs_6_ = bf16[2,528,256]{2,1,0:T(8,128)(2,1)} collective-permute-done((bf16[2,528,256]{2,1,0:T(8,128)(2,1)}, bf16[2,528,256]{2,1,0:T(8,128)(2,1)}, u32[]{:S(2)}, u32[]{:S(2)}) %collective-permute-start.27) | collective-permute-done | bytes 540704 | tf_op jit(solution)/shard_map/ppermute | solution.py:37
  140.7 10.6 %term_part.7 = (bf16[2,2,528,256]{3,2,1,0:T(8,128)(2,1)}, bf16[2,2,528,256]{3,2,1,0:T(8,128)(2,1)}, bf16[2,2,528,256]{3,2,1,0:T(8,128)(2,1)}) custom-call(s32[14]{0:T(128)} %concatenate.3.ids, bf16[2,560,256]{2,1,0:T(8,128)(2,1)} %get-tuple-element.68.refs_0_, bf16[1024,1000]{1,0:T(8,128)(2,1)} %get-tuple-element.63.refs_0_.refs_1_, ...), custom_call_target="tpu_custom_call" | custom-call | flops 62914560000 | bytes 228229120 | tf_op jit(solution)/shard_map/term_part/pallas_call | solution.py:588
  151.3 3.2 %collective-permute-start.33 = (bf16[2,2,528,256]{3,2,1,0:T(8,128)(2,1)}, bf16[2,2,528,256]{3,2,1,0:T(8,128)(2,1)}, u32[]{:S(2)}, u32[]{:S(2)}) collective-permute-start(bf16[2,2,528,256]{3,2,1,0:T(8,128)(2,1)} %get-tuple-element.76), channel_id=1, source_target_pairs={{0,6},{2,0},{4,2},{6,4},{1,7},{3,1},{5,3},{7,5},{8,14},{10,8},{12,... | collective-permute-start | bytes 3244040 | tf_op jit(solution)/shard_map/ppermute | solution.py:37
  154.9 10.0 %head_part.4 = (bf16[2,2,560,256]{3,2,1,0:T(8,128)(2,1)}, bf16[2,2,560,256]{3,2,1,0:T(8,128)(2,1)}, bf16[2,2,440,256]{3,2,1,0:T(8,128)(2,1)}, bf16[2,2,440,256]{3,2,1,0:T(8,128)(2,1)}) custom-call(s32[14]{0:T(128)} %concatenate.3.ids, bf16[2,2,528,256]{3,2,1,0:T(8,128)(2,1)} %get-tuple-element.70.refs_0_.refs_1_, ...), custom_call_target="tpu_custom_call" | custom-call | flops 83886080000 | bytes 206766080 | tf_op jit(solution)/shard_map/head_part/pallas_call | solution.py:475
  166.3 1.9 collective-permute-start.40
  168.1 2.7 %collective-permute-start.34 = (bf16[2,2,440,256]{3,2,1,0:T(8,128)(2,1)}, bf16[2,2,440,256]{3,2,1,0:T(8,128)(2,1)}, u32[]{:S(2)}, u32[]{:S(2)}) collective-permute-start(bf16[2,2,440,256]{3,2,1,0:T(8,128)(2,1)} %get-tuple-element.79), channel_id=1, source_target_pairs={{0,64},{64,0},{1,65},{65,1},{2,66},{66,2},{3,67},{67,3},{4,68},{68... | collective-permute-start | bytes 2703368 | tf_op jit(solution)/shard_map/ppermute | solution.py:41
  170.9 6.5 %head_part.5 = (bf16[2,2,560,256]{3,2,1,0:T(8,128)(2,1)}, bf16[1,2,440,256]{3,2,1,0:T(8,128)(2,1)}, bf16[1,2,440,256]{3,2,1,0:T(8,128)(2,1)}) custom-call(s32[14]{0:T(128)} %concatenate.3.ids, bf16[2,2,560,256]{3,2,1,0:T(8,128)(2,1)} %get-tuple-element.73.refs_0_, bf16[1000,1024]{1,0:T(8,128)(2,1)} %get-tuple-element.66.refs_1_.refs_2_, ...), custom_call_target="tpu_custom_call" | custom-call | flops 41943040 | bytes 123863 | tf_op jit(solution)/shard_map/head_part/pallas_call | solution.py:475
  177.6 3.6 %term_sum.1 = (bf16[1024,256]{1,0:T(8,128)(2,1)}, bf16[2,528,256]{2,1,0:T(8,128)(2,1)}, f32[16,256]{1,0:T(8,128)}, f32[1,256]{1,0:T(1,128)}) custom-call(bf16[1,2,440,256]{3,2,1,0:T(8,128)(2,1)} %get-tuple-element.74.refs_0_.keep, bf16[2,2,528,256]{3,2,1,0:T(8,128)(2,1)} %get-tuple-element.70.refs_0_.refs_1_, ...), custom_call_target="tpu_custom_call" | custom-call | flops 20000 | bytes 100000 | tf_op jit(solution)/shard_map/term_sum/pallas_call | solution.py:639
  182.3 2.0 add_bitcast_fusion
  185.1 7.8 %collective-permute-done.34.b = bf16[2,2,440,256]{3,2,1,0:T(8,128)(2,1)} collective-permute-done((bf16[2,2,440,256]{3,2,1,0:T(8,128)(2,1)}, bf16[2,2,440,256]{3,2,1,0:T(8,128)(2,1)}, u32[]{:S(2)}, u32[]{:S(2)}) %collective-permute-start.34) | collective-permute-done | bytes 901152 | tf_op jit(solution)/shard_map/ppermute | solution.py:41
  192.9 2.5 %low_sum.1 = (bf16[2,440,256]{2,1,0:T(8,128)(2,1)}, bf16[2,440,256]{2,1,0:T(8,128)(2,1)}) custom-call(bf16[1024,256]{1,0:T(8,128)(2,1)} %get-tuple-element.77._.refs_3_, bf16[2,2,440,256]{3,2,1,0:T(8,128)(2,1)} %get-tuple-element.78.a, bf16[2,2,440,256]{3,2,1,0:T(8,128)(2,1)} %collective-permute-done.34.b), custom_call_target="tpu_custom_call" | custom-call | flops 20 | bytes 60000 | tf_op jit(solution)/shard_map/low_sum/pallas_call | solution.py:502
  195.6 5.3 %collective-permute-done.39.ra = bf16[2,2,560,256]{3,2,1,0:T(8,128)(2,1)} collective-permute-done((bf16[2,2,560,256]{3,2,1,0:T(8,128)(2,1)}, bf16[2,2,560,256]{3,2,1,0:T(8,128)(2,1)}, u32[]{:S(2)}, u32[]{:S(2)}) %collective-permute-start.39) | collective-permute-done | bytes 1146912 | tf_op jit(solution)/shard_map/ppermute | solution.py:37
  200.8 2.3 fusion
  203.1 2.7 %collective-permute-start.41 = (bf16[2,560,256]{2,1,0:T(8,128)(2,1)}, bf16[2,560,256]{2,1,0:T(8,128)(2,1)}, u32[]{:S(2)}, u32[]{:S(2)}) collective-permute-start(bf16[2,560,256]{2,1,0:T(8,128)(2,1)} %fusion), channel_id=1, source_target_pairs={{0,64},{64,0},{1,65},{65,1},{2,66},{66,2},{3,67},{67,3},{4,68},{68... | collective-permute-start | bytes 1720328 | tf_op jit(solution)/shard_map/ppermute | solution.py:41
  206.8 4.5 %collective-permute-done.35.refs_0_.b1 = bf16[2,440,256]{2,1,0:T(8,128)(2,1)} collective-permute-done((bf16[2,440,256]{2,1,0:T(8,128)(2,1)}, bf16[2,440,256]{2,1,0:T(8,128)(2,1)}, u32[]{:S(2)}, u32[]{:S(2)}) %collective-permute-start.35) | collective-permute-done | bytes 450592 | tf_op jit(solution)/shard_map/ppermute | solution.py:37
  211.3 2.8 %hidden_grad.1 = (bf16[1024,256]{1,0:T(8,128)(2,1)}, f32[1,256]{1,0:T(1,128)}) custom-call(s32[14]{0:T(128)} %concatenate.3.ids, bf16[2,440,256]{2,1,0:T(8,128)(2,1)} %collective-permute-done.35.refs_0_.b1, bf16[2,440,256]{2,1,0:T(8,128)(2,1)} %collective-permute-done.36.refs_1_.b2, bf16[2,440,256]{2,1,0:T(8,128)(2,1)} %collective-permute-done.37.refs_2_.b3, ...), custom_call_target="tpu_custom_call" | custom-call | flops 20000 | bytes 40000 | tf_op jit(solution)/shard_map/hidden_grad/pallas_call | solution.py:673
  214.4 4.1 %collective-permute-start.44 = (f32[1,256]{1,0:T(1,128)}, f32[1,256]{1,0:T(1,128)S(1)}, u32[]{:S(2)}, u32[]{:S(2)}) collective-permute-start(f32[1,256]{1,0:T(1,128)} %get-tuple-element.91), channel_id=1, source_target_pairs={{0,32},{16,48},{32,0},{48,16},{1,33},{17,49},{33,1},{49,17},{2,34}... | collective-permute-start | bytes 3080 | tf_op jit(solution)/shard_map/ppermute | solution.py:41
  220.3 3.2 %collective-permute-done.45 = f32[1,256]{1,0:T(1,128)S(1)} collective-permute-done((f32[1,256]{1,0:T(1,128)}, f32[1,256]{1,0:T(1,128)S(1)}, u32[]{:S(2)}, u32[]{:S(2)}) %collective-permute-start.45) | collective-permute-done | bytes 1056 | tf_op jit(solution)/shard_map/ppermute | solution.py:41
  224.2 2.7 %collective-permute-start.46 = (f32[1,256]{1,0:T(1,128)S(1)}, f32[1,256]{1,0:T(1,128)S(1)}, u32[]{:S(2)}, u32[]{:S(2)}) collective-permute-start(f32[1,256]{1,0:T(1,128)S(1)} %add_add_fusion.1.a), channel_id=1, source_target_pairs={{0,64},{64,0},{1,65},{65,1},{2,66},{66,2},{3,67},{67,3},{4,68},{68... | collective-permute-start | bytes 3080 | tf_op jit(solution)/shard_map/ppermute | solution.py:41
  228.1 4.3 %join.1._ = bf16[1000,512]{1,0:T(8,128)(2,1)} custom-call(s32[14]{0:T(128)} %concatenate.3.ids, bf16[1024,256]{1,0:T(8,128)(2,1)} %get-tuple-element.45._, bf16[2,2,560,256]{3,2,1,0:T(8,128)(2,1)} %get-tuple-element.88.a0, bf16[2,2,560,256]{3,2,1,0:T(8,128)(2,1)} %collective-permute-done.39.ra, bf16[2,2,560,256]{3,2,1,0:T(8,128)(2,1)} %collective-permute-done.40.rb, ...), custom_call_target="tpu_custom_call" | custom-call | flops 20 | bytes 160000 | tf_op jit(solution)/shard_map/join/pallas_call | solution.py:525
  (92 shorter events, 26.0 us)
Async XLA Ops:
  0.6 16.4 %collective-permute-start.3 = (bf16[1024,256]{1,0:T(8,128)(2,1)}, bf16[1024,256]{1,0:T(8,128)(2,1)}, u32[]{:S(2)}, u32[]{:S(2)}) collective-permute-start(bf16[1024,256]{1,0:T(8,128)(2,1)} %refs_5_.1), channel_id=1, source_target_pairs={{0,2},{2,4},{4,6},{6,0},{1,3},{3,5},{5,7},{7,1},{8,10},{10,12},{12... | collective-permute-start | bytes 1572872 | tf_op jit(solution)/shard_map/ppermute | solution.py:37
  2.7 14.4 %collective-permute-start.5 = (bf16[1024,256]{1,0:T(8,128)(2,1)}, bf16[1024,256]{1,0:T(8,128)(2,1)}, u32[]{:S(2)}, u32[]{:S(2)}) collective-permute-start(bf16[1024,256]{1,0:T(8,128)(2,1)} %refs_5_.1), channel_id=1, source_target_pairs={{0,8},{8,0},{1,9},{9,1},{2,10},{10,2},{3,11},{11,3},{4,12},{12,4},... | collective-permute-start | bytes 1572872 | tf_op jit(solution)/shard_map/ppermute | solution.py:41
  4.2 14.1 %collective-permute-start.2 = (bf16[1024,256]{1,0:T(8,128)(2,1)}, bf16[1024,256]{1,0:T(8,128)(2,1)}, u32[]{:S(2)}, u32[]{:S(2)}) collective-permute-start(bf16[1024,256]{1,0:T(8,128)(2,1)} %refs_5_.1), channel_id=1, source_target_pairs={{0,1},{1,0},{2,3},{3,2},{4,5},{5,4},{6,7},{7,6},{8,9},{9,8},{10,11... | collective-permute-start | bytes 1572872 | tf_op jit(solution)/shard_map/ppermute | solution.py:41
  4.2 16.6 %collective-permute-start = (bf16[1024,256]{1,0:T(8,128)(2,1)}, bf16[1024,256]{1,0:T(8,128)(2,1)}, u32[]{:S(2)}, u32[]{:S(2)}) collective-permute-start(bf16[1024,256]{1,0:T(8,128)(2,1)} %refs_5_.1), channel_id=1, source_target_pairs={{0,6},{2,0},{4,2},{6,4},{1,7},{3,1},{5,3},{7,5},{8,14},{10,8},{12,... | collective-permute-start | bytes 1572872 | tf_op jit(solution)/shard_map/ppermute | solution.py:37
  17.1 7.3 %collective-permute-start.4 = (bf16[1024,256]{1,0:T(8,128)(2,1)}, bf16[1024,256]{1,0:T(8,128)(2,1)}, u32[]{:S(2)}, u32[]{:S(2)}) collective-permute-start(bf16[1024,256]{1,0:T(8,128)(2,1)} %collective-permute-done.3.refs_2_), channel_id=1, source_target_pairs={{0,1},{1,0},{2,3},{3,2},{4,5},{5,4},{6,7},{7,6},{8,9},{9,8},{10,11... | collective-permute-start | bytes 1572872 | tf_op jit(solution)/shard_map/ppermute | solution.py:41
  17.1 7.3 %collective-permute-start.6 = (bf16[1024,256]{1,0:T(8,128)(2,1)}, bf16[1024,256]{1,0:T(8,128)(2,1)}, u32[]{:S(2)}, u32[]{:S(2)}) collective-permute-start(bf16[1024,256]{1,0:T(8,128)(2,1)} %collective-permute-done.5.refs_4_.refs_5_), channel_id=1, source_target_pairs={{0,1},{1,0},{2,3},{3,2},{4,5},{5,4},{6,7},{7,6},{8,9},{9,8},{10,11... | collective-permute-start | bytes 1572872 | tf_op jit(solution)/shard_map/ppermute | solution.py:41
  17.6 16.8 %collective-permute-start.7 = (bf16[1024,256]{1,0:T(8,128)(2,1)}, bf16[1024,256]{1,0:T(8,128)(2,1)}, u32[]{:S(2)}, u32[]{:S(2)}) collective-permute-start(bf16[1024,256]{1,0:T(8,128)(2,1)} %collective-permute-done.3.refs_2_), channel_id=1, source_target_pairs={{0,2},{2,4},{4,6},{6,0},{1,3},{3,5},{5,7},{7,1},{8,10},{10,12},{12... | collective-permute-start | bytes 1572872 | tf_op jit(solution)/shard_map/ppermute | solution.py:37
  18.3 16.1 %collective-permute-start.8 = (bf16[1024,256]{1,0:T(8,128)(2,1)}, bf16[1024,256]{1,0:T(8,128)(2,1)}, u32[]{:S(2)}, u32[]{:S(2)}) collective-permute-start(bf16[1024,256]{1,0:T(8,128)(2,1)} %collective-permute-done.5.refs_4_.refs_5_), channel_id=1, source_target_pairs={{0,6},{2,0},{4,2},{6,4},{1,7},{3,1},{5,3},{7,5},{8,14},{10,8},{12,... | collective-permute-start | bytes 1572872 | tf_op jit(solution)/shard_map/ppermute | solution.py:37
  20.8 13.6 %collective-permute-start.9 = (bf16[1024,256]{1,0:T(8,128)(2,1)}, bf16[1024,256]{1,0:T(8,128)(2,1)}, u32[]{:S(2)}, u32[]{:S(2)}) collective-permute-start(bf16[1024,256]{1,0:T(8,128)(2,1)} %collective-permute-done.3.refs_2_), channel_id=1, source_target_pairs={{0,8},{8,0},{1,9},{9,1},{2,10},{10,2},{3,11},{11,3},{4,12},{12,4},... | collective-permute-start | bytes 1572872 | tf_op jit(solution)/shard_map/ppermute | solution.py:41
  24.4 12.1 %collective-permute-start.1 = (bf16[1024,256]{1,0:T(8,128)(2,1)}, bf16[1024,256]{1,0:T(8,128)(2,1)}, u32[]{:S(2)}, u32[]{:S(2)}) collective-permute-start(bf16[1024,256]{1,0:T(8,128)(2,1)} %collective-permute-done.refs_0_), channel_id=1, source_target_pairs={{0,1},{1,0},{2,3},{3,2},{4,5},{5,4},{6,7},{7,6},{8,9},{9,8},{10,11... | collective-permute-start | bytes 1572872 | tf_op jit(solution)/shard_map/ppermute | solution.py:41
  34.5 2.5 %collective-permute-start.10 = (bf16[1024,256]{1,0:T(8,128)(2,1)}, bf16[1024,256]{1,0:T(8,128)(2,1)}, u32[]{:S(2)}, u32[]{:S(2)}) collective-permute-start(bf16[1024,256]{1,0:T(8,128)(2,1)} %get-tuple-element.49.refs_2_), channel_id=1, source_target_pairs={{0,1},{1,0},{2,3},{3,2},{4,5},{5,4},{6,7},{7,6},{8,9},{9,8},{10,11... | collective-permute-start | bytes 1572872 | tf_op jit(solution)/shard_map/ppermute | solution.py:41
  35.0 2.6 %collective-permute-start.11 = (bf16[1024,256]{1,0:T(8,128)(2,1)}, bf16[1024,256]{1,0:T(8,128)(2,1)}, u32[]{:S(2)}, u32[]{:S(2)}) collective-permute-start(bf16[1024,256]{1,0:T(8,128)(2,1)} %get-tuple-element.50.refs_4_), channel_id=1, source_target_pairs={{0,1},{1,0},{2,3},{3,2},{4,5},{5,4},{6,7},{7,6},{8,9},{9,8},{10,11... | collective-permute-start | bytes 1572872 | tf_op jit(solution)/shard_map/ppermute | solution.py:41
  35.1 3.3 %collective-permute-start.12 = (bf16[1024,256]{1,0:T(8,128)(2,1)}, bf16[1024,256]{1,0:T(8,128)(2,1)}, u32[]{:S(2)}, u32[]{:S(2)}) collective-permute-start(bf16[1024,256]{1,0:T(8,128)(2,1)} %get-tuple-element.51.refs_6_), channel_id=1, source_target_pairs={{0,1},{1,0},{2,3},{3,2},{4,5},{5,4},{6,7},{7,6},{8,9},{9,8},{10,11... | collective-permute-start | bytes 1572872 | tf_op jit(solution)/shard_map/ppermute | solution.py:41
  35.6 15.9 %collective-permute-start.13 = (bf16[1024,256]{1,0:T(8,128)(2,1)}, bf16[1024,256]{1,0:T(8,128)(2,1)}, u32[]{:S(2)}, u32[]{:S(2)}) collective-permute-start(bf16[1024,256]{1,0:T(8,128)(2,1)} %get-tuple-element.49.refs_2_), channel_id=1, source_target_pairs={{0,8},{8,0},{1,9},{9,1},{2,10},{10,2},{3,11},{11,3},{4,12},{12,4},... | collective-permute-start | bytes 1572872 | tf_op jit(solution)/shard_map/ppermute | solution.py:41
  51.5 2.3 collective-permute-start.14
  66.1 5.7 %collective-permute-start.15 = (f32[8,1024]{1,0:T(8,128)}, f32[8,1024]{1,0:T(8,128)S(1)}, u32[]{:S(2)}, u32[]{:S(2)}) collective-permute-start(f32[8,1024]{1,0:T(8,128)} %get-tuple-element.57), channel_id=1, source_target_pairs={{0,64},{64,0},{1,65},{65,1},{2,66},{66,2},{3,67},{67,3},{4,68},{68... | collective-permute-start | bytes 98312 | tf_op jit(solution)/shard_map/ppermute | solution.py:41
  72.6 4.7 %collective-permute-start.16 = (f32[2,8,1024]{2,1,0:T(8,128)S(1)}, f32[2,8,1024]{2,1,0:T(8,128)S(1)}, u32[]{:S(2)}, u32[]{:S(2)}) collective-permute-start(f32[2,8,1024]{2,1,0:T(8,128)S(1)} %pad_maximum_fusion.refs_0_), channel_id=1, source_target_pairs={{0,16},{16,0},{32,48},{48,32},{1,17},{17,1},{33,49},{49,33},{2,18}... | collective-permute-start | bytes 196616 | tf_op jit(solution)/shard_map/ppermute | solution.py:41
  74.2 5.9 %collective-permute-start.17 = (f32[2,8,1024]{2,1,0:T(8,128)S(1)}, f32[2,8,1024]{2,1,0:T(8,128)S(1)}, u32[]{:S(2)}, u32[]{:S(2)}) collective-permute-start(f32[2,8,1024]{2,1,0:T(8,128)S(1)} %pad_maximum_fusion.refs_0_), channel_id=1, source_target_pairs={{0,32},{16,48},{32,0},{48,16},{1,33},{17,49},{33,1},{49,17},{2,34}... | collective-permute-start | bytes 196616 | tf_op jit(solution)/shard_map/ppermute | solution.py:41
  77.1 5.6 %collective-permute-start.18 = (f32[2,8,1024]{2,1,0:T(8,128)S(1)}, f32[2,8,1024]{2,1,0:T(8,128)}, u32[]{:S(2)}, u32[]{:S(2)}) collective-permute-start(f32[2,8,1024]{2,1,0:T(8,128)S(1)} %pad_maximum_fusion.refs_0_), channel_id=1, source_target_pairs={{0,48},{16,32},{32,16},{48,0},{1,49},{17,33},{33,17},{49,1},{2,50}... | collective-permute-start | bytes 196616 | tf_op jit(solution)/shard_map/ppermute | solution.py:41
  85.2 4.7 %collective-permute-start.19 = (f32[72,128]{1,0:T(8,128)}, f32[72,128]{1,0:T(8,128)S(1)}, u32[]{:S(2)}, u32[]{:S(2)}) collective-permute-start(f32[72,128]{1,0:T(8,128)} %get-tuple-element.59), channel_id=1, source_target_pairs={{0,2},{2,0},{4,6},{6,4},{1,3},{3,1},{5,7},{7,5},{8,10},{10,8},{12,... | collective-permute-start | bytes 110600 | tf_op jit(solution)/shard_map/ppermute | solution.py:41
  85.2 5.7 %collective-permute-start.20 = (f32[72,128]{1,0:T(8,128)}, f32[72,128]{1,0:T(8,128)S(1)}, u32[]{:S(2)}, u32[]{:S(2)}) collective-permute-start(f32[72,128]{1,0:T(8,128)} %get-tuple-element.59), channel_id=1, source_target_pairs={{0,4},{2,6},{4,0},{6,2},{1,5},{3,7},{5,1},{7,3},{8,12},{10,14},{12... | collective-permute-start | bytes 110600 | tf_op jit(solution)/shard_map/ppermute | solution.py:41
  88.1 5.4 %collective-permute-start.21 = (f32[72,128]{1,0:T(8,128)}, f32[72,128]{1,0:T(8,128)S(1)}, u32[]{:S(2)}, u32[]{:S(2)}) collective-permute-start(f32[72,128]{1,0:T(8,128)} %get-tuple-element.59), channel_id=1, source_target_pairs={{0,6},{2,4},{4,2},{6,0},{1,7},{3,5},{5,3},{7,1},{8,14},{10,12},{12... | collective-permute-start | bytes 110600 | tf_op jit(solution)/shard_map/ppermute | solution.py:41
  94.3 2.0 collective-permute-start.22
  94.4 4.0 %collective-permute-start.23 = (f32[72,128]{1,0:T(8,128)S(1)}, f32[72,128]{1,0:T(8,128)S(1)}, u32[]{:S(2)}, u32[]{:S(2)}) collective-permute-start(f32[72,128]{1,0:T(8,128)S(1)} %add_add_fusion.p0), channel_id=1, source_target_pairs={{0,8},{8,0},{1,9},{9,1},{2,10},{10,2},{3,11},{11,3},{4,12},{12,4},... | collective-permute-start | bytes 110600 | tf_op jit(solution)/shard_map/ppermute | solution.py:41
  95.7 3.4 %collective-permute-start.24 = (f32[72,128]{1,0:T(8,128)S(1)}, f32[72,128]{1,0:T(8,128)S(1)}, u32[]{:S(2)}, u32[]{:S(2)}) collective-permute-start(f32[72,128]{1,0:T(8,128)S(1)} %add_add_fusion.p0), channel_id=1, source_target_pairs={{0,9},{1,8},{8,1},{9,0},{2,11},{3,10},{10,3},{11,2},{4,13},{5,12},... | collective-permute-start | bytes 110600 | tf_op jit(solution)/shard_map/ppermute | solution.py:730
  111.1 8.3 %collective-permute-start.25 = (bf16[1,2,2,528,256]{4,3,2,1,0:T(8,128)(2,1)}, bf16[1,2,2,528,256]{4,3,2,1,0:T(8,128)(2,1)}, u32[]{:S(2)}, u32[]{:S(2)}) collective-permute-start(bf16[1,2,2,528,256]{4,3,2,1,0:T(8,128)(2,1)} %term_part.4.refs_0_), channel_id=1, source_target_pairs={{0,1},{1,0},{2,3},{3,2},{4,5},{5,4},{6,7},{7,6},{8,9},{9,8},{10,11... | collective-permute-start | bytes 3244040 | tf_op jit(solution)/shard_map/ppermute | solution.py:41
  119.0 21.6 %collective-permute-start.26 = (bf16[3,2,2,528,256]{4,3,2,1,0:T(8,128)(2,1)}, bf16[3,2,2,528,256]{4,3,2,1,0:T(8,128)(2,1)}, u32[]{:S(2)}, u32[]{:S(2)}) collective-permute-start(bf16[3,2,2,528,256]{4,3,2,1,0:T(8,128)(2,1)} %term_part.5.refs_0_), channel_id=1, source_target_pairs={{0,1},{1,0},{2,3},{3,2},{4,5},{5,4},{6,7},{7,6},{8,9},{9,8},{10,11... | collective-permute-start | bytes 9732104 | tf_op jit(solution)/shard_map/ppermute | solution.py:41
  124.5 15.9 %collective-permute-start.27 = (bf16[2,528,256]{2,1,0:T(8,128)(2,1)}, bf16[2,528,256]{2,1,0:T(8,128)(2,1)}, u32[]{:S(2)}, u32[]{:S(2)}) collective-permute-start(bf16[2,528,256]{2,1,0:T(8,128)(2,1)} %get-tuple-element.65.refs_0_), channel_id=1, source_target_pairs={{0,2},{2,4},{4,6},{6,0},{1,3},{3,5},{5,7},{7,1},{8,10},{10,12},{12... | collective-permute-start | bytes 1622024 | tf_op jit(solution)/shard_map/ppermute | solution.py:37
  124.5 16.1 %collective-permute-start.28 = (bf16[2,528,256]{2,1,0:T(8,128)(2,1)}, bf16[2,528,256]{2,1,0:T(8,128)(2,1)}, u32[]{:S(2)}, u32[]{:S(2)}) collective-permute-start(bf16[2,528,256]{2,1,0:T(8,128)(2,1)} %get-tuple-element.69), channel_id=1, source_target_pairs={{0,6},{2,0},{4,2},{6,4},{1,7},{3,1},{5,3},{7,5},{8,14},{10,8},{12,... | collective-permute-start | bytes 1622024 | tf_op jit(solution)/shard_map/ppermute | solution.py:37
  134.2 20.3 %collective-permute-start.29 = (bf16[1,2,440,256]{3,2,1,0:T(8,128)(2,1)}, bf16[1,2,440,256]{3,2,1,0:T(8,128)(2,1)}, u32[]{:S(2)}, u32[]{:S(2)}) collective-permute-start(bf16[1,2,440,256]{3,2,1,0:T(8,128)(2,1)} %get-tuple-element.71), channel_id=1, source_target_pairs={{0,64},{64,0},{1,65},{65,1},{2,66},{66,2},{3,67},{67,3},{4,68},{68... | collective-permute-start | bytes 1351688 | tf_op jit(solution)/shard_map/ppermute | solution.py:41
  137.0 17.5 %collective-permute-start.30 = (bf16[2,560,256]{2,1,0:T(8,128)(2,1)}, bf16[2,560,256]{2,1,0:T(8,128)(2,1)}, u32[]{:S(2)}, u32[]{:S(2)}) collective-permute-start(bf16[2,560,256]{2,1,0:T(8,128)(2,1)} %get-tuple-element.68.refs_0_), channel_id=1, source_target_pairs={{0,16},{16,32},{32,48},{48,0},{1,17},{17,33},{33,49},{49,1},{2,18}... | collective-permute-start | bytes 1720328 | tf_op jit(solution)/shard_map/ppermute | solution.py:37
  140.4 14.5 %collective-permute-start.31 = (bf16[2,560,256]{2,1,0:T(8,128)(2,1)}, bf16[2,560,256]{2,1,0:T(8,128)(2,1)}, u32[]{:S(2)}, u32[]{:S(2)}) collective-permute-start(bf16[2,560,256]{2,1,0:T(8,128)(2,1)} %get-tuple-element.72), channel_id=1, source_target_pairs={{0,48},{16,0},{32,16},{48,32},{1,49},{17,1},{33,17},{49,33},{2,50}... | collective-permute-start | bytes 1720328 | tf_op jit(solution)/shard_map/ppermute | solution.py:37
  151.3 26.4 %collective-permute-start.32 = (bf16[2,2,528,256]{3,2,1,0:T(8,128)(2,1)}, bf16[2,2,528,256]{3,2,1,0:T(8,128)(2,1)}, u32[]{:S(2)}, u32[]{:S(2)}) collective-permute-start(bf16[2,2,528,256]{3,2,1,0:T(8,128)(2,1)} %get-tuple-element.75), channel_id=1, source_target_pairs={{0,2},{2,4},{4,6},{6,0},{1,3},{3,5},{5,7},{7,1},{8,10},{10,12},{12... | collective-permute-start | bytes 3244040 | tf_op jit(solution)/shard_map/ppermute | solution.py:37
  151.3 26.4 %collective-permute-start.33 = (bf16[2,2,528,256]{3,2,1,0:T(8,128)(2,1)}, bf16[2,2,528,256]{3,2,1,0:T(8,128)(2,1)}, u32[]{:S(2)}, u32[]{:S(2)}) collective-permute-start(bf16[2,2,528,256]{3,2,1,0:T(8,128)(2,1)} %get-tuple-element.76), channel_id=1, source_target_pairs={{0,6},{2,0},{4,2},{6,4},{1,7},{3,1},{5,3},{7,5},{8,14},{10,8},{12,... | collective-permute-start | bytes 3244040 | tf_op jit(solution)/shard_map/ppermute | solution.py:37
  164.9 35.9 %collective-permute-start.39 = (bf16[2,2,560,256]{3,2,1,0:T(8,128)(2,1)}, bf16[2,2,560,256]{3,2,1,0:T(8,128)(2,1)}, u32[]{:S(2)}, u32[]{:S(2)}) collective-permute-start(bf16[2,2,560,256]{3,2,1,0:T(8,128)(2,1)} %get-tuple-element.73.refs_0_), channel_id=1, source_target_pairs={{0,16},{16,32},{32,48},{48,0},{1,17},{17,33},{33,49},{49,1},{2,18}... | collective-permute-start | bytes 3440648 | tf_op jit(solution)/shard_map/ppermute | solution.py:37
  166.3 34.5 %collective-permute-start.40 = (bf16[2,2,560,256]{3,2,1,0:T(8,128)(2,1)}, bf16[2,2,560,256]{3,2,1,0:T(8,128)(2,1)}, u32[]{:S(2)}, u32[]{:S(2)}) collective-permute-start(bf16[2,2,560,256]{3,2,1,0:T(8,128)(2,1)} %get-tuple-element.89), channel_id=1, source_target_pairs={{0,48},{16,0},{32,16},{48,32},{1,49},{17,1},{33,17},{49,33},{2,50}... | collective-permute-start | bytes 3440648 | tf_op jit(solution)/shard_map/ppermute | solution.py:37
  168.1 24.8 %collective-permute-start.34 = (bf16[2,2,440,256]{3,2,1,0:T(8,128)(2,1)}, bf16[2,2,440,256]{3,2,1,0:T(8,128)(2,1)}, u32[]{:S(2)}, u32[]{:S(2)}) collective-permute-start(bf16[2,2,440,256]{3,2,1,0:T(8,128)(2,1)} %get-tuple-element.79), channel_id=1, source_target_pairs={{0,64},{64,0},{1,65},{65,1},{2,66},{66,2},{3,67},{67,3},{4,68},{68... | collective-permute-start | bytes 2703368 | tf_op jit(solution)/shard_map/ppermute | solution.py:41
  181.3 30.1 %collective-permute-start.38 = (bf16[2,528,256]{2,1,0:T(8,128)(2,1)}, bf16[2,528,256]{2,1,0:T(8,128)(2,1)}, u32[]{:S(2)}, u32[]{:S(2)}) collective-permute-start(bf16[2,528,256]{2,1,0:T(8,128)(2,1)} %get-tuple-element.83), channel_id=1, source_target_pairs={{0,8},{8,0},{1,9},{9,1},{2,10},{10,2},{3,11},{11,3},{4,12},{12,4},... | collective-permute-start | bytes 1622024 | tf_op jit(solution)/shard_map/ppermute | solution.py:41
  184.3 21.6 %collective-permute-start.36 = (bf16[2,440,256]{2,1,0:T(8,128)(2,1)}, bf16[2,440,256]{2,1,0:T(8,128)(2,1)}, u32[]{:S(2)}, u32[]{:S(2)}) collective-permute-start(bf16[2,440,256]{2,1,0:T(8,128)(2,1)} %add_bitcast_fusion), channel_id=1, source_target_pairs={{0,32},{16,48},{32,0},{48,16},{1,33},{17,49},{33,1},{49,17},{2,34}... | collective-permute-start | bytes 1351688 | tf_op jit(solution)/shard_map/ppermute | solution.py:37
  195.4 15.9 %collective-permute-start.35 = (bf16[2,440,256]{2,1,0:T(8,128)(2,1)}, bf16[2,440,256]{2,1,0:T(8,128)(2,1)}, u32[]{:S(2)}, u32[]{:S(2)}) collective-permute-start(bf16[2,440,256]{2,1,0:T(8,128)(2,1)} %get-tuple-element.80), channel_id=1, source_target_pairs={{0,16},{16,32},{32,48},{48,0},{1,17},{17,33},{33,49},{49,1},{2,18}... | collective-permute-start | bytes 1351688 | tf_op jit(solution)/shard_map/ppermute | solution.py:37
  200.8 10.5 %collective-permute-start.37 = (bf16[2,440,256]{2,1,0:T(8,128)(2,1)}, bf16[2,440,256]{2,1,0:T(8,128)(2,1)}, u32[]{:S(2)}, u32[]{:S(2)}) collective-permute-start(bf16[2,440,256]{2,1,0:T(8,128)(2,1)} %get-tuple-element.82), channel_id=1, source_target_pairs={{0,48},{16,0},{32,16},{48,32},{1,49},{17,1},{33,17},{49,33},{2,50}... | collective-permute-start | bytes 1351688 | tf_op jit(solution)/shard_map/ppermute | solution.py:37
  203.1 25.0 %collective-permute-start.41 = (bf16[2,560,256]{2,1,0:T(8,128)(2,1)}, bf16[2,560,256]{2,1,0:T(8,128)(2,1)}, u32[]{:S(2)}, u32[]{:S(2)}) collective-permute-start(bf16[2,560,256]{2,1,0:T(8,128)(2,1)} %fusion), channel_id=1, source_target_pairs={{0,64},{64,0},{1,65},{65,1},{2,66},{66,2},{3,67},{67,3},{4,68},{68... | collective-permute-start | bytes 1720328 | tf_op jit(solution)/shard_map/ppermute | solution.py:41
  205.8 22.2 %collective-permute-start.42 = (bf16[1,2,440,256]{3,2,1,0:T(8,128)(2,1)}, bf16[1,2,440,256]{3,2,1,0:T(8,128)(2,1)}, u32[]{:S(2)}, u32[]{:S(2)}) collective-permute-start(bf16[1,2,440,256]{3,2,1,0:T(8,128)(2,1)} %get-tuple-element.90), channel_id=1, source_target_pairs={{0,64},{64,0},{1,65},{65,1},{2,66},{66,2},{3,67},{67,3},{4,68},{68... | collective-permute-start | bytes 1351688 | tf_op jit(solution)/shard_map/ppermute | solution.py:41
  214.1 4.7 %collective-permute-start.43 = (f32[1,256]{1,0:T(1,128)}, f32[1,256]{1,0:T(1,128)S(1)}, u32[]{:S(2)}, u32[]{:S(2)}) collective-permute-start(f32[1,256]{1,0:T(1,128)} %get-tuple-element.91), channel_id=1, source_target_pairs={{0,16},{16,0},{32,48},{48,32},{1,17},{17,1},{33,49},{49,33},{2,18}... | collective-permute-start | bytes 3080 | tf_op jit(solution)/shard_map/ppermute | solution.py:41
  214.4 5.9 %collective-permute-start.44 = (f32[1,256]{1,0:T(1,128)}, f32[1,256]{1,0:T(1,128)S(1)}, u32[]{:S(2)}, u32[]{:S(2)}) collective-permute-start(f32[1,256]{1,0:T(1,128)} %get-tuple-element.91), channel_id=1, source_target_pairs={{0,32},{16,48},{32,0},{48,16},{1,33},{17,49},{33,1},{49,17},{2,34}... | collective-permute-start | bytes 3080 | tf_op jit(solution)/shard_map/ppermute | solution.py:41
  218.5 5.0 %collective-permute-start.45 = (f32[1,256]{1,0:T(1,128)}, f32[1,256]{1,0:T(1,128)S(1)}, u32[]{:S(2)}, u32[]{:S(2)}) collective-permute-start(f32[1,256]{1,0:T(1,128)} %get-tuple-element.91), channel_id=1, source_target_pairs={{0,48},{16,32},{32,16},{48,0},{1,49},{17,33},{33,17},{49,1},{2,50}... | collective-permute-start | bytes 3080 | tf_op jit(solution)/shard_map/ppermute | solution.py:41
  224.2 8.2 %copy-start.7 = (f32[1,256]{1,0:T(1,128)}, f32[1,256]{1,0:T(1,128)S(1)}, u32[]{:S(2)}) copy-start(f32[1,256]{1,0:T(1,128)S(1)} %add_add_fusion.1.a) | copy-start | bytes 3076
  224.2 8.2 %collective-permute-start.46 = (f32[1,256]{1,0:T(1,128)S(1)}, f32[1,256]{1,0:T(1,128)S(1)}, u32[]{:S(2)}, u32[]{:S(2)}) collective-permute-start(f32[1,256]{1,0:T(1,128)S(1)} %add_add_fusion.1.a), channel_id=1, source_target_pairs={{0,64},{64,0},{1,65},{65,1},{2,66},{66,2},{3,67},{67,3},{4,68},{68... | collective-permute-start | bytes 3080 | tf_op jit(solution)/shard_map/ppermute | solution.py:41
  (8 other events, 18.2 us)
where the time goes:
time: 235 us; the launch traced here: 234 us
  Pallas kernels  110 us (47%)
  starting transfers between devices  56.7 us (24%)
  waiting for transfers between devices  55 us (23%)
  other arithmetic  6.44 us (3%)
  local copies, waits for them, and re-layouts  5.02 us (2%)
    ppermute x31, starting transfers between devices, swap(): return lax.ppermute(x, axis, [(i, i ^ bits) for i in range(SIZES[axis])])  37.7 us
    ppermute x31, waiting for transfers between devices, swap(): return lax.ppermute(x, axis, [(i, i ^ bits) for i in range(SIZES[axis])])  29.8 us
    pallas_call x4, Pallas kernels, term_part(): pl.pallas_call(later(len(after), functools.partial(term_kernel, count, sp...  28.3 us
    ppermute x15, waiting for transfers between devices, shift(): return lax.ppermute(x, axis, [(i, (i + step) % n) for i in range(n)])  24.5 us
    pallas_call x2, Pallas kernels, forward(): pl.pallas_call(functools.partial(forward_kernel, places, not state), out_...  23.1 us
    pallas_call x3, Pallas kernels, head_part(): pl.pallas_call(later(len(after), functools.partial(head_kernel, steps, sp...  23 us
    ppermute x15, starting transfers between devices, shift(): return lax.ppermute(x, axis, [(i, (i + step) % n) for i in range(n)])  18.5 us
    pallas_call x1, Pallas kernels, forward_last(): pl.pallas_call(functools.partial(forward_last_kernel, place), out_shape=[...  12.2 us
  transfers between devices with their start and end apart: 47, of which 20 were waited for; matrix products, arithmetic and copies ran while one was open for 3% of the time, Pallas kernels for 35%

commit v1 on v0

--- a/solution.py
+++ b/solution.py
@@ -493,21 +493,21 @@
     )(ids, *after, ht, x, gain, *adds)
 
 
-def low_sum_kernel(_, a, b, *outs):
-    for i, out in enumerate(outs):
+def low_sum_kernel(_, a13, b13, a2, b2, out_1, out_3, out_2):
+    for a, b, i, out in ((a13, b13, 0, out_1), (a13, b13, 1, out_3), (a2, b2, 0, out_2)):
         out[...] = (a[i].astype(f32) + b[i].astype(f32)).astype(bf16)
 
 
-def low_sum(after, a, b):
+def low_sum(after, *parts):
     return pl.pallas_call(
         low_sum_kernel,
-        out_shape=[jax.ShapeDtypeStruct((2, ROWS_B, BLK), bf16)] * a.shape[0],
-        in_specs=[ANY, VMEM, VMEM],
-        out_specs=[VMEM] * a.shape[0],
-        compiler_params=params(),
-        cost_estimate=cost(1000, 3_000_000),
+        out_shape=[jax.ShapeDtypeStruct((2, ROWS_B, BLK), bf16)] * 3,
+        in_specs=[ANY] + [VMEM] * 4,
+        out_specs=[VMEM] * 3,
+        compiler_params=params(),
+        cost_estimate=cost(1000, 4_000_000),
         name="low_sum",
-    )(after, a, b)
+    )(after, *parts)
 
 
 def join_kernel(ids, _, a0, ra, rb, got, keep, swapped, b1, b2, b3, out):
@@ -652,9 +652,7 @@
     )(*after, own, ra, rb, x, x_p)
 
 
-def final_kernel(ids, n_ref, got, x_ref, gain, inv_ref, dots, sums, out, sums_out):
-    tail = got[0, HALF:, :].astype(f32)
-    sums_out[...] = sums[...] + tail[2:3] + tail[3:4]
+def final_kernel(ids, n_ref, got, x_ref, gain, inv_ref, dots, out):
     g = gain[:, block_at(ids, ids[2] * 4 + ids[3], 0)]
     for half in range(2):
         lines = (dots[half * 8 : half * 8 + 8, :] + got[half, HALF:, :].astype(f32)[:8]) / D
@@ -669,16 +667,37 @@
             out[rows, :] = (grad * g - values * (inverse * inverse * column)).astype(bf16)
 
 
-def final(ids, after, n, got, x, gain, inv, dots, sums):
+def final(ids, after, n, got, x, gain, inv, dots):
     return pl.pallas_call(
         later(len(after), final_kernel),
-        out_shape=[jax.ShapeDtypeStruct((TOK, BLK), bf16), jax.ShapeDtypeStruct((1, BLK), f32)],
-        in_specs=[SMEM] + [ANY] * len(after) + [VMEM] * 7,
-        out_specs=[VMEM] * 2,
+        out_shape=jax.ShapeDtypeStruct((TOK, BLK), bf16),
+        in_specs=[SMEM] + [ANY] * len(after) + [VMEM] * 6,
+        out_specs=VMEM,
         compiler_params=params(),
         cost_estimate=cost(1_000_000, 2_000_000),
         name="hidden_grad",
-    )(ids, *after, n, got, x, gain, inv, dots, sums)
+    )(ids, *after, n, got, x, gain, inv, dots)
+
+
+def gain_vocab(after, partial, got):
+    count = len(after)
+
+    def kernel(*refs):
+        sums, tail, out = refs[count:]
+        rows = tail[0].astype(f32)
+        out[...] = sums[...] + rows[2:3] + rows[3:4]
+
+    return pl.pallas_call(
+        kernel,
+        grid=(1,),
+        out_shape=jax.ShapeDtypeStruct((1, BLK), f32),
+        in_specs=[ANY] * count
+        + [pl.BlockSpec((1, BLK), lambda k: (0, 0)), pl.BlockSpec((1, 16, BLK), lambda k: (0, HALF // 16, 0))],
+        out_specs=pl.BlockSpec((1, BLK), lambda k: (0, 0)),
+        compiler_params=params(),
+        cost_estimate=cost(1000, 5000),
+        name="gain_vocab",
+    )(*after, partial, got)
 
 
 def gain_sum_kernel(_, a, b, out):
@@ -749,9 +768,11 @@
     keep, send, dots, partial = term_sum((keep_0,), t_0, shift(t_1, "z", 1), shift(t_3, "z", -1), hidden, x_p)
     swap_0 = swap(send_0, "xh")
     got = swap(a_0[1] + ra[1] + rb[1], "xh")
-    low_1, low_3 = low_sum(keep, keep_13, swap_13)
-    low = [shift(low_1, "y", 1), shift(keep_2[0] + swap_2[0], "y", 2), shift(low_3, "y", 3)]
-    hidden_grad, gain_grad = final(ids, low, keep, swap(send, "xl"), hidden, gain, inv, dots, partial)
+    low_1, low_3, low_2 = low_sum(keep, keep_13, swap_13, keep_2, swap_2)
+    low = [shift(low_1, "y", 1), shift(low_2, "y", 2), shift(low_3, "y", 3)]
+    got_term = swap(send, "xl")
+    hidden_grad = final(ids, (swap_0,), keep, got_term, hidden, gain, inv, dots)
+    gain_grad = gain_vocab((hidden_grad, *low), partial, got_term)
     gain_grad = (gain_grad + swap(gain_grad, "y", 1)) + (swap(gain_grad, "y", 2) + swap(gain_grad, "y", 3))
     head_t = join(ids, hidden_grad, a_0, ra, rb, got, keep_0, swap_0, *low)
     return losses[0, :3], hidden_grad, head_t.T, gain_sum(head_t, gain_grad, swap(gain_grad, "xh"))[0]

time: 235 us -> 237 us (level)
    ppermute x31, waiting for transfers between devices: 29.8 us -> 39.4 us  [swap(): return lax.ppermute(x, axis, [(i, i ^ bits) for i in range(SIZES[axis])])]
    ppermute x15, waiting for transfers between devices: 24.5 us -> 16.1 us  [shift(): return lax.ppermute(x, axis, [(i, (i + step) % n) for i in range(n)])]
    ppermute x15, starting transfers between devices: 18.5 us -> 23.8 us  [shift(): return lax.ppermute(x, axis, [(i, (i + step) % n) for i in range(n)])]
    ppermute x31, starting transfers between devices: 37.7 us -> 32.9 us  [swap(): return lax.ppermute(x, axis, [(i, i ^ bits) for i in range(SIZES[axis])])]
  transfers between devices with their start and end apart: 47 -> 47, of which waited for: 20 -> 19; matrix products, arithmetic and copies ran while one was open for 3% -> 3% of each run, Pallas kernels for 35% -> 36%
where the time goes in v1:
time: 237 us; the launch traced here: 236 us
  Pallas kernels  112 us (47%)
  starting transfers between devices  57.2 us (24%)
  waiting for transfers between devices  56.3 us (24%)
  local copies, waits for them, and re-layouts  5.02 us (2%)
  other arithmetic  4.51 us (2%)
    ppermute x31, waiting for transfers between devices, swap(): return lax.ppermute(x, axis, [(i, i ^ bits) for i in range(SIZES[axis])])  39.4 us
    ppermute x31, starting transfers between devices, swap(): return lax.ppermute(x, axis, [(i, i ^ bits) for i in range(SIZES[axis])])  32.9 us
    pallas_call x4, Pallas kernels, term_part(): pl.pallas_call(later(len(after), functools.partial(term_kernel, count, sp...  28.3 us
    ppermute x15, starting transfers between devices, shift(): return lax.ppermute(x, axis, [(i, (i + step) % n) for i in range(n)])  23.8 us
    pallas_call x2, Pallas kernels, forward(): pl.pallas_call(functools.partial(forward_kernel, places, not state), out_...  23.1 us
    pallas_call x3, Pallas kernels, head_part(): pl.pallas_call(later(len(after), functools.partial(head_kernel, steps, sp...  23 us
    ppermute x15, waiting for transfers between devices, shift(): return lax.ppermute(x, axis, [(i, (i + step) % n) for i in range(n)])  16.1 us
    pallas_call x1, Pallas kernels, forward_last(): pl.pallas_call(functools.partial(forward_last_kernel, place), out_shape=[...  12.2 us
  transfers between devices with their start and end apart: 47, of which 19 were waited for; matrix products, arithmetic and copies ran while one was open for 3% of the time, Pallas kernels for 36%

profile of v1, /device:TPU:0, one launch (start us, length us, event | category | flops | bytes accessed | tf_op | source)
XLA Modules:
  0.0 235.7 jit_solution(18031475561946412975)
XLA Ops:
  0.6 2.1 collective-permute-start.3
  2.7 1.5 collective-permute-start.5
  4.2 2.2 collective-permute-start
  6.4 10.7 %collective-permute-done.3.refs_2_ = bf16[1024,256]{1,0:T(8,128)(2,1)} collective-permute-done((bf16[1024,256]{1,0:T(8,128)(2,1)}, bf16[1024,256]{1,0:T(8,128)(2,1)}, u32[]{:S(2)}, u32[]{:S(2)}) %collective-permute-start.3) | collective-permute-done | bytes 524320 | tf_op jit(solution)/shard_map/ppermute | solution.py:37
  18.3 2.5 %collective-permute-start.8 = (bf16[1024,256]{1,0:T(8,128)(2,1)}, bf16[1024,256]{1,0:T(8,128)(2,1)}, u32[]{:S(2)}, u32[]{:S(2)}) collective-permute-start(bf16[1024,256]{1,0:T(8,128)(2,1)} %collective-permute-done.5.refs_4_.refs_5_), channel_id=1, source_target_pairs={{0,6},{2,0},{4,2},{6,4},{1,7},{3,1},{5,3},{7,5},{8,14},{10,8},{12,... | collective-permute-start | bytes 1572872 | tf_op jit(solution)/shard_map/ppermute | solution.py:37
  20.8 1.5 collective-permute-start.9
  24.3 10.1 %forward_part.2 = (f32[1024,1000]{1,0:T(8,128)}, f32[1024,128]{1,0:T(8,128)}, bf16[8,2,1024,256]{3,2,1,0:T(8,128)(2,1)}) custom-call(s32[14]{0:T(128)} %concatenate.3.ids, bf16[1024,256]{1,0:T(8,128)(2,1)} %refs_3_.1, bf16[1024,256]{1,0:T(8,128)(2,1)} %collective-permute-done.2.refs_1_, bf16[1024,256]{1,0:T(8,128)(2,1)} %collective-permute-done.3.refs_2_, ...), custom_call_target="tpu_custom_call" | custom-call | flops 62914560 | bytes 340000 | tf_op jit(solution)/shard_map/forward_part/pallas_call | solution.py:168
  38.4 13.1 %forward_part.3 = (f32[1024,1000]{1,0:T(8,128)}, f32[1024,128]{1,0:T(8,128)}, bf16[8,2,1024,256]{3,2,1,0:T(8,128)(2,1)}) custom-call(s32[14]{0:T(128)} %concatenate.3.ids, bf16[1024,256]{1,0:T(8,128)(2,1)} %collective-permute-done.refs_0_, ...), custom_call_target="tpu_custom_call", output_to_operand_aliasing={{0}: (11, {}), {1}: (12, {}), {2}: (13, {})} | custom-call | flops 83886080 | bytes 400000 | tf_op jit(solution)/shard_map/forward_part/pallas_call | solution.py:168
  51.9 1.9 collective-permute-done.14.a1
  53.8 12.2 %forward_last.1 = (bf16[1024,1000]{1,0:T(8,128)(2,1)}, bf16[8,2,1024,256]{3,2,1,0:T(8,128)(2,1)}, f32[1024,1]{1,0:T(8,128)}, bf16[1024,1000]{1,0:T(8,128)(2,1)}, f32[8,1024]{1,0:T(8,128)}) custom-call(s32[14]{0:T(128)} %concatenate.3.ids, s32[8]{0:T(128)} %lengths.1, bf16[1024,256]{1,0:T(8,128)(2,1)} %touch.3.a0, ...), custom_call_target="tpu_custom_call", output_to_operand_aliasing={{1}: (9, {})} | custom-call | flops 20971520 | bytes 400000 | tf_op jit(solution)/shard_map/forward_last/pallas_call | solution.py:221
  66.1 2.9 %collective-permute-start.15 = (f32[8,1024]{1,0:T(8,128)}, f32[8,1024]{1,0:T(8,128)S(1)}, u32[]{:S(2)}, u32[]{:S(2)}) collective-permute-start(f32[8,1024]{1,0:T(8,128)} %get-tuple-element.56), channel_id=1, source_target_pairs={{0,64},{64,0},{1,65},{65,1},{2,66},{66,2},{3,67},{67,3},{4,68},{68... | collective-permute-start | bytes 98312 | tf_op jit(solution)/shard_map/ppermute | solution.py:41
  68.9 2.8 %collective-permute-done.15 = f32[8,1024]{1,0:T(8,128)S(1)} collective-permute-done((f32[8,1024]{1,0:T(8,128)}, f32[8,1024]{1,0:T(8,128)S(1)}, u32[]{:S(2)}, u32[]{:S(2)}) %collective-permute-start.15) | collective-permute-done | bytes 32800 | tf_op jit(solution)/shard_map/ppermute | solution.py:41
  72.5 1.6 collective-permute-start.16
  74.1 2.9 %collective-permute-start.17 = (f32[2,8,1024]{2,1,0:T(8,128)S(1)}, f32[2,8,1024]{2,1,0:T(8,128)S(1)}, u32[]{:S(2)}, u32[]{:S(2)}) collective-permute-start(f32[2,8,1024]{2,1,0:T(8,128)S(1)} %pad_maximum_fusion.refs_0_), channel_id=1, source_target_pairs={{0,32},{16,48},{32,0},{48,16},{1,33},{17,49},{33,1},{49,17},{2,34}... | collective-permute-start | bytes 196616 | tf_op jit(solution)/shard_map/ppermute | solution.py:41
  77.3 2.8 %collective-permute-done.17.refs_2_ = f32[2,8,1024]{2,1,0:T(8,128)S(1)} collective-permute-done((f32[2,8,1024]{2,1,0:T(8,128)S(1)}, f32[2,8,1024]{2,1,0:T(8,128)S(1)}, u32[]{:S(2)}, u32[]{:S(2)}) %collective-permute-start.17) | collective-permute-done | bytes 65568 | tf_op jit(solution)/shard_map/ppermute | solution.py:41
  80.7 2.0 collective-permute-done.18.refs_3_
  82.6 2.6 %gram.1 = (f32[64,1024]{1,0:T(8,128)}, f32[72,128]{1,0:T(8,128)}) custom-call(s32[14]{0:T(128)} %concatenate.3.ids, f32[2,8,1024]{2,1,0:T(8,128)} %copy-done, f32[2,8,1024]{2,1,0:T(8,128)} %copy-done.2, f32[2,8,1024]{2,1,0:T(8,128)} %copy-done.3, f32[2,8,1024]{2,1,0:T(8,128)} %collective-permute-done.18.refs_3_), custom_call_target="tpu_custom_call" | custom-call | tf_op jit(solution)/shard_map/gram/pallas_call | solution.py:291
  85.2 2.9 %collective-permute-start.20 = (f32[72,128]{1,0:T(8,128)}, f32[72,128]{1,0:T(8,128)S(1)}, u32[]{:S(2)}, u32[]{:S(2)}) collective-permute-start(f32[72,128]{1,0:T(8,128)} %get-tuple-element.58), channel_id=1, source_target_pairs={{0,4},{2,6},{4,0},{6,2},{1,5},{3,7},{5,1},{7,3},{8,12},{10,14},{12... | collective-permute-start | bytes 110600 | tf_op jit(solution)/shard_map/ppermute | solution.py:41
  88.1 1.8 collective-permute-start.21
  90.9 2.6 %collective-permute-done.21 = f32[72,128]{1,0:T(8,128)S(1)} collective-permute-done((f32[72,128]{1,0:T(8,128)}, f32[72,128]{1,0:T(8,128)S(1)}, u32[]{:S(2)}, u32[]{:S(2)}) %collective-permute-start.21) | collective-permute-done | bytes 36896 | tf_op jit(solution)/shard_map/ppermute | solution.py:41
  96.3 2.2 collective-permute-done.23.p2
  99.8 6.6 %logit_grad.1 = (bf16[1024,1000]{1,0:T(8,128)(2,1)}, bf16[1000,1024]{1,0:T(8,128)(2,1)}, f32[16,256]{1,0:T(8,128)}, f32[8,128]{1,0:T(8,128)}) custom-call(s32[14]{0:T(128)} %concatenate.3.ids, f32[64,1024]{1,0:T(8,128)} %get-tuple-element.57.every, f32[72,128]{1,0:T(8,128)} %copy-done.1, f32[72,128]{1,0:T(8,128)} %copy-done.4, f32[72,128]{1,0:T(8,128)} %copy-done.5, ...), custom_call_target="tpu_custom_call" | custom-call | flops 409600 | bytes 240000 | tf_op jit(solution)/shard_map/logit_grad/pallas_call | solution.py:388
  106.3 4.8 %term_part.4.refs_0_ = bf16[1,2,2,528,256]{4,3,2,1,0:T(8,128)(2,1)} custom-call(s32[14]{0:T(128)} %concatenate.3.ids, bf16[1024,1000]{1,0:T(8,128)(2,1)} %get-tuple-element.62.refs_0_.refs_1_, bf16[1000,4096]{1,0:T(8,128)(2,1)} %bitcast.19, bf16[1000,4096]{1,0:T(8,128)(2,1)} %bitcast.20, f32[16,256]{1,0:T(8,128)} %get-tuple-element.63.refs_3_.refs_4_), custom_call_target="tpu_custom_call" | custom-call | flops 20971520 | bytes 103383 | tf_op jit(solution)/shard_map/term_part/pallas_call | solution.py:588
  111.3 7.8 %term_part.5.refs_0_ = bf16[3,2,2,528,256]{4,3,2,1,0:T(8,128)(2,1)} custom-call(s32[14]{0:T(128)} %concatenate.3.ids, bf16[1,2,2,528,256]{4,3,2,1,0:T(8,128)(2,1)} %term_part.4.refs_0_, bf16[1024,1000]{1,0:T(8,128)(2,1)} %get-tuple-element.62.refs_0_.refs_1_, bf16[1000,4096]{1,0:T(8,128)(2,1)} %bitcast.21, bf16[1000,4096]{1,0:T(8,128)(2,1)} %bitcast.22, ...), custom_call_target="tpu_custom_call" | custom-call | flops 62914560000 | bytes 228229120 | tf_op jit(solution)/shard_map/term_part/pallas_call | solution.py:588
  119.4 5.1 %term_part.6 = (bf16[2,528,256]{2,1,0:T(8,128)(2,1)}, bf16[2,528,256]{2,1,0:T(8,128)(2,1)}) custom-call(s32[14]{0:T(128)} %concatenate.3.ids, bf16[3,2,2,528,256]{4,3,2,1,0:T(8,128)(2,1)} %term_part.5.refs_0_, bf16[1024,1000]{1,0:T(8,128)(2,1)} %get-tuple-element.62.refs_0_.refs_1_, bf16[1000,4096]{1,0:T(8,128)(2,1)} %bitcast.23, ...), custom_call_target="tpu_custom_call" | custom-call | flops 20971520 | bytes 103383 | tf_op jit(solution)/shard_map/term_part/pallas_call | solution.py:588
  124.5 3.2 %collective-permute-start.28 = (bf16[2,528,256]{2,1,0:T(8,128)(2,1)}, bf16[2,528,256]{2,1,0:T(8,128)(2,1)}, u32[]{:S(2)}, u32[]{:S(2)}) collective-permute-start(bf16[2,528,256]{2,1,0:T(8,128)(2,1)} %get-tuple-element.68), channel_id=1, source_target_pairs={{0,6},{2,0},{4,2},{6,4},{1,7},{3,1},{5,3},{7,5},{8,14},{10,8},{12,... | collective-permute-start | bytes 1622024 | tf_op jit(solution)/shard_map/ppermute | solution.py:37
  127.7 6.5 %head_part.3 = (bf16[2,560,256]{2,1,0:T(8,128)(2,1)}, bf16[2,560,256]{2,1,0:T(8,128)(2,1)}, bf16[1,2,440,256]{3,2,1,0:T(8,128)(2,1)}, bf16[1,2,440,256]{3,2,1,0:T(8,128)(2,1)}) custom-call(s32[14]{0:T(128)} %concatenate.3.ids, bf16[2,528,256]{2,1,0:T(8,128)(2,1)} %get-tuple-element.64.refs_0_, bf16[1000,1024]{1,0:T(8,128)(2,1)} %get-tuple-element.65.refs_1_.refs_2_, ...), custom_call_target="tpu_custom_call" | custom-call | flops 41943040000 | bytes 123863040 | tf_op jit(solution)/shard_map/head_part/pallas_call | solution.py:475
  134.2 3.2 %collective-permute-start.31 = (bf16[2,560,256]{2,1,0:T(8,128)(2,1)}, bf16[2,560,256]{2,1,0:T(8,128)(2,1)}, u32[]{:S(2)}, u32[]{:S(2)}) collective-permute-start(bf16[2,560,256]{2,1,0:T(8,128)(2,1)} %get-tuple-element.71), channel_id=1, source_target_pairs={{0,48},{16,0},{32,16},{48,32},{1,49},{17,1},{33,17},{49,33},{2,50}... | collective-permute-start | bytes 1720328 | tf_op jit(solution)/shard_map/ppermute | solution.py:37
  137.5 2.9 %collective-permute-done.27.refs_6_ = bf16[2,528,256]{2,1,0:T(8,128)(2,1)} collective-permute-done((bf16[2,528,256]{2,1,0:T(8,128)(2,1)}, bf16[2,528,256]{2,1,0:T(8,128)(2,1)}, u32[]{:S(2)}, u32[]{:S(2)}) %collective-permute-start.27) | collective-permute-done | bytes 540704 | tf_op jit(solution)/shard_map/ppermute | solution.py:37
  140.4 2.7 %collective-permute-start.29 = (bf16[1,2,440,256]{3,2,1,0:T(8,128)(2,1)}, bf16[1,2,440,256]{3,2,1,0:T(8,128)(2,1)}, u32[]{:S(2)}, u32[]{:S(2)}) collective-permute-start(bf16[1,2,440,256]{3,2,1,0:T(8,128)(2,1)} %get-tuple-element.70), channel_id=1, source_target_pairs={{0,64},{64,0},{1,65},{65,1},{2,66},{66,2},{3,67},{67,3},{4,68},{68... | collective-permute-start | bytes 1351688 | tf_op jit(solution)/shard_map/ppermute | solution.py:41
  143.1 10.7 %term_part.7 = (bf16[2,2,528,256]{3,2,1,0:T(8,128)(2,1)}, bf16[2,2,528,256]{3,2,1,0:T(8,128)(2,1)}, bf16[2,2,528,256]{3,2,1,0:T(8,128)(2,1)}) custom-call(s32[14]{0:T(128)} %concatenate.3.ids, bf16[2,560,256]{2,1,0:T(8,128)(2,1)} %get-tuple-element.67.refs_0_, bf16[1024,1000]{1,0:T(8,128)(2,1)} %get-tuple-element.62.refs_0_.refs_1_, ...), custom_call_target="tpu_custom_call" | custom-call | flops 62914560000 | bytes 228229120 | tf_op jit(solution)/shard_map/term_part/pallas_call | solution.py:588
  153.8 3.2 %collective-permute-start.34 = (bf16[2,2,528,256]{3,2,1,0:T(8,128)(2,1)}, bf16[2,2,528,256]{3,2,1,0:T(8,128)(2,1)}, u32[]{:S(2)}, u32[]{:S(2)}) collective-permute-start(bf16[2,2,528,256]{3,2,1,0:T(8,128)(2,1)} %get-tuple-element.76), channel_id=1, source_target_pairs={{0,6},{2,0},{4,2},{6,4},{1,7},{3,1},{5,3},{7,5},{8,14},{10,8},{12,... | collective-permute-start | bytes 3244040 | tf_op jit(solution)/shard_map/ppermute | solution.py:37
  157.0 10.0 %head_part.4 = (bf16[2,2,560,256]{3,2,1,0:T(8,128)(2,1)}, bf16[2,2,560,256]{3,2,1,0:T(8,128)(2,1)}, bf16[2,2,440,256]{3,2,1,0:T(8,128)(2,1)}, bf16[2,2,440,256]{3,2,1,0:T(8,128)(2,1)}) custom-call(s32[14]{0:T(128)} %concatenate.3.ids, bf16[2,2,528,256]{3,2,1,0:T(8,128)(2,1)} %get-tuple-element.69.refs_0_.refs_1_, ...), custom_call_target="tpu_custom_call" | custom-call | flops 83886080000 | bytes 206766080 | tf_op jit(solution)/shard_map/head_part/pallas_call | solution.py:475
  167.1 3.2 %collective-permute-start.37 = (bf16[2,2,560,256]{3,2,1,0:T(8,128)(2,1)}, bf16[2,2,560,256]{3,2,1,0:T(8,128)(2,1)}, u32[]{:S(2)}, u32[]{:S(2)}) collective-permute-start(bf16[2,2,560,256]{3,2,1,0:T(8,128)(2,1)} %get-tuple-element.82), channel_id=1, source_target_pairs={{0,48},{16,0},{32,16},{48,32},{1,49},{17,1},{33,17},{49,33},{2,50}... | collective-permute-start | bytes 3440648 | tf_op jit(solution)/shard_map/ppermute | solution.py:37
  171.1 6.5 %head_part.5 = (bf16[2,2,560,256]{3,2,1,0:T(8,128)(2,1)}, bf16[1,2,440,256]{3,2,1,0:T(8,128)(2,1)}, bf16[1,2,440,256]{3,2,1,0:T(8,128)(2,1)}) custom-call(s32[14]{0:T(128)} %concatenate.3.ids, bf16[2,2,560,256]{3,2,1,0:T(8,128)(2,1)} %get-tuple-element.72.refs_0_, bf16[1000,1024]{1,0:T(8,128)(2,1)} %get-tuple-element.65.refs_1_.refs_2_, ...), custom_call_target="tpu_custom_call" | custom-call | flops 41943040 | bytes 123863 | tf_op jit(solution)/shard_map/head_part/pallas_call | solution.py:475
  177.6 2.5 %collective-permute-done.33.refs_2_ = bf16[2,2,528,256]{3,2,1,0:T(8,128)(2,1)} collective-permute-done((bf16[2,2,528,256]{3,2,1,0:T(8,128)(2,1)}, bf16[2,2,528,256]{3,2,1,0:T(8,128)(2,1)}, u32[]{:S(2)}, u32[]{:S(2)}) %collective-permute-start.33) | collective-permute-done | bytes 1081376 | tf_op jit(solution)/shard_map/ppermute | solution.py:37
  180.9 3.7 %term_sum.1 = (bf16[1024,256]{1,0:T(8,128)(2,1)}, bf16[2,528,256]{2,1,0:T(8,128)(2,1)}, f32[16,256]{1,0:T(8,128)}, f32[1,256]{1,0:T(1,128)}) custom-call(bf16[1,2,440,256]{3,2,1,0:T(8,128)(2,1)} %get-tuple-element.74.refs_0_.keep, bf16[2,2,528,256]{3,2,1,0:T(8,128)(2,1)} %get-tuple-element.69.refs_0_.refs_1_, ...), custom_call_target="tpu_custom_call" | custom-call | flops 20000 | bytes 100000 | tf_op jit(solution)/shard_map/term_sum/pallas_call | solution.py:639
  185.6 9.4 %collective-permute-done.39.b13 = bf16[2,2,440,256]{3,2,1,0:T(8,128)(2,1)} collective-permute-done((bf16[2,2,440,256]{3,2,1,0:T(8,128)(2,1)}, bf16[2,2,440,256]{3,2,1,0:T(8,128)(2,1)}, u32[]{:S(2)}, u32[]{:S(2)}) %collective-permute-start.39) | collective-permute-done | bytes 901152 | tf_op jit(solution)/shard_map/ppermute | solution.py:41
  195.0 2.9 %low_sum.1 = (bf16[2,440,256]{2,1,0:T(8,128)(2,1)}, bf16[2,440,256]{2,1,0:T(8,128)(2,1)}, bf16[2,440,256]{2,1,0:T(8,128)(2,1)}) custom-call(bf16[1024,256]{1,0:T(8,128)(2,1)} %get-tuple-element.77.refs_1_._, bf16[2,2,440,256]{3,2,1,0:T(8,128)(2,1)} %get-tuple-element.83.a13, bf16[2,2,440,256]{3,2,1,0:T(8,128)(2,1)} %collective-permute-done.39.b13, ...), custom_call_target="tpu_custom_call" | custom-call | flops 20 | bytes 80000 | tf_op jit(solution)/shard_map/low_sum/pallas_call | solution.py:502
  199.4 1.8 collective-permute-start.42
  201.2 2.3 fusion
  205.5 9.1 %collective-permute-done.35.refs_2_.refs_5_ = bf16[2,528,256]{2,1,0:T(8,128)(2,1)} collective-permute-done((bf16[2,528,256]{2,1,0:T(8,128)(2,1)}, bf16[2,528,256]{2,1,0:T(8,128)(2,1)}, u32[]{:S(2)}, u32[]{:S(2)}) %collective-permute-start.35) | collective-permute-done | bytes 540704 | tf_op jit(solution)/shard_map/ppermute | solution.py:41
  214.6 2.8 %hidden_grad.1._.refs_0_ = bf16[1024,256]{1,0:T(8,128)(2,1)} custom-call(s32[14]{0:T(128)} %concatenate.3.ids, bf16[1,2,440,256]{3,2,1,0:T(8,128)(2,1)} %collective-permute-done.32.refs_0_.swapped, bf16[1024,256]{1,0:T(8,128)(2,1)} %get-tuple-element.77.refs_1_._, bf16[2,528,256]{2,1,0:T(8,128)(2,1)} %collective-permute-done.35.refs_2_.refs_5_, ...), custom_call_target="tpu_custom_call" | custom-call | flops 20000 | bytes 40000 | tf_op jit(solution)/shard_map/hidden_grad/pallas_call | solution.py:671
  218.7 2.3 collective-permute-start.44
  221.0 2.4 %collective-permute-start.45 = (f32[1,256]{1,0:T(1,128)}, f32[1,256]{1,0:T(1,128)S(1)}, u32[]{:S(2)}, u32[]{:S(2)}) collective-permute-start(f32[1,256]{1,0:T(1,128)} %gain_vocab.1), channel_id=1, source_target_pairs={{0,48},{16,32},{32,16},{48,0},{1,49},{17,33},{33,17},{49,1},{2,50}... | collective-permute-start | bytes 3080 | tf_op jit(solution)/shard_map/ppermute | solution.py:41
  223.8 2.0 collective-permute-done.45
  226.5 1.9 collective-permute-start.46
  229.6 4.3 %join.1._ = bf16[1000,512]{1,0:T(8,128)(2,1)} custom-call(s32[14]{0:T(128)} %concatenate.3.ids, bf16[1024,256]{1,0:T(8,128)(2,1)} %hidden_grad.1._.refs_0_, bf16[2,2,560,256]{3,2,1,0:T(8,128)(2,1)} %get-tuple-element.81.a0, bf16[2,2,560,256]{3,2,1,0:T(8,128)(2,1)} %collective-permute-done.36.ra, bf16[2,2,560,256]{3,2,1,0:T(8,128)(2,1)} %collective-permute-done.37.rb, ...), custom_call_target="tpu_custom_call" | custom-call | flops 20 | bytes 160000 | tf_op jit(solution)/shard_map/join/pallas_call | solution.py:525
  (92 shorter events, 26.4 us)
Async XLA Ops:
  0.6 16.4 %collective-permute-start.3 = (bf16[1024,256]{1,0:T(8,128)(2,1)}, bf16[1024,256]{1,0:T(8,128)(2,1)}, u32[]{:S(2)}, u32[]{:S(2)}) collective-permute-start(bf16[1024,256]{1,0:T(8,128)(2,1)} %refs_3_.1), channel_id=1, source_target_pairs={{0,2},{2,4},{4,6},{6,0},{1,3},{3,5},{5,7},{7,1},{8,10},{10,12},{12... | collective-permute-start | bytes 1572872 | tf_op jit(solution)/shard_map/ppermute | solution.py:37
  2.7 14.4 %collective-permute-start.5 = (bf16[1024,256]{1,0:T(8,128)(2,1)}, bf16[1024,256]{1,0:T(8,128)(2,1)}, u32[]{:S(2)}, u32[]{:S(2)}) collective-permute-start(bf16[1024,256]{1,0:T(8,128)(2,1)} %refs_3_.1), channel_id=1, source_target_pairs={{0,8},{8,0},{1,9},{9,1},{2,10},{10,2},{3,11},{11,3},{4,12},{12,4},... | collective-permute-start | bytes 1572872 | tf_op jit(solution)/shard_map/ppermute | solution.py:41
  4.2 14.1 %collective-permute-start.2 = (bf16[1024,256]{1,0:T(8,128)(2,1)}, bf16[1024,256]{1,0:T(8,128)(2,1)}, u32[]{:S(2)}, u32[]{:S(2)}) collective-permute-start(bf16[1024,256]{1,0:T(8,128)(2,1)} %refs_3_.1), channel_id=1, source_target_pairs={{0,1},{1,0},{2,3},{3,2},{4,5},{5,4},{6,7},{7,6},{8,9},{9,8},{10,11... | collective-permute-start | bytes 1572872 | tf_op jit(solution)/shard_map/ppermute | solution.py:41
  4.2 16.6 %collective-permute-start = (bf16[1024,256]{1,0:T(8,128)(2,1)}, bf16[1024,256]{1,0:T(8,128)(2,1)}, u32[]{:S(2)}, u32[]{:S(2)}) collective-permute-start(bf16[1024,256]{1,0:T(8,128)(2,1)} %refs_3_.1), channel_id=1, source_target_pairs={{0,6},{2,0},{4,2},{6,4},{1,7},{3,1},{5,3},{7,5},{8,14},{10,8},{12,... | collective-permute-start | bytes 1572872 | tf_op jit(solution)/shard_map/ppermute | solution.py:37
  17.1 7.3 %collective-permute-start.4 = (bf16[1024,256]{1,0:T(8,128)(2,1)}, bf16[1024,256]{1,0:T(8,128)(2,1)}, u32[]{:S(2)}, u32[]{:S(2)}) collective-permute-start(bf16[1024,256]{1,0:T(8,128)(2,1)} %collective-permute-done.3.refs_2_), channel_id=1, source_target_pairs={{0,1},{1,0},{2,3},{3,2},{4,5},{5,4},{6,7},{7,6},{8,9},{9,8},{10,11... | collective-permute-start | bytes 1572872 | tf_op jit(solution)/shard_map/ppermute | solution.py:41
  17.1 7.3 %collective-permute-start.6 = (bf16[1024,256]{1,0:T(8,128)(2,1)}, bf16[1024,256]{1,0:T(8,128)(2,1)}, u32[]{:S(2)}, u32[]{:S(2)}) collective-permute-start(bf16[1024,256]{1,0:T(8,128)(2,1)} %collective-permute-done.5.refs_4_.refs_5_), channel_id=1, source_target_pairs={{0,1},{1,0},{2,3},{3,2},{4,5},{5,4},{6,7},{7,6},{8,9},{9,8},{10,11... | collective-permute-start | bytes 1572872 | tf_op jit(solution)/shard_map/ppermute | solution.py:41
  17.6 16.8 %collective-permute-start.7 = (bf16[1024,256]{1,0:T(8,128)(2,1)}, bf16[1024,256]{1,0:T(8,128)(2,1)}, u32[]{:S(2)}, u32[]{:S(2)}) collective-permute-start(bf16[1024,256]{1,0:T(8,128)(2,1)} %collective-permute-done.3.refs_2_), channel_id=1, source_target_pairs={{0,2},{2,4},{4,6},{6,0},{1,3},{3,5},{5,7},{7,1},{8,10},{10,12},{12... | collective-permute-start | bytes 1572872 | tf_op jit(solution)/shard_map/ppermute | solution.py:37
  18.3 16.1 %collective-permute-start.8 = (bf16[1024,256]{1,0:T(8,128)(2,1)}, bf16[1024,256]{1,0:T(8,128)(2,1)}, u32[]{:S(2)}, u32[]{:S(2)}) collective-permute-start(bf16[1024,256]{1,0:T(8,128)(2,1)} %collective-permute-done.5.refs_4_.refs_5_), channel_id=1, source_target_pairs={{0,6},{2,0},{4,2},{6,4},{1,7},{3,1},{5,3},{7,5},{8,14},{10,8},{12,... | collective-permute-start | bytes 1572872 | tf_op jit(solution)/shard_map/ppermute | solution.py:37
  20.8 13.6 %collective-permute-start.9 = (bf16[1024,256]{1,0:T(8,128)(2,1)}, bf16[1024,256]{1,0:T(8,128)(2,1)}, u32[]{:S(2)}, u32[]{:S(2)}) collective-permute-start(bf16[1024,256]{1,0:T(8,128)(2,1)} %collective-permute-done.3.refs_2_), channel_id=1, source_target_pairs={{0,8},{8,0},{1,9},{9,1},{2,10},{10,2},{3,11},{11,3},{4,12},{12,4},... | collective-permute-start | bytes 1572872 | tf_op jit(solution)/shard_map/ppermute | solution.py:41
  24.3 12.1 %collective-permute-start.1 = (bf16[1024,256]{1,0:T(8,128)(2,1)}, bf16[1024,256]{1,0:T(8,128)(2,1)}, u32[]{:S(2)}, u32[]{:S(2)}) collective-permute-start(bf16[1024,256]{1,0:T(8,128)(2,1)} %collective-permute-done.refs_0_), channel_id=1, source_target_pairs={{0,1},{1,0},{2,3},{3,2},{4,5},{5,4},{6,7},{7,6},{8,9},{9,8},{10,11... | collective-permute-start | bytes 1572872 | tf_op jit(solution)/shard_map/ppermute | solution.py:41
  34.4 2.4 %collective-permute-start.10 = (bf16[1024,256]{1,0:T(8,128)(2,1)}, bf16[1024,256]{1,0:T(8,128)(2,1)}, u32[]{:S(2)}, u32[]{:S(2)}) collective-permute-start(bf16[1024,256]{1,0:T(8,128)(2,1)} %get-tuple-element.48.refs_2_), channel_id=1, source_target_pairs={{0,1},{1,0},{2,3},{3,2},{4,5},{5,4},{6,7},{7,6},{8,9},{9,8},{10,11... | collective-permute-start | bytes 1572872 | tf_op jit(solution)/shard_map/ppermute | solution.py:41
  35.0 2.6 %collective-permute-start.11 = (bf16[1024,256]{1,0:T(8,128)(2,1)}, bf16[1024,256]{1,0:T(8,128)(2,1)}, u32[]{:S(2)}, u32[]{:S(2)}) collective-permute-start(bf16[1024,256]{1,0:T(8,128)(2,1)} %get-tuple-element.49.refs_4_), channel_id=1, source_target_pairs={{0,1},{1,0},{2,3},{3,2},{4,5},{5,4},{6,7},{7,6},{8,9},{9,8},{10,11... | collective-permute-start | bytes 1572872 | tf_op jit(solution)/shard_map/ppermute | solution.py:41
  35.1 3.3 %collective-permute-start.12 = (bf16[1024,256]{1,0:T(8,128)(2,1)}, bf16[1024,256]{1,0:T(8,128)(2,1)}, u32[]{:S(2)}, u32[]{:S(2)}) collective-permute-start(bf16[1024,256]{1,0:T(8,128)(2,1)} %get-tuple-element.50.refs_6_), channel_id=1, source_target_pairs={{0,1},{1,0},{2,3},{3,2},{4,5},{5,4},{6,7},{7,6},{8,9},{9,8},{10,11... | collective-permute-start | bytes 1572872 | tf_op jit(solution)/shard_map/ppermute | solution.py:41
  35.5 15.9 %collective-permute-start.13 = (bf16[1024,256]{1,0:T(8,128)(2,1)}, bf16[1024,256]{1,0:T(8,128)(2,1)}, u32[]{:S(2)}, u32[]{:S(2)}) collective-permute-start(bf16[1024,256]{1,0:T(8,128)(2,1)} %get-tuple-element.48.refs_2_), channel_id=1, source_target_pairs={{0,8},{8,0},{1,9},{9,1},{2,10},{10,2},{3,11},{11,3},{4,12},{12,4},... | collective-permute-start | bytes 1572872 | tf_op jit(solution)/shard_map/ppermute | solution.py:41
  51.5 2.3 collective-permute-start.14
  66.1 5.7 %collective-permute-start.15 = (f32[8,1024]{1,0:T(8,128)}, f32[8,1024]{1,0:T(8,128)S(1)}, u32[]{:S(2)}, u32[]{:S(2)}) collective-permute-start(f32[8,1024]{1,0:T(8,128)} %get-tuple-element.56), channel_id=1, source_target_pairs={{0,64},{64,0},{1,65},{65,1},{2,66},{66,2},{3,67},{67,3},{4,68},{68... | collective-permute-start | bytes 98312 | tf_op jit(solution)/shard_map/ppermute | solution.py:41
  72.5 4.7 %collective-permute-start.16 = (f32[2,8,1024]{2,1,0:T(8,128)S(1)}, f32[2,8,1024]{2,1,0:T(8,128)S(1)}, u32[]{:S(2)}, u32[]{:S(2)}) collective-permute-start(f32[2,8,1024]{2,1,0:T(8,128)S(1)} %pad_maximum_fusion.refs_0_), channel_id=1, source_target_pairs={{0,16},{16,0},{32,48},{48,32},{1,17},{17,1},{33,49},{49,33},{2,18}... | collective-permute-start | bytes 196616 | tf_op jit(solution)/shard_map/ppermute | solution.py:41
  74.1 5.9 %collective-permute-start.17 = (f32[2,8,1024]{2,1,0:T(8,128)S(1)}, f32[2,8,1024]{2,1,0:T(8,128)S(1)}, u32[]{:S(2)}, u32[]{:S(2)}) collective-permute-start(f32[2,8,1024]{2,1,0:T(8,128)S(1)} %pad_maximum_fusion.refs_0_), channel_id=1, source_target_pairs={{0,32},{16,48},{32,0},{48,16},{1,33},{17,49},{33,1},{49,17},{2,34}... | collective-permute-start | bytes 196616 | tf_op jit(solution)/shard_map/ppermute | solution.py:41
  77.0 5.6 %collective-permute-start.18 = (f32[2,8,1024]{2,1,0:T(8,128)S(1)}, f32[2,8,1024]{2,1,0:T(8,128)}, u32[]{:S(2)}, u32[]{:S(2)}) collective-permute-start(f32[2,8,1024]{2,1,0:T(8,128)S(1)} %pad_maximum_fusion.refs_0_), channel_id=1, source_target_pairs={{0,48},{16,32},{32,16},{48,0},{1,49},{17,33},{33,17},{49,1},{2,50}... | collective-permute-start | bytes 196616 | tf_op jit(solution)/shard_map/ppermute | solution.py:41
  85.2 4.7 %collective-permute-start.19 = (f32[72,128]{1,0:T(8,128)}, f32[72,128]{1,0:T(8,128)S(1)}, u32[]{:S(2)}, u32[]{:S(2)}) collective-permute-start(f32[72,128]{1,0:T(8,128)} %get-tuple-element.58), channel_id=1, source_target_pairs={{0,2},{2,0},{4,6},{6,4},{1,3},{3,1},{5,7},{7,5},{8,10},{10,8},{12,... | collective-permute-start | bytes 110600 | tf_op jit(solution)/shard_map/ppermute | solution.py:41
  85.2 5.7 %collective-permute-start.20 = (f32[72,128]{1,0:T(8,128)}, f32[72,128]{1,0:T(8,128)S(1)}, u32[]{:S(2)}, u32[]{:S(2)}) collective-permute-start(f32[72,128]{1,0:T(8,128)} %get-tuple-element.58), channel_id=1, source_target_pairs={{0,4},{2,6},{4,0},{6,2},{1,5},{3,7},{5,1},{7,3},{8,12},{10,14},{12... | collective-permute-start | bytes 110600 | tf_op jit(solution)/shard_map/ppermute | solution.py:41
  88.1 5.4 %collective-permute-start.21 = (f32[72,128]{1,0:T(8,128)}, f32[72,128]{1,0:T(8,128)S(1)}, u32[]{:S(2)}, u32[]{:S(2)}) collective-permute-start(f32[72,128]{1,0:T(8,128)} %get-tuple-element.58), channel_id=1, source_target_pairs={{0,6},{2,4},{4,2},{6,0},{1,7},{3,5},{5,3},{7,1},{8,14},{10,12},{12... | collective-permute-start | bytes 110600 | tf_op jit(solution)/shard_map/ppermute | solution.py:41
  94.3 2.0 collective-permute-start.22
  94.4 4.0 %collective-permute-start.23 = (f32[72,128]{1,0:T(8,128)S(1)}, f32[72,128]{1,0:T(8,128)S(1)}, u32[]{:S(2)}, u32[]{:S(2)}) collective-permute-start(f32[72,128]{1,0:T(8,128)S(1)} %add_add_fusion.p0), channel_id=1, source_target_pairs={{0,8},{8,0},{1,9},{9,1},{2,10},{10,2},{3,11},{11,3},{4,12},{12,4},... | collective-permute-start | bytes 110600 | tf_op jit(solution)/shard_map/ppermute | solution.py:41
  95.7 3.4 %collective-permute-start.24 = (f32[72,128]{1,0:T(8,128)S(1)}, f32[72,128]{1,0:T(8,128)S(1)}, u32[]{:S(2)}, u32[]{:S(2)}) collective-permute-start(f32[72,128]{1,0:T(8,128)S(1)} %add_add_fusion.p0), channel_id=1, source_target_pairs={{0,9},{1,8},{8,1},{9,0},{2,11},{3,10},{10,3},{11,2},{4,13},{5,12},... | collective-permute-start | bytes 110600 | tf_op jit(solution)/shard_map/ppermute | solution.py:749
  111.1 8.3 %collective-permute-start.25 = (bf16[1,2,2,528,256]{4,3,2,1,0:T(8,128)(2,1)}, bf16[1,2,2,528,256]{4,3,2,1,0:T(8,128)(2,1)}, u32[]{:S(2)}, u32[]{:S(2)}) collective-permute-start(bf16[1,2,2,528,256]{4,3,2,1,0:T(8,128)(2,1)} %term_part.4.refs_0_), channel_id=1, source_target_pairs={{0,1},{1,0},{2,3},{3,2},{4,5},{5,4},{6,7},{7,6},{8,9},{9,8},{10,11... | collective-permute-start | bytes 3244040 | tf_op jit(solution)/shard_map/ppermute | solution.py:41
  119.0 24.1 %collective-permute-start.26 = (bf16[3,2,2,528,256]{4,3,2,1,0:T(8,128)(2,1)}, bf16[3,2,2,528,256]{4,3,2,1,0:T(8,128)(2,1)}, u32[]{:S(2)}, u32[]{:S(2)}) collective-permute-start(bf16[3,2,2,528,256]{4,3,2,1,0:T(8,128)(2,1)} %term_part.5.refs_0_), channel_id=1, source_target_pairs={{0,1},{1,0},{2,3},{3,2},{4,5},{5,4},{6,7},{7,6},{8,9},{9,8},{10,11... | collective-permute-start | bytes 9732104 | tf_op jit(solution)/shard_map/ppermute | solution.py:41
  124.5 15.9 %collective-permute-start.27 = (bf16[2,528,256]{2,1,0:T(8,128)(2,1)}, bf16[2,528,256]{2,1,0:T(8,128)(2,1)}, u32[]{:S(2)}, u32[]{:S(2)}) collective-permute-start(bf16[2,528,256]{2,1,0:T(8,128)(2,1)} %get-tuple-element.64.refs_0_), channel_id=1, source_target_pairs={{0,2},{2,4},{4,6},{6,0},{1,3},{3,5},{5,7},{7,1},{8,10},{10,12},{12... | collective-permute-start | bytes 1622024 | tf_op jit(solution)/shard_map/ppermute | solution.py:37
  124.5 18.6 %collective-permute-start.28 = (bf16[2,528,256]{2,1,0:T(8,128)(2,1)}, bf16[2,528,256]{2,1,0:T(8,128)(2,1)}, u32[]{:S(2)}, u32[]{:S(2)}) collective-permute-start(bf16[2,528,256]{2,1,0:T(8,128)(2,1)} %get-tuple-element.68), channel_id=1, source_target_pairs={{0,6},{2,0},{4,2},{6,4},{1,7},{3,1},{5,3},{7,5},{8,14},{10,8},{12,... | collective-permute-start | bytes 1622024 | tf_op jit(solution)/shard_map/ppermute | solution.py:37
  134.2 22.8 %collective-permute-start.30 = (bf16[2,560,256]{2,1,0:T(8,128)(2,1)}, bf16[2,560,256]{2,1,0:T(8,128)(2,1)}, u32[]{:S(2)}, u32[]{:S(2)}) collective-permute-start(bf16[2,560,256]{2,1,0:T(8,128)(2,1)} %get-tuple-element.67.refs_0_), channel_id=1, source_target_pairs={{0,16},{16,32},{32,48},{48,0},{1,17},{17,33},{33,49},{49,1},{2,18}... | collective-permute-start | bytes 1720328 | tf_op jit(solution)/shard_map/ppermute | solution.py:37
  134.2 22.8 %collective-permute-start.31 = (bf16[2,560,256]{2,1,0:T(8,128)(2,1)}, bf16[2,560,256]{2,1,0:T(8,128)(2,1)}, u32[]{:S(2)}, u32[]{:S(2)}) collective-permute-start(bf16[2,560,256]{2,1,0:T(8,128)(2,1)} %get-tuple-element.71), channel_id=1, source_target_pairs={{0,48},{16,0},{32,16},{48,32},{1,49},{17,1},{33,17},{49,33},{2,50}... | collective-permute-start | bytes 1720328 | tf_op jit(solution)/shard_map/ppermute | solution.py:37
  140.4 16.6 %collective-permute-start.29 = (bf16[1,2,440,256]{3,2,1,0:T(8,128)(2,1)}, bf16[1,2,440,256]{3,2,1,0:T(8,128)(2,1)}, u32[]{:S(2)}, u32[]{:S(2)}) collective-permute-start(bf16[1,2,440,256]{3,2,1,0:T(8,128)(2,1)} %get-tuple-element.70), channel_id=1, source_target_pairs={{0,64},{64,0},{1,65},{65,1},{2,66},{66,2},{3,67},{67,3},{4,68},{68... | collective-permute-start | bytes 1351688 | tf_op jit(solution)/shard_map/ppermute | solution.py:41
  153.8 26.3 %collective-permute-start.33 = (bf16[2,2,528,256]{3,2,1,0:T(8,128)(2,1)}, bf16[2,2,528,256]{3,2,1,0:T(8,128)(2,1)}, u32[]{:S(2)}, u32[]{:S(2)}) collective-permute-start(bf16[2,2,528,256]{3,2,1,0:T(8,128)(2,1)} %get-tuple-element.75), channel_id=1, source_target_pairs={{0,2},{2,4},{4,6},{6,0},{1,3},{3,5},{5,7},{7,1},{8,10},{10,12},{12... | collective-permute-start | bytes 3244040 | tf_op jit(solution)/shard_map/ppermute | solution.py:37
  153.8 27.1 %collective-permute-start.34 = (bf16[2,2,528,256]{3,2,1,0:T(8,128)(2,1)}, bf16[2,2,528,256]{3,2,1,0:T(8,128)(2,1)}, u32[]{:S(2)}, u32[]{:S(2)}) collective-permute-start(bf16[2,2,528,256]{3,2,1,0:T(8,128)(2,1)} %get-tuple-element.76), channel_id=1, source_target_pairs={{0,6},{2,0},{4,2},{6,4},{1,7},{3,1},{5,3},{7,5},{8,14},{10,8},{12,... | collective-permute-start | bytes 3244040 | tf_op jit(solution)/shard_map/ppermute | solution.py:37
  167.0 30.9 %collective-permute-start.36 = (bf16[2,2,560,256]{3,2,1,0:T(8,128)(2,1)}, bf16[2,2,560,256]{3,2,1,0:T(8,128)(2,1)}, u32[]{:S(2)}, u32[]{:S(2)}) collective-permute-start(bf16[2,2,560,256]{3,2,1,0:T(8,128)(2,1)} %get-tuple-element.72.refs_0_), channel_id=1, source_target_pairs={{0,16},{16,32},{32,48},{48,0},{1,17},{17,33},{33,49},{49,1},{2,18}... | collective-permute-start | bytes 3440648 | tf_op jit(solution)/shard_map/ppermute | solution.py:37
  167.1 32.3 %collective-permute-start.37 = (bf16[2,2,560,256]{3,2,1,0:T(8,128)(2,1)}, bf16[2,2,560,256]{3,2,1,0:T(8,128)(2,1)}, u32[]{:S(2)}, u32[]{:S(2)}) collective-permute-start(bf16[2,2,560,256]{3,2,1,0:T(8,128)(2,1)} %get-tuple-element.82), channel_id=1, source_target_pairs={{0,48},{16,0},{32,16},{48,32},{1,49},{17,1},{33,17},{49,33},{2,50}... | collective-permute-start | bytes 3440648 | tf_op jit(solution)/shard_map/ppermute | solution.py:37
  170.3 24.8 %collective-permute-start.39 = (bf16[2,2,440,256]{3,2,1,0:T(8,128)(2,1)}, bf16[2,2,440,256]{3,2,1,0:T(8,128)(2,1)}, u32[]{:S(2)}, u32[]{:S(2)}) collective-permute-start(bf16[2,2,440,256]{3,2,1,0:T(8,128)(2,1)} %get-tuple-element.84), channel_id=1, source_target_pairs={{0,64},{64,0},{1,65},{65,1},{2,66},{66,2},{3,67},{67,3},{4,68},{68... | collective-permute-start | bytes 2703368 | tf_op jit(solution)/shard_map/ppermute | solution.py:41
  180.1 24.6 %collective-permute-start.32 = (bf16[1,2,440,256]{3,2,1,0:T(8,128)(2,1)}, bf16[1,2,440,256]{3,2,1,0:T(8,128)(2,1)}, u32[]{:S(2)}, u32[]{:S(2)}) collective-permute-start(bf16[1,2,440,256]{3,2,1,0:T(8,128)(2,1)} %get-tuple-element.73), channel_id=1, source_target_pairs={{0,64},{64,0},{1,65},{65,1},{2,66},{66,2},{3,67},{67,3},{4,68},{68... | collective-permute-start | bytes 1351688 | tf_op jit(solution)/shard_map/ppermute | solution.py:41
  184.6 30.0 %collective-permute-start.35 = (bf16[2,528,256]{2,1,0:T(8,128)(2,1)}, bf16[2,528,256]{2,1,0:T(8,128)(2,1)}, u32[]{:S(2)}, u32[]{:S(2)}) collective-permute-start(bf16[2,528,256]{2,1,0:T(8,128)(2,1)} %get-tuple-element.78), channel_id=1, source_target_pairs={{0,8},{8,0},{1,9},{9,1},{2,10},{10,2},{3,11},{11,3},{4,12},{12,4},... | collective-permute-start | bytes 1622024 | tf_op jit(solution)/shard_map/ppermute | solution.py:41
  197.9 19.5 %collective-permute-start.40 = (bf16[2,440,256]{2,1,0:T(8,128)(2,1)}, bf16[2,440,256]{2,1,0:T(8,128)(2,1)}, u32[]{:S(2)}, u32[]{:S(2)}) collective-permute-start(bf16[2,440,256]{2,1,0:T(8,128)(2,1)} %get-tuple-element.86), channel_id=1, source_target_pairs={{0,16},{16,32},{32,48},{48,0},{1,17},{17,33},{33,49},{49,1},{2,18}... | collective-permute-start | bytes 1351688 | tf_op jit(solution)/shard_map/ppermute | solution.py:37
  197.9 19.5 %collective-permute-start.41 = (bf16[2,440,256]{2,1,0:T(8,128)(2,1)}, bf16[2,440,256]{2,1,0:T(8,128)(2,1)}, u32[]{:S(2)}, u32[]{:S(2)}) collective-permute-start(bf16[2,440,256]{2,1,0:T(8,128)(2,1)} %get-tuple-element.87), channel_id=1, source_target_pairs={{0,32},{16,48},{32,0},{48,16},{1,33},{17,49},{33,1},{49,17},{2,34}... | collective-permute-start | bytes 1351688 | tf_op jit(solution)/shard_map/ppermute | solution.py:37
  199.4 18.0 %collective-permute-start.42 = (bf16[2,440,256]{2,1,0:T(8,128)(2,1)}, bf16[2,440,256]{2,1,0:T(8,128)(2,1)}, u32[]{:S(2)}, u32[]{:S(2)}) collective-permute-start(bf16[2,440,256]{2,1,0:T(8,128)(2,1)} %get-tuple-element.88), channel_id=1, source_target_pairs={{0,48},{16,0},{32,16},{48,32},{1,49},{17,1},{33,17},{49,33},{2,50}... | collective-permute-start | bytes 1351688 | tf_op jit(solution)/shard_map/ppermute | solution.py:37
  204.7 24.9 %collective-permute-start.38 = (bf16[2,560,256]{2,1,0:T(8,128)(2,1)}, bf16[2,560,256]{2,1,0:T(8,128)(2,1)}, u32[]{:S(2)}, u32[]{:S(2)}) collective-permute-start(bf16[2,560,256]{2,1,0:T(8,128)(2,1)} %fusion), channel_id=1, source_target_pairs={{0,64},{64,0},{1,65},{65,1},{2,66},{66,2},{3,67},{67,3},{4,68},{68... | collective-permute-start | bytes 1720328 | tf_op jit(solution)/shard_map/ppermute | solution.py:41
  218.7 4.7 %collective-permute-start.43 = (f32[1,256]{1,0:T(1,128)}, f32[1,256]{1,0:T(1,128)S(1)}, u32[]{:S(2)}, u32[]{:S(2)}) collective-permute-start(f32[1,256]{1,0:T(1,128)} %gain_vocab.1), channel_id=1, source_target_pairs={{0,16},{16,0},{32,48},{48,32},{1,17},{17,1},{33,49},{49,33},{2,18}... | collective-permute-start | bytes 3080 | tf_op jit(solution)/shard_map/ppermute | solution.py:41
  218.7 5.1 %collective-permute-start.44 = (f32[1,256]{1,0:T(1,128)}, f32[1,256]{1,0:T(1,128)S(1)}, u32[]{:S(2)}, u32[]{:S(2)}) collective-permute-start(f32[1,256]{1,0:T(1,128)} %gain_vocab.1), channel_id=1, source_target_pairs={{0,32},{16,48},{32,0},{48,16},{1,33},{17,49},{33,1},{49,17},{2,34}... | collective-permute-start | bytes 3080 | tf_op jit(solution)/shard_map/ppermute | solution.py:41
  221.0 4.8 %collective-permute-start.45 = (f32[1,256]{1,0:T(1,128)}, f32[1,256]{1,0:T(1,128)S(1)}, u32[]{:S(2)}, u32[]{:S(2)}) collective-permute-start(f32[1,256]{1,0:T(1,128)} %gain_vocab.1), channel_id=1, source_target_pairs={{0,48},{16,32},{32,16},{48,0},{1,49},{17,33},{33,17},{49,1},{2,50}... | collective-permute-start | bytes 3080 | tf_op jit(solution)/shard_map/ppermute | solution.py:41
  226.5 7.4 %copy-start.7 = (f32[1,256]{1,0:T(1,128)}, f32[1,256]{1,0:T(1,128)S(1)}, u32[]{:S(2)}) copy-start(f32[1,256]{1,0:T(1,128)S(1)} %add_add_fusion.1.a) | copy-start | bytes 3076
  226.5 7.4 %collective-permute-start.46 = (f32[1,256]{1,0:T(1,128)S(1)}, f32[1,256]{1,0:T(1,128)S(1)}, u32[]{:S(2)}, u32[]{:S(2)}) collective-permute-start(f32[1,256]{1,0:T(1,128)S(1)} %add_add_fusion.1.a), channel_id=1, source_target_pairs={{0,64},{64,0},{1,65},{65,1},{2,66},{66,2},{3,67},{67,3},{4,68},{68... | collective-permute-start | bytes 3080 | tf_op jit(solution)/shard_map/ppermute | solution.py:41
  (8 other events, 18.2 us)

commit v2 on v1

--- a/solution.py
+++ b/solution.py
@@ -19,7 +19,7 @@
 LEN = 128
 TERMS = 1000
 BLK = 256
-ROWS_A = 560
+ROWS_A = 688
 ROWS_B = TERMS - ROWS_A
 HALF = TOK // 2
 PER = 2
@@ -493,21 +493,58 @@
     )(ids, *after, ht, x, gain, *adds)
 
 
-def low_sum_kernel(_, a13, b13, a2, b2, out_1, out_3, out_2):
+def gain_rows(gain):
+    rows = []
+    for m in range(2):
+        value = gain[m : m + 1, :]
+        high = value.astype(bf16).astype(f32)
+        rows += [high, value - high]
+    return jnp.concatenate(rows + [jnp.zeros((12, BLK), f32)], axis=0).astype(bf16)
+
+
+def low_sum_kernel(_, gain, a13, b13, a2, b2, out_1, out_3, out_2):
     for a, b, i, out in ((a13, b13, 0, out_1), (a13, b13, 1, out_3), (a2, b2, 0, out_2)):
-        out[...] = (a[i].astype(f32) + b[i].astype(f32)).astype(bf16)
+        out[0, 0:16, :] = gain_rows(gain)
+        out[1, 0:16, :] = jnp.zeros((16, BLK), bf16)
+        out[:, 16:, :] = (a[i].astype(f32) + b[i].astype(f32)).astype(bf16)
 
 
 def low_sum(after, *parts):
     return pl.pallas_call(
         low_sum_kernel,
-        out_shape=[jax.ShapeDtypeStruct((2, ROWS_B, BLK), bf16)] * 3,
-        in_specs=[ANY] + [VMEM] * 4,
+        out_shape=[jax.ShapeDtypeStruct((2, 16 + ROWS_B, BLK), bf16)] * 3,
+        in_specs=[ANY] + [VMEM] * 5,
         out_specs=[VMEM] * 3,
         compiler_params=params(),
         cost_estimate=cost(1000, 4_000_000),
         name="low_sum",
     )(after, *parts)
+
+
+def gain_kernel(ids, gain, l1, l2, l3, out, held):
+    for back, rows in enumerate((gain_rows(gain), l1[0], l2[0], l3[0])):
+        values = rows.astype(f32)
+        held[(ids[1] - back) & 3] = jnp.concatenate(
+            [values[0:1] + values[1:2], values[2:3] + values[3:4], jnp.zeros((6, BLK), f32)], axis=0
+        )
+    out[...] = (held[0] + held[1]) + (held[2] + held[3])
+
+
+def gain_along_y(ids, after, gain, *low):
+    return pl.pallas_call(
+        later(len(after), gain_kernel),
+        grid=(1,),
+        out_shape=jax.ShapeDtypeStruct((8, BLK), f32),
+        in_specs=[SMEM]
+        + [ANY] * len(after)
+        + [pl.BlockSpec((2, BLK), lambda k: (0, 0))]
+        + [pl.BlockSpec((1, 16, BLK), lambda k: (0, 0, 0))] * 3,
+        out_specs=pl.BlockSpec((8, BLK), lambda k: (0, 0)),
+        scratch_shapes=[pltpu.VMEM((4, 8, BLK), f32)],
+        compiler_params=params(),
+        cost_estimate=cost(1000, 50_000),
+        name="gain_along_y",
+    )(ids, *after, gain, *low)
 
 
 def join_kernel(ids, _, a0, ra, rb, got, keep, swapped, b1, b2, b3, out):
@@ -517,7 +554,7 @@
         out[0:ROWS_A, cols] = total.astype(bf16)
         total = keep[0, side].astype(f32) + swapped[0, side].astype(f32)
         for b in (b1, b2, b3):
-            total = total + b[side].astype(f32)
+            total = total + b[side, 16:, :].astype(f32)
         out[ROWS_A:TERMS, cols] = total.astype(bf16)
 
 
@@ -625,13 +662,8 @@
                     at = half * HALF + first
                     product = total * values[at : at + 128, :].astype(f32)
                     sums[m] = sums[m] + jnp.sum(product.reshape(16, 8, BLK), axis=0)
-    gain[...] = jnp.sum(sums[0], axis=0, keepdims=True)
-    other = jnp.sum(sums[1], axis=0, keepdims=True)
-    high = other.astype(bf16).astype(f32)
-    row = lax.broadcasted_iota(jnp.int32, (16, 1), 0)
-    tail = send[0, HALF:, :].astype(f32)
-    tail = jnp.where(row == 2, high, jnp.where(row == 3, other - high, tail))
-    send[0, HALF:, :] = tail.astype(bf16)
+    for m in range(2):
+        gain[m : m + 1, :] = jnp.sum(sums[m], axis=0, keepdims=True)
 
 
 def term_sum(after, own, ra, rb, x, x_p):
@@ -642,7 +674,7 @@
             jax.ShapeDtypeStruct((TOK, BLK), bf16),
             jax.ShapeDtypeStruct((2, ROWS_T, BLK), bf16),
             jax.ShapeDtypeStruct((16, BLK), f32),
-            jax.ShapeDtypeStruct((1, BLK), f32),
+            jax.ShapeDtypeStruct((2, BLK), f32),
         ],
         in_specs=[ANY] * count + [VMEM] * 5,
         out_specs=[VMEM] * 4,
@@ -677,43 +709,6 @@
         cost_estimate=cost(1_000_000, 2_000_000),
         name="hidden_grad",
     )(ids, *after, n, got, x, gain, inv, dots)
-
-
-def gain_vocab(after, partial, got):
-    count = len(after)
-
-    def kernel(*refs):
-        sums, tail, out = refs[count:]
-        rows = tail[0].astype(f32)
-        out[...] = sums[...] + rows[2:3] + rows[3:4]
-
-    return pl.pallas_call(
-        kernel,
-        grid=(1,),
-        out_shape=jax.ShapeDtypeStruct((1, BLK), f32),
-        in_specs=[ANY] * count
-        + [pl.BlockSpec((1, BLK), lambda k: (0, 0)), pl.BlockSpec((1, 16, BLK), lambda k: (0, HALF // 16, 0))],
-        out_specs=pl.BlockSpec((1, BLK), lambda k: (0, 0)),
-        compiler_params=params(),
-        cost_estimate=cost(1000, 5000),
-        name="gain_vocab",
-    )(*after, partial, got)
-
-
-def gain_sum_kernel(_, a, b, out):
-    out[...] = a[...] + b[...]
-
-
-def gain_sum(after, a, b):
-    return pl.pallas_call(
-        gain_sum_kernel,
-        out_shape=jax.ShapeDtypeStruct((1, BLK), f32),
-        in_specs=[ANY] + [VMEM] * 2,
-        out_specs=VMEM,
-        compiler_params=params(),
-        cost_estimate=cost(1000, 5000),
-        name="gain_sum",
-    )(after, a, b)
 
 
 def shards(hidden, norm_gain, head_weight, lengths, positives, negatives):
@@ -764,18 +759,18 @@
     a_1, a_3, keep_13, send_13 = head_part(ids, (1, 3), ht, x, gain, (t_0, swap_2), adds=adds, weight=20)
     swap_13 = swap(send_13, "xh")
     ra, rb = shift(a_1, "y", 1), shift(a_3, "y", -1)
-    a_0, keep_0, send_0 = head_part(ids, (0,), ht, x, gain, (a_1,))
-    keep, send, dots, partial = term_sum((keep_0,), t_0, shift(t_1, "z", 1), shift(t_3, "z", -1), hidden, x_p)
+    keep, send, dots, partial = term_sum((), t_0, shift(t_1, "z", 1), shift(t_3, "z", -1), hidden, x_p)
+    a_0, keep_0, send_0 = head_part(ids, (0,), ht, x, gain, (a_1, keep), weight=20)
     swap_0 = swap(send_0, "xh")
     got = swap(a_0[1] + ra[1] + rb[1], "xh")
-    low_1, low_3, low_2 = low_sum(keep, keep_13, swap_13, keep_2, swap_2)
+    low_1, low_3, low_2 = low_sum(swap_0, partial, keep_13, swap_13, keep_2, swap_2)
     low = [shift(low_1, "y", 1), shift(low_2, "y", 2), shift(low_3, "y", 3)]
-    got_term = swap(send, "xl")
-    hidden_grad = final(ids, (swap_0,), keep, got_term, hidden, gain, inv, dots)
-    gain_grad = gain_vocab((hidden_grad, *low), partial, got_term)
-    gain_grad = (gain_grad + swap(gain_grad, "y", 1)) + (swap(gain_grad, "y", 2) + swap(gain_grad, "y", 3))
+    hidden_grad = final(ids, (), keep, swap(send, "xl"), hidden, gain, inv, dots)
+    gain_grad = gain_along_y(ids, (hidden_grad, swap_0), partial, *low)
+    gain_grad = gain_grad + swap(gain_grad, "xh")
+    gain_grad = gain_grad[0] + swap(gain_grad[1], "xl")
     head_t = join(ids, hidden_grad, a_0, ra, rb, got, keep_0, swap_0, *low)
-    return losses[0, :3], hidden_grad, head_t.T, gain_sum(head_t, gain_grad, swap(gain_grad, "xh"))[0]
+    return losses[0, :3], hidden_grad, head_t.T, gain_grad
 
 
 def solution(mesh):

time: 237 us -> 236 us (level)
  waiting for transfers between devices: 56.3 us -> 62.7 us
  starting transfers between devices: 57.2 us -> 51.8 us
    ppermute x15, waiting for transfers between devices: 16.1 us -> 26.6 us  [shift(): return lax.ppermute(x, axis, [(i, (i + step) % n) for i in range(n)])]
    ppermute x31 -> x29, starting transfers between devices: 32.9 us -> 27.2 us  [swap(): return lax.ppermute(x, axis, [(i, i ^ bits) for i in range(SIZES[axis])])]
    ppermute x31 -> x29, waiting for transfers between devices: 39.4 us -> 35.5 us  [swap(): return lax.ppermute(x, axis, [(i, i ^ bits) for i in range(SIZES[axis])])]
    pallas_call x3 -> x2, Pallas kernels: 5.39 us -> 3.93 us  [the longest x1 2.51 us: low_sum(): pl.pallas_call(low_sum_kernel, out_shape=[jax.ShapeDtypeStruct((2, 16 + R...]
  transfers between devices with their start and end apart: 47 -> 45, of which waited for: 19 -> 19; matrix products, arithmetic and copies ran while one was open for 3% -> 3% of each run, Pallas kernels for 36% -> 34%
where the time goes in v2:
time: 236 us; the launch traced here: 235 us
  Pallas kernels  110 us (47%)
  waiting for transfers between devices  62.7 us (27%)
  starting transfers between devices  51.8 us (22%)
  other arithmetic  5.3 us (2%)
  local copies, waits for them, and re-layouts  4.5 us (2%)
    ppermute x29, waiting for transfers between devices, swap(): return lax.ppermute(x, axis, [(i, i ^ bits) for i in range(SIZES[axis])])  35.5 us
    pallas_call x4, Pallas kernels, term_part(): pl.pallas_call(later(len(after), functools.partial(term_kernel, count, sp...  28.2 us
    ppermute x29, starting transfers between devices, swap(): return lax.ppermute(x, axis, [(i, i ^ bits) for i in range(SIZES[axis])])  27.2 us
    ppermute x15, waiting for transfers between devices, shift(): return lax.ppermute(x, axis, [(i, (i + step) % n) for i in range(n)])  26.6 us
    ppermute x15, starting transfers between devices, shift(): return lax.ppermute(x, axis, [(i, (i + step) % n) for i in range(n)])  23.9 us
    pallas_call x2, Pallas kernels, forward(): pl.pallas_call(functools.partial(forward_kernel, places, not state), out_...  23.1 us
    pallas_call x3, Pallas kernels, head_part(): pl.pallas_call(later(len(after), functools.partial(head_kernel, steps, sp...  22.9 us
    pallas_call x1, Pallas kernels, forward_last(): pl.pallas_call(functools.partial(forward_last_kernel, place), out_shape=[...  12.3 us
  transfers between devices with their start and end apart: 45, of which 19 were waited for; matrix products, arithmetic and copies ran while one was open for 3% of the time, Pallas kernels for 34%

profile of v2, /device:TPU:0, one launch (start us, length us, event | category | flops | bytes accessed | tf_op | source)
XLA Modules:
  0.0 235.3 jit_solution(10747912907654610175)
XLA Ops:
  0.6 2.1 collective-permute-start.3
  2.7 1.5 collective-permute-start.5
  4.2 2.2 collective-permute-start
  6.4 10.7 %collective-permute-done.3.refs_2_ = bf16[1024,256]{1,0:T(8,128)(2,1)} collective-permute-done((bf16[1024,256]{1,0:T(8,128)(2,1)}, bf16[1024,256]{1,0:T(8,128)(2,1)}, u32[]{:S(2)}, u32[]{:S(2)}) %collective-permute-start.3) | collective-permute-done | bytes 524320 | tf_op jit(solution)/shard_map/ppermute | solution.py:37
  18.3 2.5 %collective-permute-start.8 = (bf16[1024,256]{1,0:T(8,128)(2,1)}, bf16[1024,256]{1,0:T(8,128)(2,1)}, u32[]{:S(2)}, u32[]{:S(2)}) collective-permute-start(bf16[1024,256]{1,0:T(8,128)(2,1)} %collective-permute-done.5.refs_4_), channel_id=1, source_target_pairs={{0,6},{2,0},{4,2},{6,4},{1,7},{3,1},{5,3},{7,5},{8,14},{10,8},{12,... | collective-permute-start | bytes 1572872 | tf_op jit(solution)/shard_map/ppermute | solution.py:37
  20.8 1.5 collective-permute-start.9
  24.4 10.1 %forward_part.2 = (f32[1024,1000]{1,0:T(8,128)}, f32[1024,128]{1,0:T(8,128)}, bf16[8,2,1024,256]{3,2,1,0:T(8,128)(2,1)}) custom-call(s32[14]{0:T(128)} %concatenate.3.ids, bf16[1024,256]{1,0:T(8,128)(2,1)} %refs_2_.1, bf16[1024,256]{1,0:T(8,128)(2,1)} %collective-permute-done.2.refs_1_, bf16[1024,256]{1,0:T(8,128)(2,1)} %collective-permute-done.3.refs_2_, ...), custom_call_target="tpu_custom_call" | custom-call | flops 62914560 | bytes 340000 | tf_op jit(solution)/shard_map/forward_part/pallas_call | solution.py:168
  38.4 13.1 %forward_part.3 = (f32[1024,1000]{1,0:T(8,128)}, f32[1024,128]{1,0:T(8,128)}, bf16[8,2,1024,256]{3,2,1,0:T(8,128)(2,1)}) custom-call(s32[14]{0:T(128)} %concatenate.3.ids, bf16[1024,256]{1,0:T(8,128)(2,1)} %collective-permute-done.refs_0_, ...), custom_call_target="tpu_custom_call", output_to_operand_aliasing={{0}: (11, {}), {1}: (12, {}), {2}: (13, {})} | custom-call | flops 83886080 | bytes 400000 | tf_op jit(solution)/shard_map/forward_part/pallas_call | solution.py:168
  52.0 1.9 collective-permute-done.14.a1
  53.9 12.3 %forward_last.1 = (bf16[1024,1000]{1,0:T(8,128)(2,1)}, bf16[8,2,1024,256]{3,2,1,0:T(8,128)(2,1)}, f32[1024,1]{1,0:T(8,128)}, bf16[1024,1000]{1,0:T(8,128)(2,1)}, f32[8,1024]{1,0:T(8,128)}) custom-call(s32[14]{0:T(128)} %concatenate.3.ids, s32[8]{0:T(128)} %lengths.1, bf16[1024,256]{1,0:T(8,128)(2,1)} %touch.3.a0, ...), custom_call_target="tpu_custom_call", output_to_operand_aliasing={{1}: (9, {})} | custom-call | flops 20971520 | bytes 400000 | tf_op jit(solution)/shard_map/forward_last/pallas_call | solution.py:221
  66.1 2.8 %collective-permute-start.15 = (f32[8,1024]{1,0:T(8,128)}, f32[8,1024]{1,0:T(8,128)S(1)}, u32[]{:S(2)}, u32[]{:S(2)}) collective-permute-start(f32[8,1024]{1,0:T(8,128)} %get-tuple-element.56), channel_id=1, source_target_pairs={{0,64},{64,0},{1,65},{65,1},{2,66},{66,2},{3,67},{67,3},{4,68},{68... | collective-permute-start | bytes 98312 | tf_op jit(solution)/shard_map/ppermute | solution.py:41
  69.0 2.9 %collective-permute-done.15 = f32[8,1024]{1,0:T(8,128)S(1)} collective-permute-done((f32[8,1024]{1,0:T(8,128)}, f32[8,1024]{1,0:T(8,128)S(1)}, u32[]{:S(2)}, u32[]{:S(2)}) %collective-permute-start.15) | collective-permute-done | bytes 32800 | tf_op jit(solution)/shard_map/ppermute | solution.py:41
  72.6 1.6 collective-permute-start.16
  74.2 2.9 %collective-permute-start.17 = (f32[2,8,1024]{2,1,0:T(8,128)S(1)}, f32[2,8,1024]{2,1,0:T(8,128)S(1)}, u32[]{:S(2)}, u32[]{:S(2)}) collective-permute-start(f32[2,8,1024]{2,1,0:T(8,128)S(1)} %pad_maximum_fusion.refs_0_), channel_id=1, source_target_pairs={{0,32},{16,48},{32,0},{48,16},{1,33},{17,49},{33,1},{49,17},{2,34}... | collective-permute-start | bytes 196616 | tf_op jit(solution)/shard_map/ppermute | solution.py:41
  77.3 2.8 %collective-permute-done.17.refs_2_ = f32[2,8,1024]{2,1,0:T(8,128)S(1)} collective-permute-done((f32[2,8,1024]{2,1,0:T(8,128)S(1)}, f32[2,8,1024]{2,1,0:T(8,128)S(1)}, u32[]{:S(2)}, u32[]{:S(2)}) %collective-permute-start.17) | collective-permute-done | bytes 65568 | tf_op jit(solution)/shard_map/ppermute | solution.py:41
  80.8 2.0 collective-permute-done.18.refs_3_
  82.7 2.6 %gram.1 = (f32[64,1024]{1,0:T(8,128)}, f32[72,128]{1,0:T(8,128)}) custom-call(s32[14]{0:T(128)} %concatenate.3.ids, f32[2,8,1024]{2,1,0:T(8,128)} %copy-done, f32[2,8,1024]{2,1,0:T(8,128)} %copy-done.2, f32[2,8,1024]{2,1,0:T(8,128)} %copy-done.3, f32[2,8,1024]{2,1,0:T(8,128)} %collective-permute-done.18.refs_3_), custom_call_target="tpu_custom_call" | custom-call | tf_op jit(solution)/shard_map/gram/pallas_call | solution.py:291
  85.3 2.9 %collective-permute-start.20 = (f32[72,128]{1,0:T(8,128)}, f32[72,128]{1,0:T(8,128)S(1)}, u32[]{:S(2)}, u32[]{:S(2)}) collective-permute-start(f32[72,128]{1,0:T(8,128)} %get-tuple-element.58), channel_id=1, source_target_pairs={{0,4},{2,6},{4,0},{6,2},{1,5},{3,7},{5,1},{7,3},{8,12},{10,14},{12... | collective-permute-start | bytes 110600 | tf_op jit(solution)/shard_map/ppermute | solution.py:41
  88.2 1.8 collective-permute-start.21
  91.0 2.6 %collective-permute-done.21 = f32[72,128]{1,0:T(8,128)S(1)} collective-permute-done((f32[72,128]{1,0:T(8,128)}, f32[72,128]{1,0:T(8,128)S(1)}, u32[]{:S(2)}, u32[]{:S(2)}) %collective-permute-start.21) | collective-permute-done | bytes 36896 | tf_op jit(solution)/shard_map/ppermute | solution.py:41
  96.3 2.2 collective-permute-done.23.p2
  99.8 6.6 %logit_grad.1 = (bf16[1024,1000]{1,0:T(8,128)(2,1)}, bf16[1000,1024]{1,0:T(8,128)(2,1)}, f32[16,256]{1,0:T(8,128)}, f32[8,128]{1,0:T(8,128)}) custom-call(s32[14]{0:T(128)} %concatenate.3.ids, f32[64,1024]{1,0:T(8,128)} %get-tuple-element.57.every, f32[72,128]{1,0:T(8,128)} %copy-done.1, f32[72,128]{1,0:T(8,128)} %copy-done.4, f32[72,128]{1,0:T(8,128)} %copy-done.5, ...), custom_call_target="tpu_custom_call" | custom-call | flops 409600 | bytes 240000 | tf_op jit(solution)/shard_map/logit_grad/pallas_call | solution.py:388
  106.4 4.7 %term_part.4.refs_0_ = bf16[1,2,2,528,256]{4,3,2,1,0:T(8,128)(2,1)} custom-call(s32[14]{0:T(128)} %concatenate.3.ids, bf16[1024,1000]{1,0:T(8,128)(2,1)} %get-tuple-element.62.refs_0_.refs_1_, bf16[1000,4096]{1,0:T(8,128)(2,1)} %bitcast.20, bf16[1000,4096]{1,0:T(8,128)(2,1)} %bitcast.21, f32[16,256]{1,0:T(8,128)} %get-tuple-element.63.refs_3_.refs_4_), custom_call_target="tpu_custom_call" | custom-call | flops 20971520 | bytes 103383 | tf_op jit(solution)/shard_map/term_part/pallas_call | solution.py:625
  111.2 7.7 %term_part.5.refs_0_ = bf16[3,2,2,528,256]{4,3,2,1,0:T(8,128)(2,1)} custom-call(s32[14]{0:T(128)} %concatenate.3.ids, bf16[1,2,2,528,256]{4,3,2,1,0:T(8,128)(2,1)} %term_part.4.refs_0_, bf16[1024,1000]{1,0:T(8,128)(2,1)} %get-tuple-element.62.refs_0_.refs_1_, bf16[1000,4096]{1,0:T(8,128)(2,1)} %bitcast.22, bf16[1000,4096]{1,0:T(8,128)(2,1)} %bitcast.23, ...), custom_call_target="tpu_custom_call" | custom-call | flops 62914560000 | bytes 228229120 | tf_op jit(solution)/shard_map/term_part/pallas_call | solution.py:625
  119.3 5.1 %term_part.6 = (bf16[2,528,256]{2,1,0:T(8,128)(2,1)}, bf16[2,528,256]{2,1,0:T(8,128)(2,1)}) custom-call(s32[14]{0:T(128)} %concatenate.3.ids, bf16[3,2,2,528,256]{4,3,2,1,0:T(8,128)(2,1)} %term_part.5.refs_0_, bf16[1024,1000]{1,0:T(8,128)(2,1)} %get-tuple-element.62.refs_0_.refs_1_, bf16[1000,4096]{1,0:T(8,128)(2,1)} %bitcast.24, ...), custom_call_target="tpu_custom_call" | custom-call | flops 20971520 | bytes 103383 | tf_op jit(solution)/shard_map/term_part/pallas_call | solution.py:625
  124.4 3.2 %collective-permute-start.28 = (bf16[2,528,256]{2,1,0:T(8,128)(2,1)}, bf16[2,528,256]{2,1,0:T(8,128)(2,1)}, u32[]{:S(2)}, u32[]{:S(2)}) collective-permute-start(bf16[2,528,256]{2,1,0:T(8,128)(2,1)} %get-tuple-element.68), channel_id=1, source_target_pairs={{0,6},{2,0},{4,2},{6,4},{1,7},{3,1},{5,3},{7,5},{8,14},{10,8},{12,... | collective-permute-start | bytes 1622024 | tf_op jit(solution)/shard_map/ppermute | solution.py:37
  127.6 6.4 %head_part.3 = (bf16[2,688,256]{2,1,0:T(8,128)(2,1)}, bf16[2,688,256]{2,1,0:T(8,128)(2,1)}, bf16[1,2,312,256]{3,2,1,0:T(8,128)(2,1)}, bf16[1,2,312,256]{3,2,1,0:T(8,128)(2,1)}) custom-call(s32[14]{0:T(128)} %concatenate.3.ids, bf16[2,528,256]{2,1,0:T(8,128)(2,1)} %get-tuple-element.64.refs_0_, bf16[1000,1024]{1,0:T(8,128)(2,1)} %get-tuple-element.65.refs_1_.refs_2_, ...), custom_call_target="tpu_custom_call" | custom-call | flops 41943040000 | bytes 123863040 | tf_op jit(solution)/shard_map/head_part/pallas_call | solution.py:475
  134.1 3.2 %collective-permute-start.34 = (bf16[2,688,256]{2,1,0:T(8,128)(2,1)}, bf16[2,688,256]{2,1,0:T(8,128)(2,1)}, u32[]{:S(2)}, u32[]{:S(2)}) collective-permute-start(bf16[2,688,256]{2,1,0:T(8,128)(2,1)} %get-tuple-element.77), channel_id=1, source_target_pairs={{0,48},{16,0},{32,16},{48,32},{1,49},{17,1},{33,17},{49,33},{2,50}... | collective-permute-start | bytes 2113544 | tf_op jit(solution)/shard_map/ppermute | solution.py:37
  137.3 2.9 %collective-permute-done.27.refs_6_ = bf16[2,528,256]{2,1,0:T(8,128)(2,1)} collective-permute-done((bf16[2,528,256]{2,1,0:T(8,128)(2,1)}, bf16[2,528,256]{2,1,0:T(8,128)(2,1)}, u32[]{:S(2)}, u32[]{:S(2)}) %collective-permute-start.27) | collective-permute-done | bytes 540704 | tf_op jit(solution)/shard_map/ppermute | solution.py:37
  140.2 2.7 %collective-permute-start.32 = (bf16[1,2,312,256]{3,2,1,0:T(8,128)(2,1)}, bf16[1,2,312,256]{3,2,1,0:T(8,128)(2,1)}, u32[]{:S(2)}, u32[]{:S(2)}) collective-permute-start(bf16[1,2,312,256]{3,2,1,0:T(8,128)(2,1)} %get-tuple-element.76), channel_id=1, source_target_pairs={{0,64},{64,0},{1,65},{65,1},{2,66},{66,2},{3,67},{67,3},{4,68},{68... | collective-permute-start | bytes 958472 | tf_op jit(solution)/shard_map/ppermute | solution.py:41
  143.0 10.7 %term_part.7 = (bf16[2,2,528,256]{3,2,1,0:T(8,128)(2,1)}, bf16[2,2,528,256]{3,2,1,0:T(8,128)(2,1)}, bf16[2,2,528,256]{3,2,1,0:T(8,128)(2,1)}) custom-call(s32[14]{0:T(128)} %concatenate.3.ids, bf16[2,688,256]{2,1,0:T(8,128)(2,1)} %get-tuple-element.67.refs_0_, bf16[1024,1000]{1,0:T(8,128)(2,1)} %get-tuple-element.62.refs_0_.refs_1_, ...), custom_call_target="tpu_custom_call" | custom-call | flops 62914560000 | bytes 228229120 | tf_op jit(solution)/shard_map/term_part/pallas_call | solution.py:625
  153.7 3.2 %collective-permute-start.30 = (bf16[2,2,528,256]{3,2,1,0:T(8,128)(2,1)}, bf16[2,2,528,256]{3,2,1,0:T(8,128)(2,1)}, u32[]{:S(2)}, u32[]{:S(2)}) collective-permute-start(bf16[2,2,528,256]{3,2,1,0:T(8,128)(2,1)} %get-tuple-element.71), channel_id=1, source_target_pairs={{0,6},{2,0},{4,2},{6,4},{1,7},{3,1},{5,3},{7,5},{8,14},{10,8},{12,... | collective-permute-start | bytes 3244040 | tf_op jit(solution)/shard_map/ppermute | solution.py:37
  156.9 10.0 %head_part.4 = (bf16[2,2,688,256]{3,2,1,0:T(8,128)(2,1)}, bf16[2,2,688,256]{3,2,1,0:T(8,128)(2,1)}, bf16[2,2,312,256]{3,2,1,0:T(8,128)(2,1)}, bf16[2,2,312,256]{3,2,1,0:T(8,128)(2,1)}) custom-call(s32[14]{0:T(128)} %concatenate.3.ids, bf16[2,2,528,256]{3,2,1,0:T(8,128)(2,1)} %get-tuple-element.69.refs_0_, ...), custom_call_target="tpu_custom_call" | custom-call | flops 83886080000 | bytes 206766080 | tf_op jit(solution)/shard_map/head_part/pallas_call | solution.py:475
  167.7 3.2 %collective-permute-start.36 = (bf16[2,2,688,256]{3,2,1,0:T(8,128)(2,1)}, bf16[2,2,688,256]{3,2,1,0:T(8,128)(2,1)}, u32[]{:S(2)}, u32[]{:S(2)}) collective-permute-start(bf16[2,2,688,256]{3,2,1,0:T(8,128)(2,1)} %get-tuple-element.80), channel_id=1, source_target_pairs={{0,48},{16,0},{32,16},{48,32},{1,49},{17,1},{33,17},{49,33},{2,50}... | collective-permute-start | bytes 4227080 | tf_op jit(solution)/shard_map/ppermute | solution.py:37
  171.0 9.0 %collective-permute-done.29.refs_1_ = bf16[2,2,528,256]{3,2,1,0:T(8,128)(2,1)} collective-permute-done((bf16[2,2,528,256]{3,2,1,0:T(8,128)(2,1)}, bf16[2,2,528,256]{3,2,1,0:T(8,128)(2,1)}, u32[]{:S(2)}, u32[]{:S(2)}) %collective-permute-start.29) | collective-permute-done | bytes 1081376 | tf_op jit(solution)/shard_map/ppermute | solution.py:37
  180.0 3.5 %term_sum.1 = (bf16[1024,256]{1,0:T(8,128)(2,1)}, bf16[2,528,256]{2,1,0:T(8,128)(2,1)}, f32[16,256]{1,0:T(8,128)}, f32[2,256]{1,0:T(2,128)}) custom-call(bf16[2,2,528,256]{3,2,1,0:T(8,128)(2,1)} %get-tuple-element.69.refs_0_, bf16[2,2,528,256]{3,2,1,0:T(8,128)(2,1)} %collective-permute-done.29.refs_1_, ...), custom_call_target="tpu_custom_call" | custom-call | flops 20000 | bytes 100000 | tf_op jit(solution)/shard_map/term_sum/pallas_call | solution.py:671
  183.5 6.4 %head_part.5 = (bf16[2,2,688,256]{3,2,1,0:T(8,128)(2,1)}, bf16[1,2,312,256]{3,2,1,0:T(8,128)(2,1)}, bf16[1,2,312,256]{3,2,1,0:T(8,128)(2,1)}) custom-call(s32[14]{0:T(128)} %concatenate.3.ids, bf16[2,2,688,256]{3,2,1,0:T(8,128)(2,1)} %get-tuple-element.78.refs_0_, bf16[1024,256]{1,0:T(8,128)(2,1)} %get-tuple-element.72.refs_0_.refs_1_, ...), custom_call_target="tpu_custom_call" | custom-call | flops 41943040000 | bytes 123863040 | tf_op jit(solution)/shard_map/head_part/pallas_call | solution.py:475
  191.8 10.5 %collective-permute-done.38._.swapped.refs_1_ = bf16[1,2,312,256]{3,2,1,0:T(8,128)(2,1)} collective-permute-done((bf16[1,2,312,256]{3,2,1,0:T(8,128)(2,1)}, bf16[1,2,312,256]{3,2,1,0:T(8,128)(2,1)}, u32[]{:S(2)}, u32[]{:S(2)}) %collective-permute-start.38) | collective-permute-done | bytes 319520 | tf_op jit(solution)/shard_map/ppermute | solution.py:41
  202.2 2.5 %low_sum.1 = (bf16[2,328,256]{2,1,0:T(8,128)(2,1)}, bf16[2,328,256]{2,1,0:T(8,128)(2,1)}, bf16[2,328,256]{2,1,0:T(8,128)(2,1)}) custom-call(bf16[1,2,312,256]{3,2,1,0:T(8,128)(2,1)} %collective-permute-done.38._.swapped.refs_1_, f32[2,256]{1,0:T(2,128)} %get-tuple-element.83.gain.refs_2_, bf16[2,2,312,256]{3,2,1,0:T(8,128)(2,1)} %get-tuple-element.84.a13, ...), custom_call_target="tpu_custom_call" | custom-call | flops 20 | bytes 80000 | tf_op jit(solution)/shard_map/low_sum/pallas_call | solution.py:513
  204.8 1.7 collective-permute-start.41
  206.5 1.7 collective-permute-start.42
  208.2 2.5 %fusion = bf16[2,688,256]{2,1,0:T(8,128)(2,1)} fusion(bf16[2,2,688,256]{3,2,1,0:T(8,128)(2,1)} %collective-permute-done.36.rb, bf16[2,2,688,256]{3,2,1,0:T(8,128)(2,1)} %collective-permute-done.35.ra, bf16[2,2,688,256]{3,2,1,0:T(8,128)(2,1)} %get-tuple-element.79.a0), kind=kLoop, calls=%fused_computation.1 | loop fusion | flops 704512 | bytes 2818048 | tf_op jit(solution)/shard_map/add | solution.py:765
  211.5 2.8 %hidden_grad.1._.refs_0_ = bf16[1024,256]{1,0:T(8,128)(2,1)} custom-call(s32[14]{0:T(128)} %concatenate.3.ids, bf16[1024,256]{1,0:T(8,128)(2,1)} %get-tuple-element.72.refs_0_.refs_1_, bf16[2,528,256]{2,1,0:T(8,128)(2,1)} %collective-permute-done.31.refs_1_, bf16[1024,256]{1,0:T(8,128)(2,1)} %refs_2_.1, f32[1,4096]{1,0:T(1,128)} %bitcast.35, ...), custom_call_target="tpu_custom_call" | custom-call | flops 20000 | bytes 40000 | tf_op jit(solution)/shard_map/hidden_grad/pallas_call | solution.py:703
  214.3 3.3 %collective-permute-done.40.b1.refs_3_ = bf16[2,328,256]{2,1,0:T(8,128)(2,1)} collective-permute-done((bf16[2,328,256]{2,1,0:T(8,128)(2,1)}, bf16[2,328,256]{2,1,0:T(8,128)(2,1)}, u32[]{:S(2)}, u32[]{:S(2)}) %collective-permute-start.40) | collective-permute-done | bytes 335904 | tf_op jit(solution)/shard_map/ppermute | solution.py:37
  218.2 1.4 gain_along_y.1
  220.4 5.7 %collective-permute-done.43 = f32[8,256]{1,0:T(8,128)S(1)} collective-permute-done((f32[8,256]{1,0:T(8,128)}, f32[8,256]{1,0:T(8,128)S(1)}, u32[]{:S(2)}, u32[]{:S(2)}) %collective-permute-start.43) | collective-permute-done | bytes 8224 | tf_op jit(solution)/shard_map/ppermute | solution.py:41
  228.3 2.1 collective-permute-done.44
  231.0 4.3 %join.1 = bf16[1000,512]{1,0:T(8,128)(2,1)} custom-call(s32[14]{0:T(128)} %concatenate.3.ids, bf16[1024,256]{1,0:T(8,128)(2,1)} %hidden_grad.1._.refs_0_, bf16[2,2,688,256]{3,2,1,0:T(8,128)(2,1)} %get-tuple-element.79.a0, bf16[2,2,688,256]{3,2,1,0:T(8,128)(2,1)} %collective-permute-done.35.ra, bf16[2,2,688,256]{3,2,1,0:T(8,128)(2,1)} %collective-permute-done.36.rb, ...), custom_call_target="tpu_custom_call" | custom-call | flops 20 | bytes 160000 | tf_op jit(solution)/shard_map/join/pallas_call | solution.py:562
  (85 shorter events, 22.5 us)
Async XLA Ops:
  0.6 16.4 %collective-permute-start.3 = (bf16[1024,256]{1,0:T(8,128)(2,1)}, bf16[1024,256]{1,0:T(8,128)(2,1)}, u32[]{:S(2)}, u32[]{:S(2)}) collective-permute-start(bf16[1024,256]{1,0:T(8,128)(2,1)} %refs_2_.1), channel_id=1, source_target_pairs={{0,2},{2,4},{4,6},{6,0},{1,3},{3,5},{5,7},{7,1},{8,10},{10,12},{12... | collective-permute-start | bytes 1572872 | tf_op jit(solution)/shard_map/ppermute | solution.py:37
  2.7 14.4 %collective-permute-start.5 = (bf16[1024,256]{1,0:T(8,128)(2,1)}, bf16[1024,256]{1,0:T(8,128)(2,1)}, u32[]{:S(2)}, u32[]{:S(2)}) collective-permute-start(bf16[1024,256]{1,0:T(8,128)(2,1)} %refs_2_.1), channel_id=1, source_target_pairs={{0,8},{8,0},{1,9},{9,1},{2,10},{10,2},{3,11},{11,3},{4,12},{12,4},... | collective-permute-start | bytes 1572872 | tf_op jit(solution)/shard_map/ppermute | solution.py:41
  4.2 14.1 %collective-permute-start.2 = (bf16[1024,256]{1,0:T(8,128)(2,1)}, bf16[1024,256]{1,0:T(8,128)(2,1)}, u32[]{:S(2)}, u32[]{:S(2)}) collective-permute-start(bf16[1024,256]{1,0:T(8,128)(2,1)} %refs_2_.1), channel_id=1, source_target_pairs={{0,1},{1,0},{2,3},{3,2},{4,5},{5,4},{6,7},{7,6},{8,9},{9,8},{10,11... | collective-permute-start | bytes 1572872 | tf_op jit(solution)/shard_map/ppermute | solution.py:41
  4.2 16.6 %collective-permute-start = (bf16[1024,256]{1,0:T(8,128)(2,1)}, bf16[1024,256]{1,0:T(8,128)(2,1)}, u32[]{:S(2)}, u32[]{:S(2)}) collective-permute-start(bf16[1024,256]{1,0:T(8,128)(2,1)} %refs_2_.1), channel_id=1, source_target_pairs={{0,6},{2,0},{4,2},{6,4},{1,7},{3,1},{5,3},{7,5},{8,14},{10,8},{12,... | collective-permute-start | bytes 1572872 | tf_op jit(solution)/shard_map/ppermute | solution.py:37
  17.1 7.3 %collective-permute-start.4 = (bf16[1024,256]{1,0:T(8,128)(2,1)}, bf16[1024,256]{1,0:T(8,128)(2,1)}, u32[]{:S(2)}, u32[]{:S(2)}) collective-permute-start(bf16[1024,256]{1,0:T(8,128)(2,1)} %collective-permute-done.3.refs_2_), channel_id=1, source_target_pairs={{0,1},{1,0},{2,3},{3,2},{4,5},{5,4},{6,7},{7,6},{8,9},{9,8},{10,11... | collective-permute-start | bytes 1572872 | tf_op jit(solution)/shard_map/ppermute | solution.py:41
  17.1 7.3 %collective-permute-start.6 = (bf16[1024,256]{1,0:T(8,128)(2,1)}, bf16[1024,256]{1,0:T(8,128)(2,1)}, u32[]{:S(2)}, u32[]{:S(2)}) collective-permute-start(bf16[1024,256]{1,0:T(8,128)(2,1)} %collective-permute-done.5.refs_4_), channel_id=1, source_target_pairs={{0,1},{1,0},{2,3},{3,2},{4,5},{5,4},{6,7},{7,6},{8,9},{9,8},{10,11... | collective-permute-start | bytes 1572872 | tf_op jit(solution)/shard_map/ppermute | solution.py:41
  17.6 16.9 %collective-permute-start.7 = (bf16[1024,256]{1,0:T(8,128)(2,1)}, bf16[1024,256]{1,0:T(8,128)(2,1)}, u32[]{:S(2)}, u32[]{:S(2)}) collective-permute-start(bf16[1024,256]{1,0:T(8,128)(2,1)} %collective-permute-done.3.refs_2_), channel_id=1, source_target_pairs={{0,2},{2,4},{4,6},{6,0},{1,3},{3,5},{5,7},{7,1},{8,10},{10,12},{12... | collective-permute-start | bytes 1572872 | tf_op jit(solution)/shard_map/ppermute | solution.py:37
  18.3 16.1 %collective-permute-start.8 = (bf16[1024,256]{1,0:T(8,128)(2,1)}, bf16[1024,256]{1,0:T(8,128)(2,1)}, u32[]{:S(2)}, u32[]{:S(2)}) collective-permute-start(bf16[1024,256]{1,0:T(8,128)(2,1)} %collective-permute-done.5.refs_4_), channel_id=1, source_target_pairs={{0,6},{2,0},{4,2},{6,4},{1,7},{3,1},{5,3},{7,5},{8,14},{10,8},{12,... | collective-permute-start | bytes 1572872 | tf_op jit(solution)/shard_map/ppermute | solution.py:37
  20.8 13.6 %collective-permute-start.9 = (bf16[1024,256]{1,0:T(8,128)(2,1)}, bf16[1024,256]{1,0:T(8,128)(2,1)}, u32[]{:S(2)}, u32[]{:S(2)}) collective-permute-start(bf16[1024,256]{1,0:T(8,128)(2,1)} %collective-permute-done.3.refs_2_), channel_id=1, source_target_pairs={{0,8},{8,0},{1,9},{9,1},{2,10},{10,2},{3,11},{11,3},{4,12},{12,4},... | collective-permute-start | bytes 1572872 | tf_op jit(solution)/shard_map/ppermute | solution.py:41
  24.4 12.1 %collective-permute-start.1 = (bf16[1024,256]{1,0:T(8,128)(2,1)}, bf16[1024,256]{1,0:T(8,128)(2,1)}, u32[]{:S(2)}, u32[]{:S(2)}) collective-permute-start(bf16[1024,256]{1,0:T(8,128)(2,1)} %collective-permute-done.refs_0_), channel_id=1, source_target_pairs={{0,1},{1,0},{2,3},{3,2},{4,5},{5,4},{6,7},{7,6},{8,9},{9,8},{10,11... | collective-permute-start | bytes 1572872 | tf_op jit(solution)/shard_map/ppermute | solution.py:41
  34.5 2.4 %collective-permute-start.10 = (bf16[1024,256]{1,0:T(8,128)(2,1)}, bf16[1024,256]{1,0:T(8,128)(2,1)}, u32[]{:S(2)}, u32[]{:S(2)}) collective-permute-start(bf16[1024,256]{1,0:T(8,128)(2,1)} %get-tuple-element.48.refs_2_), channel_id=1, source_target_pairs={{0,1},{1,0},{2,3},{3,2},{4,5},{5,4},{6,7},{7,6},{8,9},{9,8},{10,11... | collective-permute-start | bytes 1572872 | tf_op jit(solution)/shard_map/ppermute | solution.py:41
  35.0 2.6 %collective-permute-start.11 = (bf16[1024,256]{1,0:T(8,128)(2,1)}, bf16[1024,256]{1,0:T(8,128)(2,1)}, u32[]{:S(2)}, u32[]{:S(2)}) collective-permute-start(bf16[1024,256]{1,0:T(8,128)(2,1)} %get-tuple-element.49.refs_4_), channel_id=1, source_target_pairs={{0,1},{1,0},{2,3},{3,2},{4,5},{5,4},{6,7},{7,6},{8,9},{9,8},{10,11... | collective-permute-start | bytes 1572872 | tf_op jit(solution)/shard_map/ppermute | solution.py:41
  35.1 3.3 %collective-permute-start.12 = (bf16[1024,256]{1,0:T(8,128)(2,1)}, bf16[1024,256]{1,0:T(8,128)(2,1)}, u32[]{:S(2)}, u32[]{:S(2)}) collective-permute-start(bf16[1024,256]{1,0:T(8,128)(2,1)} %get-tuple-element.50.refs_6_), channel_id=1, source_target_pairs={{0,1},{1,0},{2,3},{3,2},{4,5},{5,4},{6,7},{7,6},{8,9},{9,8},{10,11... | collective-permute-start | bytes 1572872 | tf_op jit(solution)/shard_map/ppermute | solution.py:41
  35.6 15.9 %collective-permute-start.13 = (bf16[1024,256]{1,0:T(8,128)(2,1)}, bf16[1024,256]{1,0:T(8,128)(2,1)}, u32[]{:S(2)}, u32[]{:S(2)}) collective-permute-start(bf16[1024,256]{1,0:T(8,128)(2,1)} %get-tuple-element.48.refs_2_), channel_id=1, source_target_pairs={{0,8},{8,0},{1,9},{9,1},{2,10},{10,2},{3,11},{11,3},{4,12},{12,4},... | collective-permute-start | bytes 1572872 | tf_op jit(solution)/shard_map/ppermute | solution.py:41
  51.5 2.3 collective-permute-start.14
  66.1 5.7 %collective-permute-start.15 = (f32[8,1024]{1,0:T(8,128)}, f32[8,1024]{1,0:T(8,128)S(1)}, u32[]{:S(2)}, u32[]{:S(2)}) collective-permute-start(f32[8,1024]{1,0:T(8,128)} %get-tuple-element.56), channel_id=1, source_target_pairs={{0,64},{64,0},{1,65},{65,1},{2,66},{66,2},{3,67},{67,3},{4,68},{68... | collective-permute-start | bytes 98312 | tf_op jit(solution)/shard_map/ppermute | solution.py:41
  72.6 4.5 %copy-start = (f32[2,8,1024]{2,1,0:T(8,128)}, f32[2,8,1024]{2,1,0:T(8,128)S(1)}, u32[]{:S(2)}) copy-start(f32[2,8,1024]{2,1,0:T(8,128)S(1)} %pad_maximum_fusion.refs_0_) | copy-start | bytes 196612
  72.6 4.7 %collective-permute-start.16 = (f32[2,8,1024]{2,1,0:T(8,128)S(1)}, f32[2,8,1024]{2,1,0:T(8,128)S(1)}, u32[]{:S(2)}, u32[]{:S(2)}) collective-permute-start(f32[2,8,1024]{2,1,0:T(8,128)S(1)} %pad_maximum_fusion.refs_0_), channel_id=1, source_target_pairs={{0,16},{16,0},{32,48},{48,32},{1,17},{17,1},{33,49},{49,33},{2,18}... | collective-permute-start | bytes 196616 | tf_op jit(solution)/shard_map/ppermute | solution.py:41
  74.2 5.9 %collective-permute-start.17 = (f32[2,8,1024]{2,1,0:T(8,128)S(1)}, f32[2,8,1024]{2,1,0:T(8,128)S(1)}, u32[]{:S(2)}, u32[]{:S(2)}) collective-permute-start(f32[2,8,1024]{2,1,0:T(8,128)S(1)} %pad_maximum_fusion.refs_0_), channel_id=1, source_target_pairs={{0,32},{16,48},{32,0},{48,16},{1,33},{17,49},{33,1},{49,17},{2,34}... | collective-permute-start | bytes 196616 | tf_op jit(solution)/shard_map/ppermute | solution.py:41
  77.1 5.6 %collective-permute-start.18 = (f32[2,8,1024]{2,1,0:T(8,128)S(1)}, f32[2,8,1024]{2,1,0:T(8,128)}, u32[]{:S(2)}, u32[]{:S(2)}) collective-permute-start(f32[2,8,1024]{2,1,0:T(8,128)S(1)} %pad_maximum_fusion.refs_0_), channel_id=1, source_target_pairs={{0,48},{16,32},{32,16},{48,0},{1,49},{17,33},{33,17},{49,1},{2,50}... | collective-permute-start | bytes 196616 | tf_op jit(solution)/shard_map/ppermute | solution.py:41
  85.3 4.7 %collective-permute-start.19 = (f32[72,128]{1,0:T(8,128)}, f32[72,128]{1,0:T(8,128)S(1)}, u32[]{:S(2)}, u32[]{:S(2)}) collective-permute-start(f32[72,128]{1,0:T(8,128)} %get-tuple-element.58), channel_id=1, source_target_pairs={{0,2},{2,0},{4,6},{6,4},{1,3},{3,1},{5,7},{7,5},{8,10},{10,8},{12,... | collective-permute-start | bytes 110600 | tf_op jit(solution)/shard_map/ppermute | solution.py:41
  85.3 5.7 %collective-permute-start.20 = (f32[72,128]{1,0:T(8,128)}, f32[72,128]{1,0:T(8,128)S(1)}, u32[]{:S(2)}, u32[]{:S(2)}) collective-permute-start(f32[72,128]{1,0:T(8,128)} %get-tuple-element.58), channel_id=1, source_target_pairs={{0,4},{2,6},{4,0},{6,2},{1,5},{3,7},{5,1},{7,3},{8,12},{10,14},{12... | collective-permute-start | bytes 110600 | tf_op jit(solution)/shard_map/ppermute | solution.py:41
  88.2 5.4 %collective-permute-start.21 = (f32[72,128]{1,0:T(8,128)}, f32[72,128]{1,0:T(8,128)S(1)}, u32[]{:S(2)}, u32[]{:S(2)}) collective-permute-start(f32[72,128]{1,0:T(8,128)} %get-tuple-element.58), channel_id=1, source_target_pairs={{0,6},{2,4},{4,2},{6,0},{1,7},{3,5},{5,3},{7,1},{8,14},{10,12},{12... | collective-permute-start | bytes 110600 | tf_op jit(solution)/shard_map/ppermute | solution.py:41
  94.4 5.4 %copy-start.1 = (f32[72,128]{1,0:T(8,128)}, f32[72,128]{1,0:T(8,128)S(1)}, u32[]{:S(2)}) copy-start(f32[72,128]{1,0:T(8,128)S(1)} %add_add_fusion.p0) | copy-start | bytes 110596
  94.4 2.0 collective-permute-start.22
  94.5 4.0 %collective-permute-start.23 = (f32[72,128]{1,0:T(8,128)S(1)}, f32[72,128]{1,0:T(8,128)S(1)}, u32[]{:S(2)}, u32[]{:S(2)}) collective-permute-start(f32[72,128]{1,0:T(8,128)S(1)} %add_add_fusion.p0), channel_id=1, source_target_pairs={{0,8},{8,0},{1,9},{9,1},{2,10},{10,2},{3,11},{11,3},{4,12},{12,4},... | collective-permute-start | bytes 110600 | tf_op jit(solution)/shard_map/ppermute | solution.py:41
  95.7 3.4 %collective-permute-start.24 = (f32[72,128]{1,0:T(8,128)S(1)}, f32[72,128]{1,0:T(8,128)S(1)}, u32[]{:S(2)}, u32[]{:S(2)}) collective-permute-start(f32[72,128]{1,0:T(8,128)S(1)} %add_add_fusion.p0), channel_id=1, source_target_pairs={{0,9},{1,8},{8,1},{9,0},{2,11},{3,10},{10,3},{11,2},{4,13},{5,12},... | collective-permute-start | bytes 110600 | tf_op jit(solution)/shard_map/ppermute | solution.py:744
  96.3 2.8 %copy-start.4 = (f32[72,128]{1,0:T(8,128)}, f32[72,128]{1,0:T(8,128)S(1)}, u32[]{:S(2)}) copy-start(f32[72,128]{1,0:T(8,128)S(1)} %collective-permute-done.22.p1) | copy-start | bytes 110596
  111.1 8.2 %collective-permute-start.25 = (bf16[1,2,2,528,256]{4,3,2,1,0:T(8,128)(2,1)}, bf16[1,2,2,528,256]{4,3,2,1,0:T(8,128)(2,1)}, u32[]{:S(2)}, u32[]{:S(2)}) collective-permute-start(bf16[1,2,2,528,256]{4,3,2,1,0:T(8,128)(2,1)} %term_part.4.refs_0_), channel_id=1, source_target_pairs={{0,1},{1,0},{2,3},{3,2},{4,5},{5,4},{6,7},{7,6},{8,9},{9,8},{10,11... | collective-permute-start | bytes 3244040 | tf_op jit(solution)/shard_map/ppermute | solution.py:41
  119.0 24.0 %collective-permute-start.26 = (bf16[3,2,2,528,256]{4,3,2,1,0:T(8,128)(2,1)}, bf16[3,2,2,528,256]{4,3,2,1,0:T(8,128)(2,1)}, u32[]{:S(2)}, u32[]{:S(2)}) collective-permute-start(bf16[3,2,2,528,256]{4,3,2,1,0:T(8,128)(2,1)} %term_part.5.refs_0_), channel_id=1, source_target_pairs={{0,1},{1,0},{2,3},{3,2},{4,5},{5,4},{6,7},{7,6},{8,9},{9,8},{10,11... | collective-permute-start | bytes 9732104 | tf_op jit(solution)/shard_map/ppermute | solution.py:41
  124.4 15.9 %collective-permute-start.27 = (bf16[2,528,256]{2,1,0:T(8,128)(2,1)}, bf16[2,528,256]{2,1,0:T(8,128)(2,1)}, u32[]{:S(2)}, u32[]{:S(2)}) collective-permute-start(bf16[2,528,256]{2,1,0:T(8,128)(2,1)} %get-tuple-element.64.refs_0_), channel_id=1, source_target_pairs={{0,2},{2,4},{4,6},{6,0},{1,3},{3,5},{5,7},{7,1},{8,10},{10,12},{12... | collective-permute-start | bytes 1622024 | tf_op jit(solution)/shard_map/ppermute | solution.py:37
  124.4 18.6 %collective-permute-start.28 = (bf16[2,528,256]{2,1,0:T(8,128)(2,1)}, bf16[2,528,256]{2,1,0:T(8,128)(2,1)}, u32[]{:S(2)}, u32[]{:S(2)}) collective-permute-start(bf16[2,528,256]{2,1,0:T(8,128)(2,1)} %get-tuple-element.68), channel_id=1, source_target_pairs={{0,6},{2,0},{4,2},{6,4},{1,7},{3,1},{5,3},{7,5},{8,14},{10,8},{12,... | collective-permute-start | bytes 1622024 | tf_op jit(solution)/shard_map/ppermute | solution.py:37
  134.1 22.8 %collective-permute-start.33 = (bf16[2,688,256]{2,1,0:T(8,128)(2,1)}, bf16[2,688,256]{2,1,0:T(8,128)(2,1)}, u32[]{:S(2)}, u32[]{:S(2)}) collective-permute-start(bf16[2,688,256]{2,1,0:T(8,128)(2,1)} %get-tuple-element.67.refs_0_), channel_id=1, source_target_pairs={{0,16},{16,32},{32,48},{48,0},{1,17},{17,33},{33,49},{49,1},{2,18}... | collective-permute-start | bytes 2113544 | tf_op jit(solution)/shard_map/ppermute | solution.py:37
  134.1 22.8 %collective-permute-start.34 = (bf16[2,688,256]{2,1,0:T(8,128)(2,1)}, bf16[2,688,256]{2,1,0:T(8,128)(2,1)}, u32[]{:S(2)}, u32[]{:S(2)}) collective-permute-start(bf16[2,688,256]{2,1,0:T(8,128)(2,1)} %get-tuple-element.77), channel_id=1, source_target_pairs={{0,48},{16,0},{32,16},{48,32},{1,49},{17,1},{33,17},{49,33},{2,50}... | collective-permute-start | bytes 2113544 | tf_op jit(solution)/shard_map/ppermute | solution.py:37
  140.2 16.6 %collective-permute-start.32 = (bf16[1,2,312,256]{3,2,1,0:T(8,128)(2,1)}, bf16[1,2,312,256]{3,2,1,0:T(8,128)(2,1)}, u32[]{:S(2)}, u32[]{:S(2)}) collective-permute-start(bf16[1,2,312,256]{3,2,1,0:T(8,128)(2,1)} %get-tuple-element.76), channel_id=1, source_target_pairs={{0,64},{64,0},{1,65},{65,1},{2,66},{66,2},{3,67},{67,3},{4,68},{68... | collective-permute-start | bytes 958472 | tf_op jit(solution)/shard_map/ppermute | solution.py:41
  153.7 26.3 %collective-permute-start.29 = (bf16[2,2,528,256]{3,2,1,0:T(8,128)(2,1)}, bf16[2,2,528,256]{3,2,1,0:T(8,128)(2,1)}, u32[]{:S(2)}, u32[]{:S(2)}) collective-permute-start(bf16[2,2,528,256]{3,2,1,0:T(8,128)(2,1)} %get-tuple-element.70), channel_id=1, source_target_pairs={{0,2},{2,4},{4,6},{6,0},{1,3},{3,5},{5,7},{7,1},{8,10},{10,12},{12... | collective-permute-start | bytes 3244040 | tf_op jit(solution)/shard_map/ppermute | solution.py:37
  153.7 26.3 %collective-permute-start.30 = (bf16[2,2,528,256]{3,2,1,0:T(8,128)(2,1)}, bf16[2,2,528,256]{3,2,1,0:T(8,128)(2,1)}, u32[]{:S(2)}, u32[]{:S(2)}) collective-permute-start(bf16[2,2,528,256]{3,2,1,0:T(8,128)(2,1)} %get-tuple-element.71), channel_id=1, source_target_pairs={{0,6},{2,0},{4,2},{6,4},{1,7},{3,1},{5,3},{7,5},{8,14},{10,8},{12,... | collective-permute-start | bytes 3244040 | tf_op jit(solution)/shard_map/ppermute | solution.py:37
  166.9 24.8 %collective-permute-start.39 = (bf16[2,2,312,256]{3,2,1,0:T(8,128)(2,1)}, bf16[2,2,312,256]{3,2,1,0:T(8,128)(2,1)}, u32[]{:S(2)}, u32[]{:S(2)}) collective-permute-start(bf16[2,2,312,256]{3,2,1,0:T(8,128)(2,1)} %get-tuple-element.85), channel_id=1, source_target_pairs={{0,64},{64,0},{1,65},{65,1},{2,66},{66,2},{3,67},{67,3},{4,68},{68... | collective-permute-start | bytes 1916936 | tf_op jit(solution)/shard_map/ppermute | solution.py:41
  167.7 38.8 %collective-permute-start.35 = (bf16[2,2,688,256]{3,2,1,0:T(8,128)(2,1)}, bf16[2,2,688,256]{3,2,1,0:T(8,128)(2,1)}, u32[]{:S(2)}, u32[]{:S(2)}) collective-permute-start(bf16[2,2,688,256]{3,2,1,0:T(8,128)(2,1)} %get-tuple-element.78.refs_0_), channel_id=1, source_target_pairs={{0,16},{16,32},{32,48},{48,0},{1,17},{17,33},{33,49},{49,1},{2,18}... | collective-permute-start | bytes 4227080 | tf_op jit(solution)/shard_map/ppermute | solution.py:37
  167.7 40.5 %collective-permute-start.36 = (bf16[2,2,688,256]{3,2,1,0:T(8,128)(2,1)}, bf16[2,2,688,256]{3,2,1,0:T(8,128)(2,1)}, u32[]{:S(2)}, u32[]{:S(2)}) collective-permute-start(bf16[2,2,688,256]{3,2,1,0:T(8,128)(2,1)} %get-tuple-element.80), channel_id=1, source_target_pairs={{0,48},{16,0},{32,16},{48,32},{1,49},{17,1},{33,17},{49,33},{2,50}... | collective-permute-start | bytes 4227080 | tf_op jit(solution)/shard_map/ppermute | solution.py:37
  190.0 12.3 %collective-permute-start.38 = (bf16[1,2,312,256]{3,2,1,0:T(8,128)(2,1)}, bf16[1,2,312,256]{3,2,1,0:T(8,128)(2,1)}, u32[]{:S(2)}, u32[]{:S(2)}) collective-permute-start(bf16[1,2,312,256]{3,2,1,0:T(8,128)(2,1)} %get-tuple-element.82), channel_id=1, source_target_pairs={{0,64},{64,0},{1,65},{65,1},{2,66},{66,2},{3,67},{67,3},{4,68},{68... | collective-permute-start | bytes 958472 | tf_op jit(solution)/shard_map/ppermute | solution.py:41
  190.8 20.8 %collective-permute-start.31 = (bf16[2,528,256]{2,1,0:T(8,128)(2,1)}, bf16[2,528,256]{2,1,0:T(8,128)(2,1)}, u32[]{:S(2)}, u32[]{:S(2)}) collective-permute-start(bf16[2,528,256]{2,1,0:T(8,128)(2,1)} %get-tuple-element.73), channel_id=1, source_target_pairs={{0,8},{8,0},{1,9},{9,1},{2,10},{10,2},{3,11},{11,3},{4,12},{12,4},... | collective-permute-start | bytes 1622024 | tf_op jit(solution)/shard_map/ppermute | solution.py:41
  204.8 12.8 %collective-permute-start.40 = (bf16[2,328,256]{2,1,0:T(8,128)(2,1)}, bf16[2,328,256]{2,1,0:T(8,128)(2,1)}, u32[]{:S(2)}, u32[]{:S(2)}) collective-permute-start(bf16[2,328,256]{2,1,0:T(8,128)(2,1)} %get-tuple-element.87), channel_id=1, source_target_pairs={{0,16},{16,32},{32,48},{48,0},{1,17},{17,33},{33,49},{49,1},{2,18}... | collective-permute-start | bytes 1007624 | tf_op jit(solution)/shard_map/ppermute | solution.py:37
  204.8 12.8 %collective-permute-start.41 = (bf16[2,328,256]{2,1,0:T(8,128)(2,1)}, bf16[2,328,256]{2,1,0:T(8,128)(2,1)}, u32[]{:S(2)}, u32[]{:S(2)}) collective-permute-start(bf16[2,328,256]{2,1,0:T(8,128)(2,1)} %get-tuple-element.88), channel_id=1, source_target_pairs={{0,32},{16,48},{32,0},{48,16},{1,33},{17,49},{33,1},{49,17},{2,34}... | collective-permute-start | bytes 1007624 | tf_op jit(solution)/shard_map/ppermute | solution.py:37
  206.5 11.7 %collective-permute-start.42 = (bf16[2,328,256]{2,1,0:T(8,128)(2,1)}, bf16[2,328,256]{2,1,0:T(8,128)(2,1)}, u32[]{:S(2)}, u32[]{:S(2)}) collective-permute-start(bf16[2,328,256]{2,1,0:T(8,128)(2,1)} %get-tuple-element.89), channel_id=1, source_target_pairs={{0,48},{16,0},{32,16},{48,32},{1,49},{17,1},{33,17},{49,33},{2,50}... | collective-permute-start | bytes 1007624 | tf_op jit(solution)/shard_map/ppermute | solution.py:37
  210.7 20.2 %collective-permute-start.37 = (bf16[2,688,256]{2,1,0:T(8,128)(2,1)}, bf16[2,688,256]{2,1,0:T(8,128)(2,1)}, u32[]{:S(2)}, u32[]{:S(2)}) collective-permute-start(bf16[2,688,256]{2,1,0:T(8,128)(2,1)} %fusion), channel_id=1, source_target_pairs={{0,64},{64,0},{1,65},{65,1},{2,66},{66,2},{3,67},{67,3},{4,68},{68... | collective-permute-start | bytes 2113544 | tf_op jit(solution)/shard_map/ppermute | solution.py:41
  219.6 6.5 %collective-permute-start.43 = (f32[8,256]{1,0:T(8,128)}, f32[8,256]{1,0:T(8,128)S(1)}, u32[]{:S(2)}, u32[]{:S(2)}) collective-permute-start(f32[8,256]{1,0:T(8,128)} %gain_along_y.1), channel_id=1, source_target_pairs={{0,64},{64,0},{1,65},{65,1},{2,66},{66,2},{3,67},{67,3},{4,68},{68... | collective-permute-start | bytes 24584 | tf_op jit(solution)/shard_map/ppermute | solution.py:41
  226.8 3.6 %collective-permute-start.44 = (f32[256]{0:T(256)S(1)}, f32[256]{0:T(256)S(1)}, u32[]{:S(2)}, u32[]{:S(2)}) collective-permute-start(f32[256]{0:T(256)S(1)} %bitcast.39), channel_id=1, source_target_pairs={{0,8},{8,0},{1,9},{9,1},{2,10},{10,2},{3,11},{11,3},{4,12},{12,4},... | collective-permute-start | bytes 3080 | tf_op jit(solution)/shard_map/ppermute | solution.py:41
  (4 other events, 4.7 us)

commit v3 on v2

--- a/solution.py
+++ b/solution.py
@@ -502,23 +502,23 @@
     return jnp.concatenate(rows + [jnp.zeros((12, BLK), f32)], axis=0).astype(bf16)
 
 
-def low_sum_kernel(_, gain, a13, b13, a2, b2, out_1, out_3, out_2):
+def low_sum_kernel(_, __, gain, a13, b13, a2, b2, out_1, out_3, out_2):
     for a, b, i, out in ((a13, b13, 0, out_1), (a13, b13, 1, out_3), (a2, b2, 0, out_2)):
         out[0, 0:16, :] = gain_rows(gain)
         out[1, 0:16, :] = jnp.zeros((16, BLK), bf16)
         out[:, 16:, :] = (a[i].astype(f32) + b[i].astype(f32)).astype(bf16)
 
 
-def low_sum(after, *parts):
+def low_sum(after, also, *parts):
     return pl.pallas_call(
         low_sum_kernel,
         out_shape=[jax.ShapeDtypeStruct((2, 16 + ROWS_B, BLK), bf16)] * 3,
-        in_specs=[ANY] + [VMEM] * 5,
+        in_specs=[ANY] * 2 + [VMEM] * 5,
         out_specs=[VMEM] * 3,
         compiler_params=params(),
         cost_estimate=cost(1000, 4_000_000),
         name="low_sum",
-    )(after, *parts)
+    )(after, also, *parts)
 
 
 def gain_kernel(ids, gain, l1, l2, l3, out, held):
@@ -711,6 +711,22 @@
     )(ids, *after, n, got, x, gain, inv, dots)
 
 
+def gain_sum_kernel(_, here, there, other, both, out):
+    out[...] = (here[0:1, :] + there[0:1, :]) + (other[1:2, :] + both[1:2, :])
+
+
+def gain_sum(after, parts):
+    return pl.pallas_call(
+        gain_sum_kernel,
+        out_shape=jax.ShapeDtypeStruct((1, BLK), f32),
+        in_specs=[ANY] + [VMEM] * 4,
+        out_specs=VMEM,
+        compiler_params=params(),
+        cost_estimate=cost(1000, 5000),
+        name="gain_sum",
+    )(after, *parts)
+
+
 def shards(hidden, norm_gain, head_weight, lengths, positives, negatives):
     xh, y, xl, z, c = (lax.axis_index(a).astype(jnp.int32) for a in ("xh", "y", "xl", "z", "c"))
     nil = jnp.int32(0)
@@ -762,15 +778,17 @@
     keep, send, dots, partial = term_sum((), t_0, shift(t_1, "z", 1), shift(t_3, "z", -1), hidden, x_p)
     a_0, keep_0, send_0 = head_part(ids, (0,), ht, x, gain, (a_1, keep), weight=20)
     swap_0 = swap(send_0, "xh")
-    got = swap(a_0[1] + ra[1] + rb[1], "xh")
-    low_1, low_3, low_2 = low_sum(swap_0, partial, keep_13, swap_13, keep_2, swap_2)
+    mine = a_0[1] + ra[1] + rb[1]
+    got = swap(mine, "xh")
+    low_1, low_3, low_2 = low_sum(mine, swap_0, partial, keep_13, swap_13, keep_2, swap_2)
     low = [shift(low_1, "y", 1), shift(low_2, "y", 2), shift(low_3, "y", 3)]
     hidden_grad = final(ids, (), keep, swap(send, "xl"), hidden, gain, inv, dots)
     gain_grad = gain_along_y(ids, (hidden_grad, swap_0), partial, *low)
-    gain_grad = gain_grad + swap(gain_grad, "xh")
-    gain_grad = gain_grad[0] + swap(gain_grad[1], "xl")
+    both = lax.ppermute(gain_grad, ("xh", "xl"), [(i, i ^ 3) for i in range(4)])
+    parts = (gain_grad, swap(gain_grad, "xh"), swap(gain_grad, "xl"), both)
     head_t = join(ids, hidden_grad, a_0, ra, rb, got, keep_0, swap_0, *low)
-    return losses[0, :3], hidden_grad, head_t.T, gain_grad
+    gain_grad = gain_sum(head_t, parts)
+    return losses[0, :3], hidden_grad, head_t.T, gain_grad[0]
 
 
 def solution(mesh):

time: 236 us -> 237 us (level)
  waiting for transfers between devices: 62.7 us -> 57.9 us
  starting transfers between devices: 51.8 us -> 55.8 us
    ppermute x29, waiting for transfers between devices: 35.5 us -> 19.4 us  [swap(): return lax.ppermute(x, axis, [(i, i ^ bits) for i in range(SIZES[axis])])]
    ppermute x15, waiting for transfers between devices: 26.6 us -> 37.7 us  [shift(): return lax.ppermute(x, axis, [(i, (i + step) % n) for i in range(n)])]
  transfers between devices with their start and end apart: 45 -> 46, of which waited for: 19 -> 18; matrix products, arithmetic and copies ran while one was open for 3% -> 2% of each run, Pallas kernels for 34% -> 36%
where the time goes in v3:
time: 237 us; the launch traced here: 236 us
  Pallas kernels  112 us (47%)
  waiting for transfers between devices  57.9 us (24%)
  starting transfers between devices  55.8 us (24%)
  local copies, waits for them, and re-layouts  5.61 us (2%)
  other arithmetic  4.03 us (2%)
    ppermute x15, waiting for transfers between devices, shift(): return lax.ppermute(x, axis, [(i, (i + step) % n) for i in range(n)])  37.7 us
    ppermute x29, starting transfers between devices, swap(): return lax.ppermute(x, axis, [(i, i ^ bits) for i in range(SIZES[axis])])  29.4 us
    pallas_call x4, Pallas kernels, term_part(): pl.pallas_call(later(len(after), functools.partial(term_kernel, count, sp...  28.3 us
    ppermute x15, starting transfers between devices, shift(): return lax.ppermute(x, axis, [(i, (i + step) % n) for i in range(n)])  24.9 us
    pallas_call x2, Pallas kernels, forward(): pl.pallas_call(functools.partial(forward_kernel, places, not state), out_...  23.1 us
    pallas_call x3, Pallas kernels, head_part(): pl.pallas_call(later(len(after), functools.partial(head_kernel, steps, sp...  23 us
    ppermute x29, waiting for transfers between devices, swap(): return lax.ppermute(x, axis, [(i, i ^ bits) for i in range(SIZES[axis])])  19.4 us
    pallas_call x1, Pallas kernels, forward_last(): pl.pallas_call(functools.partial(forward_last_kernel, place), out_shape=[...  12.2 us
  transfers between devices with their start and end apart: 46, of which 18 were waited for; matrix products, arithmetic and copies ran while one was open for 2% of the time, Pallas kernels for 36%

profile of v3, /device:TPU:0, one launch (start us, length us, event | category | flops | bytes accessed | tf_op | source)
XLA Modules:
  0.0 236.0 jit_solution(1730073218171262168)
XLA Ops:
  0.6 2.1 collective-permute-start.3
  2.7 1.5 collective-permute-start.5
  4.2 2.2 collective-permute-start
  6.4 10.7 %collective-permute-done.3.refs_2_ = bf16[1024,256]{1,0:T(8,128)(2,1)} collective-permute-done((bf16[1024,256]{1,0:T(8,128)(2,1)}, bf16[1024,256]{1,0:T(8,128)(2,1)}, u32[]{:S(2)}, u32[]{:S(2)}) %collective-permute-start.3) | collective-permute-done | bytes 524320 | tf_op jit(solution)/shard_map/ppermute | solution.py:37
  18.3 2.5 %collective-permute-start.8 = (bf16[1024,256]{1,0:T(8,128)(2,1)}, bf16[1024,256]{1,0:T(8,128)(2,1)}, u32[]{:S(2)}, u32[]{:S(2)}) collective-permute-start(bf16[1024,256]{1,0:T(8,128)(2,1)} %collective-permute-done.5.refs_4_), channel_id=1, source_target_pairs={{0,6},{2,0},{4,2},{6,4},{1,7},{3,1},{5,3},{7,5},{8,14},{10,8},{12,... | collective-permute-start | bytes 1572872 | tf_op jit(solution)/shard_map/ppermute | solution.py:37
  20.8 1.5 collective-permute-start.9
  24.3 10.1 %forward_part.2 = (f32[1024,1000]{1,0:T(8,128)}, f32[1024,128]{1,0:T(8,128)}, bf16[8,2,1024,256]{3,2,1,0:T(8,128)(2,1)}) custom-call(s32[14]{0:T(128)} %concatenate.3.ids, bf16[1024,256]{1,0:T(8,128)(2,1)} %refs_2_.1, bf16[1024,256]{1,0:T(8,128)(2,1)} %collective-permute-done.2.refs_1_, bf16[1024,256]{1,0:T(8,128)(2,1)} %collective-permute-done.3.refs_2_, ...), custom_call_target="tpu_custom_call" | custom-call | flops 62914560 | bytes 340000 | tf_op jit(solution)/shard_map/forward_part/pallas_call | solution.py:168
  38.4 13.1 %forward_part.3 = (f32[1024,1000]{1,0:T(8,128)}, f32[1024,128]{1,0:T(8,128)}, bf16[8,2,1024,256]{3,2,1,0:T(8,128)(2,1)}) custom-call(s32[14]{0:T(128)} %concatenate.3.ids, bf16[1024,256]{1,0:T(8,128)(2,1)} %collective-permute-done.refs_0_, ...), custom_call_target="tpu_custom_call", output_to_operand_aliasing={{0}: (11, {}), {1}: (12, {}), {2}: (13, {})} | custom-call | flops 83886080 | bytes 400000 | tf_op jit(solution)/shard_map/forward_part/pallas_call | solution.py:168
  51.9 1.9 collective-permute-done.14.a1
  53.8 12.2 %forward_last.1 = (bf16[1024,1000]{1,0:T(8,128)(2,1)}, bf16[8,2,1024,256]{3,2,1,0:T(8,128)(2,1)}, f32[1024,1]{1,0:T(8,128)}, bf16[1024,1000]{1,0:T(8,128)(2,1)}, f32[8,1024]{1,0:T(8,128)}) custom-call(s32[14]{0:T(128)} %concatenate.3.ids, s32[8]{0:T(128)} %lengths.1, bf16[1024,256]{1,0:T(8,128)(2,1)} %touch.3.a0, ...), custom_call_target="tpu_custom_call", output_to_operand_aliasing={{1}: (9, {})} | custom-call | flops 20971520 | bytes 400000 | tf_op jit(solution)/shard_map/forward_last/pallas_call | solution.py:221
  66.0 2.9 %collective-permute-start.15 = (f32[8,1024]{1,0:T(8,128)}, f32[8,1024]{1,0:T(8,128)S(1)}, u32[]{:S(2)}, u32[]{:S(2)}) collective-permute-start(f32[8,1024]{1,0:T(8,128)} %get-tuple-element.56), channel_id=1, source_target_pairs={{0,64},{64,0},{1,65},{65,1},{2,66},{66,2},{3,67},{67,3},{4,68},{68... | collective-permute-start | bytes 98312 | tf_op jit(solution)/shard_map/ppermute | solution.py:41
  68.9 2.8 %collective-permute-done.15 = f32[8,1024]{1,0:T(8,128)S(1)} collective-permute-done((f32[8,1024]{1,0:T(8,128)}, f32[8,1024]{1,0:T(8,128)S(1)}, u32[]{:S(2)}, u32[]{:S(2)}) %collective-permute-start.15) | collective-permute-done | bytes 32800 | tf_op jit(solution)/shard_map/ppermute | solution.py:41
  72.5 1.6 collective-permute-start.16
  74.1 2.9 %collective-permute-start.17 = (f32[2,8,1024]{2,1,0:T(8,128)S(1)}, f32[2,8,1024]{2,1,0:T(8,128)S(1)}, u32[]{:S(2)}, u32[]{:S(2)}) collective-permute-start(f32[2,8,1024]{2,1,0:T(8,128)S(1)} %pad_maximum_fusion.refs_0_), channel_id=1, source_target_pairs={{0,32},{16,48},{32,0},{48,16},{1,33},{17,49},{33,1},{49,17},{2,34}... | collective-permute-start | bytes 196616 | tf_op jit(solution)/shard_map/ppermute | solution.py:41
  77.2 2.8 %collective-permute-done.17.refs_2_ = f32[2,8,1024]{2,1,0:T(8,128)S(1)} collective-permute-done((f32[2,8,1024]{2,1,0:T(8,128)S(1)}, f32[2,8,1024]{2,1,0:T(8,128)S(1)}, u32[]{:S(2)}, u32[]{:S(2)}) %collective-permute-start.17) | collective-permute-done | bytes 65568 | tf_op jit(solution)/shard_map/ppermute | solution.py:41
  80.6 2.0 collective-permute-done.18.refs_3_
  82.6 2.6 %gram.1 = (f32[64,1024]{1,0:T(8,128)}, f32[72,128]{1,0:T(8,128)}) custom-call(s32[14]{0:T(128)} %concatenate.3.ids, f32[2,8,1024]{2,1,0:T(8,128)} %copy-done, f32[2,8,1024]{2,1,0:T(8,128)} %copy-done.2, f32[2,8,1024]{2,1,0:T(8,128)} %copy-done.3, f32[2,8,1024]{2,1,0:T(8,128)} %collective-permute-done.18.refs_3_), custom_call_target="tpu_custom_call" | custom-call | tf_op jit(solution)/shard_map/gram/pallas_call | solution.py:291
  85.2 2.9 %collective-permute-start.20 = (f32[72,128]{1,0:T(8,128)}, f32[72,128]{1,0:T(8,128)S(1)}, u32[]{:S(2)}, u32[]{:S(2)}) collective-permute-start(f32[72,128]{1,0:T(8,128)} %get-tuple-element.58), channel_id=1, source_target_pairs={{0,4},{2,6},{4,0},{6,2},{1,5},{3,7},{5,1},{7,3},{8,12},{10,14},{12... | collective-permute-start | bytes 110600 | tf_op jit(solution)/shard_map/ppermute | solution.py:41
  88.1 1.8 collective-permute-start.21
  90.9 2.6 %collective-permute-done.21 = f32[72,128]{1,0:T(8,128)S(1)} collective-permute-done((f32[72,128]{1,0:T(8,128)}, f32[72,128]{1,0:T(8,128)S(1)}, u32[]{:S(2)}, u32[]{:S(2)}) %collective-permute-start.21) | collective-permute-done | bytes 36896 | tf_op jit(solution)/shard_map/ppermute | solution.py:41
  96.3 2.2 collective-permute-done.23.p2
  99.8 6.6 %logit_grad.1 = (bf16[1024,1000]{1,0:T(8,128)(2,1)}, bf16[1000,1024]{1,0:T(8,128)(2,1)}, f32[16,256]{1,0:T(8,128)}, f32[8,128]{1,0:T(8,128)}) custom-call(s32[14]{0:T(128)} %concatenate.3.ids, f32[64,1024]{1,0:T(8,128)} %get-tuple-element.57.every, f32[72,128]{1,0:T(8,128)} %copy-done.1, f32[72,128]{1,0:T(8,128)} %copy-done.4, f32[72,128]{1,0:T(8,128)} %copy-done.5, ...), custom_call_target="tpu_custom_call" | custom-call | flops 409600 | bytes 240000 | tf_op jit(solution)/shard_map/logit_grad/pallas_call | solution.py:388
  106.3 4.8 %term_part.4.refs_0_ = bf16[1,2,2,528,256]{4,3,2,1,0:T(8,128)(2,1)} custom-call(s32[14]{0:T(128)} %concatenate.3.ids, bf16[1024,1000]{1,0:T(8,128)(2,1)} %get-tuple-element.62.refs_0_.refs_1_, bf16[1000,4096]{1,0:T(8,128)(2,1)} %bitcast.19, bf16[1000,4096]{1,0:T(8,128)(2,1)} %bitcast.20, f32[16,256]{1,0:T(8,128)} %get-tuple-element.63.refs_3_.refs_4_), custom_call_target="tpu_custom_call" | custom-call | flops 20971520 | bytes 103383 | tf_op jit(solution)/shard_map/term_part/pallas_call | solution.py:625
  111.3 7.8 %term_part.5.refs_0_ = bf16[3,2,2,528,256]{4,3,2,1,0:T(8,128)(2,1)} custom-call(s32[14]{0:T(128)} %concatenate.3.ids, bf16[1,2,2,528,256]{4,3,2,1,0:T(8,128)(2,1)} %term_part.4.refs_0_, bf16[1024,1000]{1,0:T(8,128)(2,1)} %get-tuple-element.62.refs_0_.refs_1_, bf16[1000,4096]{1,0:T(8,128)(2,1)} %bitcast.21, bf16[1000,4096]{1,0:T(8,128)(2,1)} %bitcast.22, ...), custom_call_target="tpu_custom_call" | custom-call | flops 62914560000 | bytes 228229120 | tf_op jit(solution)/shard_map/term_part/pallas_call | solution.py:625
  119.4 5.1 %term_part.6 = (bf16[2,528,256]{2,1,0:T(8,128)(2,1)}, bf16[2,528,256]{2,1,0:T(8,128)(2,1)}) custom-call(s32[14]{0:T(128)} %concatenate.3.ids, bf16[3,2,2,528,256]{4,3,2,1,0:T(8,128)(2,1)} %term_part.5.refs_0_, bf16[1024,1000]{1,0:T(8,128)(2,1)} %get-tuple-element.62.refs_0_.refs_1_, bf16[1000,4096]{1,0:T(8,128)(2,1)} %bitcast.23, ...), custom_call_target="tpu_custom_call" | custom-call | flops 20971520 | bytes 103383 | tf_op jit(solution)/shard_map/term_part/pallas_call | solution.py:625
  124.5 3.2 %collective-permute-start.28 = (bf16[2,528,256]{2,1,0:T(8,128)(2,1)}, bf16[2,528,256]{2,1,0:T(8,128)(2,1)}, u32[]{:S(2)}, u32[]{:S(2)}) collective-permute-start(bf16[2,528,256]{2,1,0:T(8,128)(2,1)} %get-tuple-element.68), channel_id=1, source_target_pairs={{0,6},{2,0},{4,2},{6,4},{1,7},{3,1},{5,3},{7,5},{8,14},{10,8},{12,... | collective-permute-start | bytes 1622024 | tf_op jit(solution)/shard_map/ppermute | solution.py:37
  127.7 6.4 %head_part.3 = (bf16[2,688,256]{2,1,0:T(8,128)(2,1)}, bf16[2,688,256]{2,1,0:T(8,128)(2,1)}, bf16[1,2,312,256]{3,2,1,0:T(8,128)(2,1)}, bf16[1,2,312,256]{3,2,1,0:T(8,128)(2,1)}) custom-call(s32[14]{0:T(128)} %concatenate.3.ids, bf16[2,528,256]{2,1,0:T(8,128)(2,1)} %get-tuple-element.64.refs_0_, bf16[1000,1024]{1,0:T(8,128)(2,1)} %get-tuple-element.65.refs_1_.refs_2_, ...), custom_call_target="tpu_custom_call" | custom-call | flops 41943040000 | bytes 123863040 | tf_op jit(solution)/shard_map/head_part/pallas_call | solution.py:475
  134.2 3.2 %collective-permute-start.34 = (bf16[2,688,256]{2,1,0:T(8,128)(2,1)}, bf16[2,688,256]{2,1,0:T(8,128)(2,1)}, u32[]{:S(2)}, u32[]{:S(2)}) collective-permute-start(bf16[2,688,256]{2,1,0:T(8,128)(2,1)} %get-tuple-element.77), channel_id=1, source_target_pairs={{0,48},{16,0},{32,16},{48,32},{1,49},{17,1},{33,17},{49,33},{2,50}... | collective-permute-start | bytes 2113544 | tf_op jit(solution)/shard_map/ppermute | solution.py:37
  137.4 3.0 %collective-permute-done.27.refs_6_ = bf16[2,528,256]{2,1,0:T(8,128)(2,1)} collective-permute-done((bf16[2,528,256]{2,1,0:T(8,128)(2,1)}, bf16[2,528,256]{2,1,0:T(8,128)(2,1)}, u32[]{:S(2)}, u32[]{:S(2)}) %collective-permute-start.27) | collective-permute-done | bytes 540704 | tf_op jit(solution)/shard_map/ppermute | solution.py:37
  140.4 2.7 %collective-permute-start.32 = (bf16[1,2,312,256]{3,2,1,0:T(8,128)(2,1)}, bf16[1,2,312,256]{3,2,1,0:T(8,128)(2,1)}, u32[]{:S(2)}, u32[]{:S(2)}) collective-permute-start(bf16[1,2,312,256]{3,2,1,0:T(8,128)(2,1)} %get-tuple-element.76), channel_id=1, source_target_pairs={{0,64},{64,0},{1,65},{65,1},{2,66},{66,2},{3,67},{67,3},{4,68},{68... | collective-permute-start | bytes 958472 | tf_op jit(solution)/shard_map/ppermute | solution.py:41
  143.1 10.6 %term_part.7 = (bf16[2,2,528,256]{3,2,1,0:T(8,128)(2,1)}, bf16[2,2,528,256]{3,2,1,0:T(8,128)(2,1)}, bf16[2,2,528,256]{3,2,1,0:T(8,128)(2,1)}) custom-call(s32[14]{0:T(128)} %concatenate.3.ids, bf16[2,688,256]{2,1,0:T(8,128)(2,1)} %get-tuple-element.67.refs_0_, bf16[1024,1000]{1,0:T(8,128)(2,1)} %get-tuple-element.62.refs_0_.refs_1_, ...), custom_call_target="tpu_custom_call" | custom-call | flops 62914560000 | bytes 228229120 | tf_op jit(solution)/shard_map/term_part/pallas_call | solution.py:625
  153.7 3.2 %collective-permute-start.30 = (bf16[2,2,528,256]{3,2,1,0:T(8,128)(2,1)}, bf16[2,2,528,256]{3,2,1,0:T(8,128)(2,1)}, u32[]{:S(2)}, u32[]{:S(2)}) collective-permute-start(bf16[2,2,528,256]{3,2,1,0:T(8,128)(2,1)} %get-tuple-element.71), channel_id=1, source_target_pairs={{0,6},{2,0},{4,2},{6,4},{1,7},{3,1},{5,3},{7,5},{8,14},{10,8},{12,... | collective-permute-start | bytes 3244040 | tf_op jit(solution)/shard_map/ppermute | solution.py:37
  157.0 10.1 %head_part.4 = (bf16[2,2,688,256]{3,2,1,0:T(8,128)(2,1)}, bf16[2,2,688,256]{3,2,1,0:T(8,128)(2,1)}, bf16[2,2,312,256]{3,2,1,0:T(8,128)(2,1)}, bf16[2,2,312,256]{3,2,1,0:T(8,128)(2,1)}) custom-call(s32[14]{0:T(128)} %concatenate.3.ids, bf16[2,2,528,256]{3,2,1,0:T(8,128)(2,1)} %get-tuple-element.69.refs_0_, ...), custom_call_target="tpu_custom_call" | custom-call | flops 83886080000 | bytes 206766080 | tf_op jit(solution)/shard_map/head_part/pallas_call | solution.py:475
  167.1 3.2 %collective-permute-start.36 = (bf16[2,2,688,256]{3,2,1,0:T(8,128)(2,1)}, bf16[2,2,688,256]{3,2,1,0:T(8,128)(2,1)}, u32[]{:S(2)}, u32[]{:S(2)}) collective-permute-start(bf16[2,2,688,256]{3,2,1,0:T(8,128)(2,1)} %get-tuple-element.80), channel_id=1, source_target_pairs={{0,48},{16,0},{32,16},{48,32},{1,49},{17,1},{33,17},{49,33},{2,50}... | collective-permute-start | bytes 4227080 | tf_op jit(solution)/shard_map/ppermute | solution.py:37
  171.1 8.9 %collective-permute-done.29.refs_1_ = bf16[2,2,528,256]{3,2,1,0:T(8,128)(2,1)} collective-permute-done((bf16[2,2,528,256]{3,2,1,0:T(8,128)(2,1)}, bf16[2,2,528,256]{3,2,1,0:T(8,128)(2,1)}, u32[]{:S(2)}, u32[]{:S(2)}) %collective-permute-start.29) | collective-permute-done | bytes 1081376 | tf_op jit(solution)/shard_map/ppermute | solution.py:37
  180.0 3.6 %term_sum.1 = (bf16[1024,256]{1,0:T(8,128)(2,1)}, bf16[2,528,256]{2,1,0:T(8,128)(2,1)}, f32[16,256]{1,0:T(8,128)}, f32[2,256]{1,0:T(2,128)}) custom-call(bf16[2,2,528,256]{3,2,1,0:T(8,128)(2,1)} %get-tuple-element.69.refs_0_, bf16[2,2,528,256]{3,2,1,0:T(8,128)(2,1)} %collective-permute-done.29.refs_1_, ...), custom_call_target="tpu_custom_call" | custom-call | flops 20000 | bytes 100000 | tf_op jit(solution)/shard_map/term_sum/pallas_call | solution.py:671
  183.6 6.5 %head_part.5 = (bf16[2,2,688,256]{3,2,1,0:T(8,128)(2,1)}, bf16[1,2,312,256]{3,2,1,0:T(8,128)(2,1)}, bf16[1,2,312,256]{3,2,1,0:T(8,128)(2,1)}) custom-call(s32[14]{0:T(128)} %concatenate.3.ids, bf16[2,2,688,256]{3,2,1,0:T(8,128)(2,1)} %get-tuple-element.78.refs_0_, bf16[1024,256]{1,0:T(8,128)(2,1)} %get-tuple-element.72.refs_0_.refs_1_, ...), custom_call_target="tpu_custom_call" | custom-call | flops 41943040000 | bytes 123863040 | tf_op jit(solution)/shard_map/head_part/pallas_call | solution.py:475
  192.0 7.9 %collective-permute-done.35.ra = bf16[2,2,688,256]{3,2,1,0:T(8,128)(2,1)} collective-permute-done((bf16[2,2,688,256]{3,2,1,0:T(8,128)(2,1)}, bf16[2,2,688,256]{3,2,1,0:T(8,128)(2,1)}, u32[]{:S(2)}, u32[]{:S(2)}) %collective-permute-start.35) | collective-permute-done | bytes 1409056 | tf_op jit(solution)/shard_map/ppermute | solution.py:37
  199.9 2.5 %fusion._ = bf16[2,688,256]{2,1,0:T(8,128)(2,1)} fusion(bf16[2,2,688,256]{3,2,1,0:T(8,128)(2,1)} %collective-permute-done.36.rb, bf16[2,2,688,256]{3,2,1,0:T(8,128)(2,1)} %collective-permute-done.35.ra, bf16[2,2,688,256]{3,2,1,0:T(8,128)(2,1)} %get-tuple-element.79.a0), kind=kLoop, calls=%fused_computation.1 | loop fusion | flops 704512 | bytes 2818048 | tf_op jit(solution)/shard_map/add | solution.py:781
  203.2 2.5 %low_sum.1 = (bf16[2,328,256]{2,1,0:T(8,128)(2,1)}, bf16[2,328,256]{2,1,0:T(8,128)(2,1)}, bf16[2,328,256]{2,1,0:T(8,128)(2,1)}) custom-call(bf16[2,688,256]{2,1,0:T(8,128)(2,1)} %fusion._, bf16[1,2,312,256]{3,2,1,0:T(8,128)(2,1)} %collective-permute-done.38.__.swapped.refs_1_, f32[2,256]{1,0:T(2,128)} %get-tuple-element.83.gain.refs_2_, ...), custom_call_target="tpu_custom_call" | custom-call | flops 20 | bytes 80000 | tf_op jit(solution)/shard_map/low_sum/pallas_call | solution.py:513
  205.7 4.4 %collective-permute-start.41 = (bf16[2,328,256]{2,1,0:T(8,128)(2,1)}, bf16[2,328,256]{2,1,0:T(8,128)(2,1)}, u32[]{:S(2)}, u32[]{:S(2)}) collective-permute-start(bf16[2,328,256]{2,1,0:T(8,128)(2,1)} %get-tuple-element.88), channel_id=1, source_target_pairs={{0,32},{16,48},{32,0},{48,16},{1,33},{17,49},{33,1},{49,17},{2,34}... | collective-permute-start | bytes 1007624 | tf_op jit(solution)/shard_map/ppermute | solution.py:37
  210.1 2.2 collective-permute-done.31.refs_1_
  212.3 2.8 %hidden_grad.1._.refs_0_ = bf16[1024,256]{1,0:T(8,128)(2,1)} custom-call(s32[14]{0:T(128)} %concatenate.3.ids, bf16[1024,256]{1,0:T(8,128)(2,1)} %get-tuple-element.72.refs_0_.refs_1_, bf16[2,528,256]{2,1,0:T(8,128)(2,1)} %collective-permute-done.31.refs_1_, bf16[1024,256]{1,0:T(8,128)(2,1)} %refs_2_.1, f32[1,4096]{1,0:T(1,128)} %bitcast.34, ...), custom_call_target="tpu_custom_call" | custom-call | flops 20000 | bytes 40000 | tf_op jit(solution)/shard_map/hidden_grad/pallas_call | solution.py:703
  215.1 2.5 %collective-permute-done.40.b1.refs_3_ = bf16[2,328,256]{2,1,0:T(8,128)(2,1)} collective-permute-done((bf16[2,328,256]{2,1,0:T(8,128)(2,1)}, bf16[2,328,256]{2,1,0:T(8,128)(2,1)}, u32[]{:S(2)}, u32[]{:S(2)}) %collective-permute-start.40) | collective-permute-done | bytes 335904 | tf_op jit(solution)/shard_map/ppermute | solution.py:37
  217.6 4.8 %collective-permute-done.41.b2.refs_4_ = bf16[2,328,256]{2,1,0:T(8,128)(2,1)} collective-permute-done((bf16[2,328,256]{2,1,0:T(8,128)(2,1)}, bf16[2,328,256]{2,1,0:T(8,128)(2,1)}, u32[]{:S(2)}, u32[]{:S(2)}) %collective-permute-start.41) | collective-permute-done | bytes 335904 | tf_op jit(solution)/shard_map/ppermute | solution.py:37
  222.4 1.4 gain_along_y.1.here
  223.8 2.7 %collective-permute-start.43 = (f32[8,256]{1,0:T(8,128)}, f32[8,256]{1,0:T(8,128)S(1)}, u32[]{:S(2)}, u32[]{:S(2)}) collective-permute-start(f32[8,256]{1,0:T(8,128)} %gain_along_y.1.here), channel_id=1, source_target_pairs={{0,64},{64,0},{1,65},{65,1},{2,66},{66,2},{3,67},{67,3},{4,68},{68... | collective-permute-start | bytes 24584 | tf_op jit(solution)/shard_map/ppermute | solution.py:41
  229.1 4.3 %join.1._ = bf16[1000,512]{1,0:T(8,128)(2,1)} custom-call(s32[14]{0:T(128)} %concatenate.3.ids, bf16[1024,256]{1,0:T(8,128)(2,1)} %hidden_grad.1._.refs_0_, bf16[2,2,688,256]{3,2,1,0:T(8,128)(2,1)} %get-tuple-element.79.a0, bf16[2,2,688,256]{3,2,1,0:T(8,128)(2,1)} %collective-permute-done.35.ra, bf16[2,2,688,256]{3,2,1,0:T(8,128)(2,1)} %collective-permute-done.36.rb, ...), custom_call_target="tpu_custom_call" | custom-call | flops 20 | bytes 160000 | tf_op jit(solution)/shard_map/join/pallas_call | solution.py:562
  (91 shorter events, 23.4 us)
Async XLA Ops:
  0.6 16.4 %collective-permute-start.3 = (bf16[1024,256]{1,0:T(8,128)(2,1)}, bf16[1024,256]{1,0:T(8,128)(2,1)}, u32[]{:S(2)}, u32[]{:S(2)}) collective-permute-start(bf16[1024,256]{1,0:T(8,128)(2,1)} %refs_2_.1), channel_id=1, source_target_pairs={{0,2},{2,4},{4,6},{6,0},{1,3},{3,5},{5,7},{7,1},{8,10},{10,12},{12... | collective-permute-start | bytes 1572872 | tf_op jit(solution)/shard_map/ppermute | solution.py:37
  2.7 14.4 %collective-permute-start.5 = (bf16[1024,256]{1,0:T(8,128)(2,1)}, bf16[1024,256]{1,0:T(8,128)(2,1)}, u32[]{:S(2)}, u32[]{:S(2)}) collective-permute-start(bf16[1024,256]{1,0:T(8,128)(2,1)} %refs_2_.1), channel_id=1, source_target_pairs={{0,8},{8,0},{1,9},{9,1},{2,10},{10,2},{3,11},{11,3},{4,12},{12,4},... | collective-permute-start | bytes 1572872 | tf_op jit(solution)/shard_map/ppermute | solution.py:41
  4.2 14.1 %collective-permute-start.2 = (bf16[1024,256]{1,0:T(8,128)(2,1)}, bf16[1024,256]{1,0:T(8,128)(2,1)}, u32[]{:S(2)}, u32[]{:S(2)}) collective-permute-start(bf16[1024,256]{1,0:T(8,128)(2,1)} %refs_2_.1), channel_id=1, source_target_pairs={{0,1},{1,0},{2,3},{3,2},{4,5},{5,4},{6,7},{7,6},{8,9},{9,8},{10,11... | collective-permute-start | bytes 1572872 | tf_op jit(solution)/shard_map/ppermute | solution.py:41
  4.2 16.6 %collective-permute-start = (bf16[1024,256]{1,0:T(8,128)(2,1)}, bf16[1024,256]{1,0:T(8,128)(2,1)}, u32[]{:S(2)}, u32[]{:S(2)}) collective-permute-start(bf16[1024,256]{1,0:T(8,128)(2,1)} %refs_2_.1), channel_id=1, source_target_pairs={{0,6},{2,0},{4,2},{6,4},{1,7},{3,1},{5,3},{7,5},{8,14},{10,8},{12,... | collective-permute-start | bytes 1572872 | tf_op jit(solution)/shard_map/ppermute | solution.py:37
  17.1 7.3 %collective-permute-start.4 = (bf16[1024,256]{1,0:T(8,128)(2,1)}, bf16[1024,256]{1,0:T(8,128)(2,1)}, u32[]{:S(2)}, u32[]{:S(2)}) collective-permute-start(bf16[1024,256]{1,0:T(8,128)(2,1)} %collective-permute-done.3.refs_2_), channel_id=1, source_target_pairs={{0,1},{1,0},{2,3},{3,2},{4,5},{5,4},{6,7},{7,6},{8,9},{9,8},{10,11... | collective-permute-start | bytes 1572872 | tf_op jit(solution)/shard_map/ppermute | solution.py:41
  17.1 7.3 %collective-permute-start.6 = (bf16[1024,256]{1,0:T(8,128)(2,1)}, bf16[1024,256]{1,0:T(8,128)(2,1)}, u32[]{:S(2)}, u32[]{:S(2)}) collective-permute-start(bf16[1024,256]{1,0:T(8,128)(2,1)} %collective-permute-done.5.refs_4_), channel_id=1, source_target_pairs={{0,1},{1,0},{2,3},{3,2},{4,5},{5,4},{6,7},{7,6},{8,9},{9,8},{10,11... | collective-permute-start | bytes 1572872 | tf_op jit(solution)/shard_map/ppermute | solution.py:41
  17.6 16.8 %collective-permute-start.7 = (bf16[1024,256]{1,0:T(8,128)(2,1)}, bf16[1024,256]{1,0:T(8,128)(2,1)}, u32[]{:S(2)}, u32[]{:S(2)}) collective-permute-start(bf16[1024,256]{1,0:T(8,128)(2,1)} %collective-permute-done.3.refs_2_), channel_id=1, source_target_pairs={{0,2},{2,4},{4,6},{6,0},{1,3},{3,5},{5,7},{7,1},{8,10},{10,12},{12... | collective-permute-start | bytes 1572872 | tf_op jit(solution)/shard_map/ppermute | solution.py:37
  18.3 16.1 %collective-permute-start.8 = (bf16[1024,256]{1,0:T(8,128)(2,1)}, bf16[1024,256]{1,0:T(8,128)(2,1)}, u32[]{:S(2)}, u32[]{:S(2)}) collective-permute-start(bf16[1024,256]{1,0:T(8,128)(2,1)} %collective-permute-done.5.refs_4_), channel_id=1, source_target_pairs={{0,6},{2,0},{4,2},{6,4},{1,7},{3,1},{5,3},{7,5},{8,14},{10,8},{12,... | collective-permute-start | bytes 1572872 | tf_op jit(solution)/shard_map/ppermute | solution.py:37
  20.8 13.6 %collective-permute-start.9 = (bf16[1024,256]{1,0:T(8,128)(2,1)}, bf16[1024,256]{1,0:T(8,128)(2,1)}, u32[]{:S(2)}, u32[]{:S(2)}) collective-permute-start(bf16[1024,256]{1,0:T(8,128)(2,1)} %collective-permute-done.3.refs_2_), channel_id=1, source_target_pairs={{0,8},{8,0},{1,9},{9,1},{2,10},{10,2},{3,11},{11,3},{4,12},{12,4},... | collective-permute-start | bytes 1572872 | tf_op jit(solution)/shard_map/ppermute | solution.py:41
  24.3 12.1 %collective-permute-start.1 = (bf16[1024,256]{1,0:T(8,128)(2,1)}, bf16[1024,256]{1,0:T(8,128)(2,1)}, u32[]{:S(2)}, u32[]{:S(2)}) collective-permute-start(bf16[1024,256]{1,0:T(8,128)(2,1)} %collective-permute-done.refs_0_), channel_id=1, source_target_pairs={{0,1},{1,0},{2,3},{3,2},{4,5},{5,4},{6,7},{7,6},{8,9},{9,8},{10,11... | collective-permute-start | bytes 1572872 | tf_op jit(solution)/shard_map/ppermute | solution.py:41
  34.4 2.4 %collective-permute-start.10 = (bf16[1024,256]{1,0:T(8,128)(2,1)}, bf16[1024,256]{1,0:T(8,128)(2,1)}, u32[]{:S(2)}, u32[]{:S(2)}) collective-permute-start(bf16[1024,256]{1,0:T(8,128)(2,1)} %get-tuple-element.48.refs_2_), channel_id=1, source_target_pairs={{0,1},{1,0},{2,3},{3,2},{4,5},{5,4},{6,7},{7,6},{8,9},{9,8},{10,11... | collective-permute-start | bytes 1572872 | tf_op jit(solution)/shard_map/ppermute | solution.py:41
  35.0 2.6 %collective-permute-start.11 = (bf16[1024,256]{1,0:T(8,128)(2,1)}, bf16[1024,256]{1,0:T(8,128)(2,1)}, u32[]{:S(2)}, u32[]{:S(2)}) collective-permute-start(bf16[1024,256]{1,0:T(8,128)(2,1)} %get-tuple-element.49.refs_4_), channel_id=1, source_target_pairs={{0,1},{1,0},{2,3},{3,2},{4,5},{5,4},{6,7},{7,6},{8,9},{9,8},{10,11... | collective-permute-start | bytes 1572872 | tf_op jit(solution)/shard_map/ppermute | solution.py:41
  35.1 3.3 %collective-permute-start.12 = (bf16[1024,256]{1,0:T(8,128)(2,1)}, bf16[1024,256]{1,0:T(8,128)(2,1)}, u32[]{:S(2)}, u32[]{:S(2)}) collective-permute-start(bf16[1024,256]{1,0:T(8,128)(2,1)} %get-tuple-element.50.refs_6_), channel_id=1, source_target_pairs={{0,1},{1,0},{2,3},{3,2},{4,5},{5,4},{6,7},{7,6},{8,9},{9,8},{10,11... | collective-permute-start | bytes 1572872 | tf_op jit(solution)/shard_map/ppermute | solution.py:41
  35.5 15.9 %collective-permute-start.13 = (bf16[1024,256]{1,0:T(8,128)(2,1)}, bf16[1024,256]{1,0:T(8,128)(2,1)}, u32[]{:S(2)}, u32[]{:S(2)}) collective-permute-start(bf16[1024,256]{1,0:T(8,128)(2,1)} %get-tuple-element.48.refs_2_), channel_id=1, source_target_pairs={{0,8},{8,0},{1,9},{9,1},{2,10},{10,2},{3,11},{11,3},{4,12},{12,4},... | collective-permute-start | bytes 1572872 | tf_op jit(solution)/shard_map/ppermute | solution.py:41
  51.5 2.3 collective-permute-start.14
  66.0 5.7 %collective-permute-start.15 = (f32[8,1024]{1,0:T(8,128)}, f32[8,1024]{1,0:T(8,128)S(1)}, u32[]{:S(2)}, u32[]{:S(2)}) collective-permute-start(f32[8,1024]{1,0:T(8,128)} %get-tuple-element.56), channel_id=1, source_target_pairs={{0,64},{64,0},{1,65},{65,1},{2,66},{66,2},{3,67},{67,3},{4,68},{68... | collective-permute-start | bytes 98312 | tf_op jit(solution)/shard_map/ppermute | solution.py:41
  72.5 4.5 %copy-start = (f32[2,8,1024]{2,1,0:T(8,128)}, f32[2,8,1024]{2,1,0:T(8,128)S(1)}, u32[]{:S(2)}) copy-start(f32[2,8,1024]{2,1,0:T(8,128)S(1)} %pad_maximum_fusion.refs_0_) | copy-start | bytes 196612
  72.5 4.7 %collective-permute-start.16 = (f32[2,8,1024]{2,1,0:T(8,128)S(1)}, f32[2,8,1024]{2,1,0:T(8,128)S(1)}, u32[]{:S(2)}, u32[]{:S(2)}) collective-permute-start(f32[2,8,1024]{2,1,0:T(8,128)S(1)} %pad_maximum_fusion.refs_0_), channel_id=1, source_target_pairs={{0,16},{16,0},{32,48},{48,32},{1,17},{17,1},{33,49},{49,33},{2,18}... | collective-permute-start | bytes 196616 | tf_op jit(solution)/shard_map/ppermute | solution.py:41
  74.1 5.9 %collective-permute-start.17 = (f32[2,8,1024]{2,1,0:T(8,128)S(1)}, f32[2,8,1024]{2,1,0:T(8,128)S(1)}, u32[]{:S(2)}, u32[]{:S(2)}) collective-permute-start(f32[2,8,1024]{2,1,0:T(8,128)S(1)} %pad_maximum_fusion.refs_0_), channel_id=1, source_target_pairs={{0,32},{16,48},{32,0},{48,16},{1,33},{17,49},{33,1},{49,17},{2,34}... | collective-permute-start | bytes 196616 | tf_op jit(solution)/shard_map/ppermute | solution.py:41
  77.0 5.6 %collective-permute-start.18 = (f32[2,8,1024]{2,1,0:T(8,128)S(1)}, f32[2,8,1024]{2,1,0:T(8,128)}, u32[]{:S(2)}, u32[]{:S(2)}) collective-permute-start(f32[2,8,1024]{2,1,0:T(8,128)S(1)} %pad_maximum_fusion.refs_0_), channel_id=1, source_target_pairs={{0,48},{16,32},{32,16},{48,0},{1,49},{17,33},{33,17},{49,1},{2,50}... | collective-permute-start | bytes 196616 | tf_op jit(solution)/shard_map/ppermute | solution.py:41
  85.2 4.7 %collective-permute-start.19 = (f32[72,128]{1,0:T(8,128)}, f32[72,128]{1,0:T(8,128)S(1)}, u32[]{:S(2)}, u32[]{:S(2)}) collective-permute-start(f32[72,128]{1,0:T(8,128)} %get-tuple-element.58), channel_id=1, source_target_pairs={{0,2},{2,0},{4,6},{6,4},{1,3},{3,1},{5,7},{7,5},{8,10},{10,8},{12,... | collective-permute-start | bytes 110600 | tf_op jit(solution)/shard_map/ppermute | solution.py:41
  85.2 5.7 %collective-permute-start.20 = (f32[72,128]{1,0:T(8,128)}, f32[72,128]{1,0:T(8,128)S(1)}, u32[]{:S(2)}, u32[]{:S(2)}) collective-permute-start(f32[72,128]{1,0:T(8,128)} %get-tuple-element.58), channel_id=1, source_target_pairs={{0,4},{2,6},{4,0},{6,2},{1,5},{3,7},{5,1},{7,3},{8,12},{10,14},{12... | collective-permute-start | bytes 110600 | tf_op jit(solution)/shard_map/ppermute | solution.py:41
  88.1 5.4 %collective-permute-start.21 = (f32[72,128]{1,0:T(8,128)}, f32[72,128]{1,0:T(8,128)S(1)}, u32[]{:S(2)}, u32[]{:S(2)}) collective-permute-start(f32[72,128]{1,0:T(8,128)} %get-tuple-element.58), channel_id=1, source_target_pairs={{0,6},{2,4},{4,2},{6,0},{1,7},{3,5},{5,3},{7,1},{8,14},{10,12},{12... | collective-permute-start | bytes 110600 | tf_op jit(solution)/shard_map/ppermute | solution.py:41
  94.3 5.5 %copy-start.1 = (f32[72,128]{1,0:T(8,128)}, f32[72,128]{1,0:T(8,128)S(1)}, u32[]{:S(2)}) copy-start(f32[72,128]{1,0:T(8,128)S(1)} %add_add_fusion.p0) | copy-start | bytes 110596
  94.3 2.0 collective-permute-start.22
  94.4 4.0 %collective-permute-start.23 = (f32[72,128]{1,0:T(8,128)S(1)}, f32[72,128]{1,0:T(8,128)S(1)}, u32[]{:S(2)}, u32[]{:S(2)}) collective-permute-start(f32[72,128]{1,0:T(8,128)S(1)} %add_add_fusion.p0), channel_id=1, source_target_pairs={{0,8},{8,0},{1,9},{9,1},{2,10},{10,2},{3,11},{11,3},{4,12},{12,4},... | collective-permute-start | bytes 110600 | tf_op jit(solution)/shard_map/ppermute | solution.py:41
  95.7 3.4 %collective-permute-start.24 = (f32[72,128]{1,0:T(8,128)S(1)}, f32[72,128]{1,0:T(8,128)S(1)}, u32[]{:S(2)}, u32[]{:S(2)}) collective-permute-start(f32[72,128]{1,0:T(8,128)S(1)} %add_add_fusion.p0), channel_id=1, source_target_pairs={{0,9},{1,8},{8,1},{9,0},{2,11},{3,10},{10,3},{11,2},{4,13},{5,12},... | collective-permute-start | bytes 110600 | tf_op jit(solution)/shard_map/ppermute | solution.py:760
  111.1 8.3 %collective-permute-start.25 = (bf16[1,2,2,528,256]{4,3,2,1,0:T(8,128)(2,1)}, bf16[1,2,2,528,256]{4,3,2,1,0:T(8,128)(2,1)}, u32[]{:S(2)}, u32[]{:S(2)}) collective-permute-start(bf16[1,2,2,528,256]{4,3,2,1,0:T(8,128)(2,1)} %term_part.4.refs_0_), channel_id=1, source_target_pairs={{0,1},{1,0},{2,3},{3,2},{4,5},{5,4},{6,7},{7,6},{8,9},{9,8},{10,11... | collective-permute-start | bytes 3244040 | tf_op jit(solution)/shard_map/ppermute | solution.py:41
  119.0 24.1 %collective-permute-start.26 = (bf16[3,2,2,528,256]{4,3,2,1,0:T(8,128)(2,1)}, bf16[3,2,2,528,256]{4,3,2,1,0:T(8,128)(2,1)}, u32[]{:S(2)}, u32[]{:S(2)}) collective-permute-start(bf16[3,2,2,528,256]{4,3,2,1,0:T(8,128)(2,1)} %term_part.5.refs_0_), channel_id=1, source_target_pairs={{0,1},{1,0},{2,3},{3,2},{4,5},{5,4},{6,7},{7,6},{8,9},{9,8},{10,11... | collective-permute-start | bytes 9732104 | tf_op jit(solution)/shard_map/ppermute | solution.py:41
  124.5 15.9 %collective-permute-start.27 = (bf16[2,528,256]{2,1,0:T(8,128)(2,1)}, bf16[2,528,256]{2,1,0:T(8,128)(2,1)}, u32[]{:S(2)}, u32[]{:S(2)}) collective-permute-start(bf16[2,528,256]{2,1,0:T(8,128)(2,1)} %get-tuple-element.64.refs_0_), channel_id=1, source_target_pairs={{0,2},{2,4},{4,6},{6,0},{1,3},{3,5},{5,7},{7,1},{8,10},{10,12},{12... | collective-permute-start | bytes 1622024 | tf_op jit(solution)/shard_map/ppermute | solution.py:37
  124.5 18.6 %collective-permute-start.28 = (bf16[2,528,256]{2,1,0:T(8,128)(2,1)}, bf16[2,528,256]{2,1,0:T(8,128)(2,1)}, u32[]{:S(2)}, u32[]{:S(2)}) collective-permute-start(bf16[2,528,256]{2,1,0:T(8,128)(2,1)} %get-tuple-element.68), channel_id=1, source_target_pairs={{0,6},{2,0},{4,2},{6,4},{1,7},{3,1},{5,3},{7,5},{8,14},{10,8},{12,... | collective-permute-start | bytes 1622024 | tf_op jit(solution)/shard_map/ppermute | solution.py:37
  134.2 22.8 %collective-permute-start.33 = (bf16[2,688,256]{2,1,0:T(8,128)(2,1)}, bf16[2,688,256]{2,1,0:T(8,128)(2,1)}, u32[]{:S(2)}, u32[]{:S(2)}) collective-permute-start(bf16[2,688,256]{2,1,0:T(8,128)(2,1)} %get-tuple-element.67.refs_0_), channel_id=1, source_target_pairs={{0,16},{16,32},{32,48},{48,0},{1,17},{17,33},{33,49},{49,1},{2,18}... | collective-permute-start | bytes 2113544 | tf_op jit(solution)/shard_map/ppermute | solution.py:37
  134.2 22.8 %collective-permute-start.34 = (bf16[2,688,256]{2,1,0:T(8,128)(2,1)}, bf16[2,688,256]{2,1,0:T(8,128)(2,1)}, u32[]{:S(2)}, u32[]{:S(2)}) collective-permute-start(bf16[2,688,256]{2,1,0:T(8,128)(2,1)} %get-tuple-element.77), channel_id=1, source_target_pairs={{0,48},{16,0},{32,16},{48,32},{1,49},{17,1},{33,17},{49,33},{2,50}... | collective-permute-start | bytes 2113544 | tf_op jit(solution)/shard_map/ppermute | solution.py:37
  140.4 16.6 %collective-permute-start.32 = (bf16[1,2,312,256]{3,2,1,0:T(8,128)(2,1)}, bf16[1,2,312,256]{3,2,1,0:T(8,128)(2,1)}, u32[]{:S(2)}, u32[]{:S(2)}) collective-permute-start(bf16[1,2,312,256]{3,2,1,0:T(8,128)(2,1)} %get-tuple-element.76), channel_id=1, source_target_pairs={{0,64},{64,0},{1,65},{65,1},{2,66},{66,2},{3,67},{67,3},{4,68},{68... | collective-permute-start | bytes 958472 | tf_op jit(solution)/shard_map/ppermute | solution.py:41
  153.7 26.3 %collective-permute-start.29 = (bf16[2,2,528,256]{3,2,1,0:T(8,128)(2,1)}, bf16[2,2,528,256]{3,2,1,0:T(8,128)(2,1)}, u32[]{:S(2)}, u32[]{:S(2)}) collective-permute-start(bf16[2,2,528,256]{3,2,1,0:T(8,128)(2,1)} %get-tuple-element.70), channel_id=1, source_target_pairs={{0,2},{2,4},{4,6},{6,0},{1,3},{3,5},{5,7},{7,1},{8,10},{10,12},{12... | collective-permute-start | bytes 3244040 | tf_op jit(solution)/shard_map/ppermute | solution.py:37
  153.7 26.3 %collective-permute-start.30 = (bf16[2,2,528,256]{3,2,1,0:T(8,128)(2,1)}, bf16[2,2,528,256]{3,2,1,0:T(8,128)(2,1)}, u32[]{:S(2)}, u32[]{:S(2)}) collective-permute-start(bf16[2,2,528,256]{3,2,1,0:T(8,128)(2,1)} %get-tuple-element.71), channel_id=1, source_target_pairs={{0,6},{2,0},{4,2},{6,4},{1,7},{3,1},{5,3},{7,5},{8,14},{10,8},{12,... | collective-permute-start | bytes 3244040 | tf_op jit(solution)/shard_map/ppermute | solution.py:37
  167.1 32.8 %collective-permute-start.35 = (bf16[2,2,688,256]{3,2,1,0:T(8,128)(2,1)}, bf16[2,2,688,256]{3,2,1,0:T(8,128)(2,1)}, u32[]{:S(2)}, u32[]{:S(2)}) collective-permute-start(bf16[2,2,688,256]{3,2,1,0:T(8,128)(2,1)} %get-tuple-element.78.refs_0_), channel_id=1, source_target_pairs={{0,16},{16,32},{32,48},{48,0},{1,17},{17,33},{33,49},{49,1},{2,18}... | collective-permute-start | bytes 4227080 | tf_op jit(solution)/shard_map/ppermute | solution.py:37
  167.1 32.8 %collective-permute-start.36 = (bf16[2,2,688,256]{3,2,1,0:T(8,128)(2,1)}, bf16[2,2,688,256]{3,2,1,0:T(8,128)(2,1)}, u32[]{:S(2)}, u32[]{:S(2)}) collective-permute-start(bf16[2,2,688,256]{3,2,1,0:T(8,128)(2,1)} %get-tuple-element.80), channel_id=1, source_target_pairs={{0,48},{16,0},{32,16},{48,32},{1,49},{17,1},{33,17},{49,33},{2,50}... | collective-permute-start | bytes 4227080 | tf_op jit(solution)/shard_map/ppermute | solution.py:37
  170.3 32.9 %collective-permute-start.39 = (bf16[2,2,312,256]{3,2,1,0:T(8,128)(2,1)}, bf16[2,2,312,256]{3,2,1,0:T(8,128)(2,1)}, u32[]{:S(2)}, u32[]{:S(2)}) collective-permute-start(bf16[2,2,312,256]{3,2,1,0:T(8,128)(2,1)} %get-tuple-element.85), channel_id=1, source_target_pairs={{0,64},{64,0},{1,65},{65,1},{2,66},{66,2},{3,67},{67,3},{4,68},{68... | collective-permute-start | bytes 1916936 | tf_op jit(solution)/shard_map/ppermute | solution.py:41
  190.1 13.0 %collective-permute-start.38 = (bf16[1,2,312,256]{3,2,1,0:T(8,128)(2,1)}, bf16[1,2,312,256]{3,2,1,0:T(8,128)(2,1)}, u32[]{:S(2)}, u32[]{:S(2)}) collective-permute-start(bf16[1,2,312,256]{3,2,1,0:T(8,128)(2,1)} %get-tuple-element.82), channel_id=1, source_target_pairs={{0,64},{64,0},{1,65},{65,1},{2,66},{66,2},{3,67},{67,3},{4,68},{68... | collective-permute-start | bytes 958472 | tf_op jit(solution)/shard_map/ppermute | solution.py:41
  191.0 21.4 %collective-permute-start.31 = (bf16[2,528,256]{2,1,0:T(8,128)(2,1)}, bf16[2,528,256]{2,1,0:T(8,128)(2,1)}, u32[]{:S(2)}, u32[]{:S(2)}) collective-permute-start(bf16[2,528,256]{2,1,0:T(8,128)(2,1)} %get-tuple-element.73), channel_id=1, source_target_pairs={{0,8},{8,0},{1,9},{9,1},{2,10},{10,2},{3,11},{11,3},{4,12},{12,4},... | collective-permute-start | bytes 1622024 | tf_op jit(solution)/shard_map/ppermute | solution.py:41
  202.3 26.8 %collective-permute-start.37 = (bf16[2,688,256]{2,1,0:T(8,128)(2,1)}, bf16[2,688,256]{2,1,0:T(8,128)(2,1)}, u32[]{:S(2)}, u32[]{:S(2)}) collective-permute-start(bf16[2,688,256]{2,1,0:T(8,128)(2,1)} %fusion._), channel_id=1, source_target_pairs={{0,64},{64,0},{1,65},{65,1},{2,66},{66,2},{3,67},{67,3},{4,68},{68... | collective-permute-start | bytes 2113544 | tf_op jit(solution)/shard_map/ppermute | solution.py:41
  205.7 11.9 %collective-permute-start.40 = (bf16[2,328,256]{2,1,0:T(8,128)(2,1)}, bf16[2,328,256]{2,1,0:T(8,128)(2,1)}, u32[]{:S(2)}, u32[]{:S(2)}) collective-permute-start(bf16[2,328,256]{2,1,0:T(8,128)(2,1)} %get-tuple-element.87), channel_id=1, source_target_pairs={{0,16},{16,32},{32,48},{48,0},{1,17},{17,33},{33,49},{49,1},{2,18}... | collective-permute-start | bytes 1007624 | tf_op jit(solution)/shard_map/ppermute | solution.py:37
  205.7 16.7 %collective-permute-start.41 = (bf16[2,328,256]{2,1,0:T(8,128)(2,1)}, bf16[2,328,256]{2,1,0:T(8,128)(2,1)}, u32[]{:S(2)}, u32[]{:S(2)}) collective-permute-start(bf16[2,328,256]{2,1,0:T(8,128)(2,1)} %get-tuple-element.88), channel_id=1, source_target_pairs={{0,32},{16,48},{32,0},{48,16},{1,33},{17,49},{33,1},{49,17},{2,34}... | collective-permute-start | bytes 1007624 | tf_op jit(solution)/shard_map/ppermute | solution.py:37
  210.1 12.3 %collective-permute-start.42 = (bf16[2,328,256]{2,1,0:T(8,128)(2,1)}, bf16[2,328,256]{2,1,0:T(8,128)(2,1)}, u32[]{:S(2)}, u32[]{:S(2)}) collective-permute-start(bf16[2,328,256]{2,1,0:T(8,128)(2,1)} %get-tuple-element.89), channel_id=1, source_target_pairs={{0,48},{16,0},{32,16},{48,32},{1,49},{17,1},{33,17},{49,33},{2,50}... | collective-permute-start | bytes 1007624 | tf_op jit(solution)/shard_map/ppermute | solution.py:37
  223.8 9.6 %collective-permute-start.43 = (f32[8,256]{1,0:T(8,128)}, f32[8,256]{1,0:T(8,128)S(1)}, u32[]{:S(2)}, u32[]{:S(2)}) collective-permute-start(f32[8,256]{1,0:T(8,128)} %gain_along_y.1.here), channel_id=1, source_target_pairs={{0,64},{64,0},{1,65},{65,1},{2,66},{66,2},{3,67},{67,3},{4,68},{68... | collective-permute-start | bytes 24584 | tf_op jit(solution)/shard_map/ppermute | solution.py:41
  226.6 6.9 %collective-permute-start.44 = (f32[8,256]{1,0:T(8,128)}, f32[8,256]{1,0:T(8,128)S(1)}, u32[]{:S(2)}, u32[]{:S(2)}) collective-permute-start(f32[8,256]{1,0:T(8,128)} %gain_along_y.1.here), channel_id=1, source_target_pairs={{0,8},{8,0},{1,9},{9,1},{2,10},{10,2},{3,11},{11,3},{4,12},{12,4},... | collective-permute-start | bytes 24584 | tf_op jit(solution)/shard_map/ppermute | solution.py:41
  226.9 6.6 %collective-permute-start.45 = (f32[8,256]{1,0:T(8,128)}, f32[8,256]{1,0:T(8,128)S(1)}, u32[]{:S(2)}, u32[]{:S(2)}) collective-permute-start(f32[8,256]{1,0:T(8,128)} %gain_along_y.1.here), channel_id=1, source_target_pairs={{0,72},{8,64},{64,8},{72,0},{1,73},{9,65},{65,9},{73,1},{2,74},{10... | collective-permute-start | bytes 24584 | tf_op jit(solution)/shard_map/ppermute | solution.py:787
  (8 other events, 9.4 us)

commit v4 on v2

--- a/solution.py
+++ b/solution.py
@@ -767,8 +767,8 @@
     low = [shift(low_1, "y", 1), shift(low_2, "y", 2), shift(low_3, "y", 3)]
     hidden_grad = final(ids, (), keep, swap(send, "xl"), hidden, gain, inv, dots)
     gain_grad = gain_along_y(ids, (hidden_grad, swap_0), partial, *low)
-    gain_grad = gain_grad + swap(gain_grad, "xh")
-    gain_grad = gain_grad[0] + swap(gain_grad[1], "xl")
+    both = lax.ppermute(gain_grad, ("xh", "xl"), [(i, i ^ 3) for i in range(4)])
+    gain_grad = (gain_grad[0] + swap(gain_grad, "xh")[0]) + (swap(gain_grad, "xl")[1] + both[1])
     head_t = join(ids, hidden_grad, a_0, ra, rb, got, keep_0, swap_0, *low)
     return losses[0, :3], hidden_grad, head_t.T, gain_grad
 

time: 236 us -> 233 us (0.987)
  waiting for transfers between devices: 62.7 us -> 56.5 us
  starting transfers between devices: 51.8 us -> 54.7 us
    ppermute x29, waiting for transfers between devices: 35.5 us -> 29.1 us  [swap(): return lax.ppermute(x, axis, [(i, i ^ bits) for i in range(SIZES[axis])])]
  transfers between devices with their start and end apart: 45 -> 46, of which waited for: 19 -> 19; matrix products, arithmetic and copies ran while one was open for 3% -> 3% of each run, Pallas kernels for 34% -> 34%
where the time goes in v4:
time: 233 us; the launch traced here: 232 us
  Pallas kernels  110 us (47%)
  waiting for transfers between devices  56.5 us (24%)
  starting transfers between devices  54.7 us (23%)
  other arithmetic  5.3 us (2%)
  local copies, waits for them, and re-layouts  4.49 us (2%)
    ppermute x29, waiting for transfers between devices, swap(): return lax.ppermute(x, axis, [(i, i ^ bits) for i in range(SIZES[axis])])  29.1 us
    pallas_call x4, Pallas kernels, term_part(): pl.pallas_call(later(len(after), functools.partial(term_kernel, count, sp...  28.2 us
    ppermute x29, starting transfers between devices, swap(): return lax.ppermute(x, axis, [(i, i ^ bits) for i in range(SIZES[axis])])  27.9 us
    ppermute x15, waiting for transfers between devices, shift(): return lax.ppermute(x, axis, [(i, (i + step) % n) for i in range(n)])  26.6 us
    ppermute x15, starting transfers between devices, shift(): return lax.ppermute(x, axis, [(i, (i + step) % n) for i in range(n)])  23.9 us
    pallas_call x2, Pallas kernels, forward(): pl.pallas_call(functools.partial(forward_kernel, places, not state), out_...  23.1 us
    pallas_call x3, Pallas kernels, head_part(): pl.pallas_call(later(len(after), functools.partial(head_kernel, steps, sp...  22.9 us
    pallas_call x1, Pallas kernels, forward_last(): pl.pallas_call(functools.partial(forward_last_kernel, place), out_shape=[...  12.3 us
  transfers between devices with their start and end apart: 46, of which 19 were waited for; matrix products, arithmetic and copies ran while one was open for 3% of the time, Pallas kernels for 34%

profile of v4, /device:TPU:0, one launch (start us, length us, event | category | flops | bytes accessed | tf_op | source)
XLA Modules:
  0.0 232.1 jit_solution(8058141680592261985)
XLA Ops:
  0.6 2.1 collective-permute-start.3
  2.7 1.5 collective-permute-start.5
  4.2 2.2 collective-permute-start
  6.4 10.7 %collective-permute-done.3.refs_2_ = bf16[1024,256]{1,0:T(8,128)(2,1)} collective-permute-done((bf16[1024,256]{1,0:T(8,128)(2,1)}, bf16[1024,256]{1,0:T(8,128)(2,1)}, u32[]{:S(2)}, u32[]{:S(2)}) %collective-permute-start.3) | collective-permute-done | bytes 524320 | tf_op jit(solution)/shard_map/ppermute | solution.py:37
  18.3 2.5 %collective-permute-start.8 = (bf16[1024,256]{1,0:T(8,128)(2,1)}, bf16[1024,256]{1,0:T(8,128)(2,1)}, u32[]{:S(2)}, u32[]{:S(2)}) collective-permute-start(bf16[1024,256]{1,0:T(8,128)(2,1)} %collective-permute-done.5.refs_4_), channel_id=1, source_target_pairs={{0,6},{2,0},{4,2},{6,4},{1,7},{3,1},{5,3},{7,5},{8,14},{10,8},{12,... | collective-permute-start | bytes 1572872 | tf_op jit(solution)/shard_map/ppermute | solution.py:37
  20.8 1.5 collective-permute-start.9
  24.4 10.1 %forward_part.2 = (f32[1024,1000]{1,0:T(8,128)}, f32[1024,128]{1,0:T(8,128)}, bf16[8,2,1024,256]{3,2,1,0:T(8,128)(2,1)}) custom-call(s32[14]{0:T(128)} %concatenate.3.ids, bf16[1024,256]{1,0:T(8,128)(2,1)} %refs_2_.1, bf16[1024,256]{1,0:T(8,128)(2,1)} %collective-permute-done.2.refs_1_, bf16[1024,256]{1,0:T(8,128)(2,1)} %collective-permute-done.3.refs_2_, ...), custom_call_target="tpu_custom_call" | custom-call | flops 62914560 | bytes 340000 | tf_op jit(solution)/shard_map/forward_part/pallas_call | solution.py:168
  38.4 13.1 %forward_part.3 = (f32[1024,1000]{1,0:T(8,128)}, f32[1024,128]{1,0:T(8,128)}, bf16[8,2,1024,256]{3,2,1,0:T(8,128)(2,1)}) custom-call(s32[14]{0:T(128)} %concatenate.3.ids, bf16[1024,256]{1,0:T(8,128)(2,1)} %collective-permute-done.refs_0_, ...), custom_call_target="tpu_custom_call", output_to_operand_aliasing={{0}: (11, {}), {1}: (12, {}), {2}: (13, {})} | custom-call | flops 83886080 | bytes 400000 | tf_op jit(solution)/shard_map/forward_part/pallas_call | solution.py:168
  52.0 1.9 collective-permute-done.14.a1
  53.9 12.3 %forward_last.1 = (bf16[1024,1000]{1,0:T(8,128)(2,1)}, bf16[8,2,1024,256]{3,2,1,0:T(8,128)(2,1)}, f32[1024,1]{1,0:T(8,128)}, bf16[1024,1000]{1,0:T(8,128)(2,1)}, f32[8,1024]{1,0:T(8,128)}) custom-call(s32[14]{0:T(128)} %concatenate.3.ids, s32[8]{0:T(128)} %lengths.1, bf16[1024,256]{1,0:T(8,128)(2,1)} %touch.3.a0, ...), custom_call_target="tpu_custom_call", output_to_operand_aliasing={{1}: (9, {})} | custom-call | flops 20971520 | bytes 400000 | tf_op jit(solution)/shard_map/forward_last/pallas_call | solution.py:221
  66.1 2.8 %collective-permute-start.15 = (f32[8,1024]{1,0:T(8,128)}, f32[8,1024]{1,0:T(8,128)S(1)}, u32[]{:S(2)}, u32[]{:S(2)}) collective-permute-start(f32[8,1024]{1,0:T(8,128)} %get-tuple-element.56), channel_id=1, source_target_pairs={{0,64},{64,0},{1,65},{65,1},{2,66},{66,2},{3,67},{67,3},{4,68},{68... | collective-permute-start | bytes 98312 | tf_op jit(solution)/shard_map/ppermute | solution.py:41
  69.0 2.9 %collective-permute-done.15 = f32[8,1024]{1,0:T(8,128)S(1)} collective-permute-done((f32[8,1024]{1,0:T(8,128)}, f32[8,1024]{1,0:T(8,128)S(1)}, u32[]{:S(2)}, u32[]{:S(2)}) %collective-permute-start.15) | collective-permute-done | bytes 32800 | tf_op jit(solution)/shard_map/ppermute | solution.py:41
  72.6 1.6 collective-permute-start.16
  74.2 2.9 %collective-permute-start.17 = (f32[2,8,1024]{2,1,0:T(8,128)S(1)}, f32[2,8,1024]{2,1,0:T(8,128)S(1)}, u32[]{:S(2)}, u32[]{:S(2)}) collective-permute-start(f32[2,8,1024]{2,1,0:T(8,128)S(1)} %pad_maximum_fusion.refs_0_), channel_id=1, source_target_pairs={{0,32},{16,48},{32,0},{48,16},{1,33},{17,49},{33,1},{49,17},{2,34}... | collective-permute-start | bytes 196616 | tf_op jit(solution)/shard_map/ppermute | solution.py:41
  77.3 2.8 %collective-permute-done.17.refs_2_ = f32[2,8,1024]{2,1,0:T(8,128)S(1)} collective-permute-done((f32[2,8,1024]{2,1,0:T(8,128)S(1)}, f32[2,8,1024]{2,1,0:T(8,128)S(1)}, u32[]{:S(2)}, u32[]{:S(2)}) %collective-permute-start.17) | collective-permute-done | bytes 65568 | tf_op jit(solution)/shard_map/ppermute | solution.py:41
  80.8 2.0 collective-permute-done.18.refs_3_
  82.7 2.6 %gram.1 = (f32[64,1024]{1,0:T(8,128)}, f32[72,128]{1,0:T(8,128)}) custom-call(s32[14]{0:T(128)} %concatenate.3.ids, f32[2,8,1024]{2,1,0:T(8,128)} %copy-done, f32[2,8,1024]{2,1,0:T(8,128)} %copy-done.2, f32[2,8,1024]{2,1,0:T(8,128)} %copy-done.3, f32[2,8,1024]{2,1,0:T(8,128)} %collective-permute-done.18.refs_3_), custom_call_target="tpu_custom_call" | custom-call | tf_op jit(solution)/shard_map/gram/pallas_call | solution.py:291
  85.3 2.9 %collective-permute-start.20 = (f32[72,128]{1,0:T(8,128)}, f32[72,128]{1,0:T(8,128)S(1)}, u32[]{:S(2)}, u32[]{:S(2)}) collective-permute-start(f32[72,128]{1,0:T(8,128)} %get-tuple-element.58), channel_id=1, source_target_pairs={{0,4},{2,6},{4,0},{6,2},{1,5},{3,7},{5,1},{7,3},{8,12},{10,14},{12... | collective-permute-start | bytes 110600 | tf_op jit(solution)/shard_map/ppermute | solution.py:41
  88.2 1.8 collective-permute-start.21
  91.0 2.6 %collective-permute-done.21 = f32[72,128]{1,0:T(8,128)S(1)} collective-permute-done((f32[72,128]{1,0:T(8,128)}, f32[72,128]{1,0:T(8,128)S(1)}, u32[]{:S(2)}, u32[]{:S(2)}) %collective-permute-start.21) | collective-permute-done | bytes 36896 | tf_op jit(solution)/shard_map/ppermute | solution.py:41
  96.3 2.2 collective-permute-done.23.p2
  99.8 6.6 %logit_grad.1 = (bf16[1024,1000]{1,0:T(8,128)(2,1)}, bf16[1000,1024]{1,0:T(8,128)(2,1)}, f32[16,256]{1,0:T(8,128)}, f32[8,128]{1,0:T(8,128)}) custom-call(s32[14]{0:T(128)} %concatenate.3.ids, f32[64,1024]{1,0:T(8,128)} %get-tuple-element.57.every, f32[72,128]{1,0:T(8,128)} %copy-done.1, f32[72,128]{1,0:T(8,128)} %copy-done.4, f32[72,128]{1,0:T(8,128)} %copy-done.5, ...), custom_call_target="tpu_custom_call" | custom-call | flops 409600 | bytes 240000 | tf_op jit(solution)/shard_map/logit_grad/pallas_call | solution.py:388
  106.4 4.7 %term_part.4.refs_0_ = bf16[1,2,2,528,256]{4,3,2,1,0:T(8,128)(2,1)} custom-call(s32[14]{0:T(128)} %concatenate.3.ids, bf16[1024,1000]{1,0:T(8,128)(2,1)} %get-tuple-element.62.refs_0_.refs_1_, bf16[1000,4096]{1,0:T(8,128)(2,1)} %bitcast.19, bf16[1000,4096]{1,0:T(8,128)(2,1)} %bitcast.20, f32[16,256]{1,0:T(8,128)} %get-tuple-element.63.refs_3_.refs_4_), custom_call_target="tpu_custom_call" | custom-call | flops 20971520 | bytes 103383 | tf_op jit(solution)/shard_map/term_part/pallas_call | solution.py:625
  111.2 7.7 %term_part.5.refs_0_ = bf16[3,2,2,528,256]{4,3,2,1,0:T(8,128)(2,1)} custom-call(s32[14]{0:T(128)} %concatenate.3.ids, bf16[1,2,2,528,256]{4,3,2,1,0:T(8,128)(2,1)} %term_part.4.refs_0_, bf16[1024,1000]{1,0:T(8,128)(2,1)} %get-tuple-element.62.refs_0_.refs_1_, bf16[1000,4096]{1,0:T(8,128)(2,1)} %bitcast.21, bf16[1000,4096]{1,0:T(8,128)(2,1)} %bitcast.22, ...), custom_call_target="tpu_custom_call" | custom-call | flops 62914560000 | bytes 228229120 | tf_op jit(solution)/shard_map/term_part/pallas_call | solution.py:625
  119.3 5.1 %term_part.6 = (bf16[2,528,256]{2,1,0:T(8,128)(2,1)}, bf16[2,528,256]{2,1,0:T(8,128)(2,1)}) custom-call(s32[14]{0:T(128)} %concatenate.3.ids, bf16[3,2,2,528,256]{4,3,2,1,0:T(8,128)(2,1)} %term_part.5.refs_0_, bf16[1024,1000]{1,0:T(8,128)(2,1)} %get-tuple-element.62.refs_0_.refs_1_, bf16[1000,4096]{1,0:T(8,128)(2,1)} %bitcast.23, ...), custom_call_target="tpu_custom_call" | custom-call | flops 20971520 | bytes 103383 | tf_op jit(solution)/shard_map/term_part/pallas_call | solution.py:625
  124.4 3.2 %collective-permute-start.28 = (bf16[2,528,256]{2,1,0:T(8,128)(2,1)}, bf16[2,528,256]{2,1,0:T(8,128)(2,1)}, u32[]{:S(2)}, u32[]{:S(2)}) collective-permute-start(bf16[2,528,256]{2,1,0:T(8,128)(2,1)} %get-tuple-element.68), channel_id=1, source_target_pairs={{0,6},{2,0},{4,2},{6,4},{1,7},{3,1},{5,3},{7,5},{8,14},{10,8},{12,... | collective-permute-start | bytes 1622024 | tf_op jit(solution)/shard_map/ppermute | solution.py:37
  127.6 6.4 %head_part.3 = (bf16[2,688,256]{2,1,0:T(8,128)(2,1)}, bf16[2,688,256]{2,1,0:T(8,128)(2,1)}, bf16[1,2,312,256]{3,2,1,0:T(8,128)(2,1)}, bf16[1,2,312,256]{3,2,1,0:T(8,128)(2,1)}) custom-call(s32[14]{0:T(128)} %concatenate.3.ids, bf16[2,528,256]{2,1,0:T(8,128)(2,1)} %get-tuple-element.64.refs_0_, bf16[1000,1024]{1,0:T(8,128)(2,1)} %get-tuple-element.65.refs_1_.refs_2_, ...), custom_call_target="tpu_custom_call" | custom-call | flops 41943040000 | bytes 123863040 | tf_op jit(solution)/shard_map/head_part/pallas_call | solution.py:475
  134.1 3.2 %collective-permute-start.34 = (bf16[2,688,256]{2,1,0:T(8,128)(2,1)}, bf16[2,688,256]{2,1,0:T(8,128)(2,1)}, u32[]{:S(2)}, u32[]{:S(2)}) collective-permute-start(bf16[2,688,256]{2,1,0:T(8,128)(2,1)} %get-tuple-element.77), channel_id=1, source_target_pairs={{0,48},{16,0},{32,16},{48,32},{1,49},{17,1},{33,17},{49,33},{2,50}... | collective-permute-start | bytes 2113544 | tf_op jit(solution)/shard_map/ppermute | solution.py:37
  137.3 2.9 %collective-permute-done.27.refs_6_ = bf16[2,528,256]{2,1,0:T(8,128)(2,1)} collective-permute-done((bf16[2,528,256]{2,1,0:T(8,128)(2,1)}, bf16[2,528,256]{2,1,0:T(8,128)(2,1)}, u32[]{:S(2)}, u32[]{:S(2)}) %collective-permute-start.27) | collective-permute-done | bytes 540704 | tf_op jit(solution)/shard_map/ppermute | solution.py:37
  140.2 2.7 %collective-permute-start.32 = (bf16[1,2,312,256]{3,2,1,0:T(8,128)(2,1)}, bf16[1,2,312,256]{3,2,1,0:T(8,128)(2,1)}, u32[]{:S(2)}, u32[]{:S(2)}) collective-permute-start(bf16[1,2,312,256]{3,2,1,0:T(8,128)(2,1)} %get-tuple-element.76), channel_id=1, source_target_pairs={{0,64},{64,0},{1,65},{65,1},{2,66},{66,2},{3,67},{67,3},{4,68},{68... | collective-permute-start | bytes 958472 | tf_op jit(solution)/shard_map/ppermute | solution.py:41
  143.0 10.7 %term_part.7 = (bf16[2,2,528,256]{3,2,1,0:T(8,128)(2,1)}, bf16[2,2,528,256]{3,2,1,0:T(8,128)(2,1)}, bf16[2,2,528,256]{3,2,1,0:T(8,128)(2,1)}) custom-call(s32[14]{0:T(128)} %concatenate.3.ids, bf16[2,688,256]{2,1,0:T(8,128)(2,1)} %get-tuple-element.67.refs_0_, bf16[1024,1000]{1,0:T(8,128)(2,1)} %get-tuple-element.62.refs_0_.refs_1_, ...), custom_call_target="tpu_custom_call" | custom-call | flops 62914560000 | bytes 228229120 | tf_op jit(solution)/shard_map/term_part/pallas_call | solution.py:625
  153.7 3.2 %collective-permute-start.30 = (bf16[2,2,528,256]{3,2,1,0:T(8,128)(2,1)}, bf16[2,2,528,256]{3,2,1,0:T(8,128)(2,1)}, u32[]{:S(2)}, u32[]{:S(2)}) collective-permute-start(bf16[2,2,528,256]{3,2,1,0:T(8,128)(2,1)} %get-tuple-element.71), channel_id=1, source_target_pairs={{0,6},{2,0},{4,2},{6,4},{1,7},{3,1},{5,3},{7,5},{8,14},{10,8},{12,... | collective-permute-start | bytes 3244040 | tf_op jit(solution)/shard_map/ppermute | solution.py:37
  156.9 10.0 %head_part.4 = (bf16[2,2,688,256]{3,2,1,0:T(8,128)(2,1)}, bf16[2,2,688,256]{3,2,1,0:T(8,128)(2,1)}, bf16[2,2,312,256]{3,2,1,0:T(8,128)(2,1)}, bf16[2,2,312,256]{3,2,1,0:T(8,128)(2,1)}) custom-call(s32[14]{0:T(128)} %concatenate.3.ids, bf16[2,2,528,256]{3,2,1,0:T(8,128)(2,1)} %get-tuple-element.69.refs_0_, ...), custom_call_target="tpu_custom_call" | custom-call | flops 83886080000 | bytes 206766080 | tf_op jit(solution)/shard_map/head_part/pallas_call | solution.py:475
  167.7 3.2 %collective-permute-start.36 = (bf16[2,2,688,256]{3,2,1,0:T(8,128)(2,1)}, bf16[2,2,688,256]{3,2,1,0:T(8,128)(2,1)}, u32[]{:S(2)}, u32[]{:S(2)}) collective-permute-start(bf16[2,2,688,256]{3,2,1,0:T(8,128)(2,1)} %get-tuple-element.80), channel_id=1, source_target_pairs={{0,48},{16,0},{32,16},{48,32},{1,49},{17,1},{33,17},{49,33},{2,50}... | collective-permute-start | bytes 4227080 | tf_op jit(solution)/shard_map/ppermute | solution.py:37
  171.0 9.0 %collective-permute-done.29.refs_1_ = bf16[2,2,528,256]{3,2,1,0:T(8,128)(2,1)} collective-permute-done((bf16[2,2,528,256]{3,2,1,0:T(8,128)(2,1)}, bf16[2,2,528,256]{3,2,1,0:T(8,128)(2,1)}, u32[]{:S(2)}, u32[]{:S(2)}) %collective-permute-start.29) | collective-permute-done | bytes 1081376 | tf_op jit(solution)/shard_map/ppermute | solution.py:37
  180.0 3.5 %term_sum.1 = (bf16[1024,256]{1,0:T(8,128)(2,1)}, bf16[2,528,256]{2,1,0:T(8,128)(2,1)}, f32[16,256]{1,0:T(8,128)}, f32[2,256]{1,0:T(2,128)}) custom-call(bf16[2,2,528,256]{3,2,1,0:T(8,128)(2,1)} %get-tuple-element.69.refs_0_, bf16[2,2,528,256]{3,2,1,0:T(8,128)(2,1)} %collective-permute-done.29.refs_1_, ...), custom_call_target="tpu_custom_call" | custom-call | flops 20000 | bytes 100000 | tf_op jit(solution)/shard_map/term_sum/pallas_call | solution.py:671
  183.5 6.4 %head_part.5 = (bf16[2,2,688,256]{3,2,1,0:T(8,128)(2,1)}, bf16[1,2,312,256]{3,2,1,0:T(8,128)(2,1)}, bf16[1,2,312,256]{3,2,1,0:T(8,128)(2,1)}) custom-call(s32[14]{0:T(128)} %concatenate.3.ids, bf16[2,2,688,256]{3,2,1,0:T(8,128)(2,1)} %get-tuple-element.78.refs_0_, bf16[1024,256]{1,0:T(8,128)(2,1)} %get-tuple-element.72.refs_0_.refs_1_, ...), custom_call_target="tpu_custom_call" | custom-call | flops 41943040000 | bytes 123863040 | tf_op jit(solution)/shard_map/head_part/pallas_call | solution.py:475
  191.8 10.5 %collective-permute-done.38._.swapped.refs_1_ = bf16[1,2,312,256]{3,2,1,0:T(8,128)(2,1)} collective-permute-done((bf16[1,2,312,256]{3,2,1,0:T(8,128)(2,1)}, bf16[1,2,312,256]{3,2,1,0:T(8,128)(2,1)}, u32[]{:S(2)}, u32[]{:S(2)}) %collective-permute-start.38) | collective-permute-done | bytes 319520 | tf_op jit(solution)/shard_map/ppermute | solution.py:41
  202.2 2.5 %low_sum.1 = (bf16[2,328,256]{2,1,0:T(8,128)(2,1)}, bf16[2,328,256]{2,1,0:T(8,128)(2,1)}, bf16[2,328,256]{2,1,0:T(8,128)(2,1)}) custom-call(bf16[1,2,312,256]{3,2,1,0:T(8,128)(2,1)} %collective-permute-done.38._.swapped.refs_1_, f32[2,256]{1,0:T(2,128)} %get-tuple-element.83.gain.refs_2_, bf16[2,2,312,256]{3,2,1,0:T(8,128)(2,1)} %get-tuple-element.84.a13, ...), custom_call_target="tpu_custom_call" | custom-call | flops 20 | bytes 80000 | tf_op jit(solution)/shard_map/low_sum/pallas_call | solution.py:513
  204.8 1.7 collective-permute-start.41
  206.5 1.7 collective-permute-start.42
  208.2 2.5 %fusion = bf16[2,688,256]{2,1,0:T(8,128)(2,1)} fusion(bf16[2,2,688,256]{3,2,1,0:T(8,128)(2,1)} %collective-permute-done.36.rb, bf16[2,2,688,256]{3,2,1,0:T(8,128)(2,1)} %collective-permute-done.35.ra, bf16[2,2,688,256]{3,2,1,0:T(8,128)(2,1)} %get-tuple-element.79.a0), kind=kLoop, calls=%fused_computation.1 | loop fusion | flops 704512 | bytes 2818048 | tf_op jit(solution)/shard_map/add | solution.py:765
  211.5 2.8 %hidden_grad.1._.refs_0_ = bf16[1024,256]{1,0:T(8,128)(2,1)} custom-call(s32[14]{0:T(128)} %concatenate.3.ids, bf16[1024,256]{1,0:T(8,128)(2,1)} %get-tuple-element.72.refs_0_.refs_1_, bf16[2,528,256]{2,1,0:T(8,128)(2,1)} %collective-permute-done.31.refs_1_, bf16[1024,256]{1,0:T(8,128)(2,1)} %refs_2_.1, f32[1,4096]{1,0:T(1,128)} %bitcast.34, ...), custom_call_target="tpu_custom_call" | custom-call | flops 20000 | bytes 40000 | tf_op jit(solution)/shard_map/hidden_grad/pallas_call | solution.py:703
  214.3 3.3 %collective-permute-done.40.b1.refs_3_ = bf16[2,328,256]{2,1,0:T(8,128)(2,1)} collective-permute-done((bf16[2,328,256]{2,1,0:T(8,128)(2,1)}, bf16[2,328,256]{2,1,0:T(8,128)(2,1)}, u32[]{:S(2)}, u32[]{:S(2)}) %collective-permute-start.40) | collective-permute-done | bytes 335904 | tf_op jit(solution)/shard_map/ppermute | solution.py:37
  218.2 1.4 gain_along_y.1
  221.4 2.4 %collective-permute-start.45 = (f32[8,256]{1,0:T(8,128)}, f32[8,256]{1,0:T(8,128)S(1)}, u32[]{:S(2)}, u32[]{:S(2)}) collective-permute-start(f32[8,256]{1,0:T(8,128)} %gain_along_y.1), channel_id=1, source_target_pairs={{0,72},{8,64},{64,8},{72,0},{1,73},{9,65},{65,9},{73,1},{2,74},{10... | collective-permute-start | bytes 24584 | tf_op jit(solution)/shard_map/ppermute | solution.py:770
  224.9 1.3 collective-permute-done.43
  227.7 4.3 %join.1 = bf16[1000,512]{1,0:T(8,128)(2,1)} custom-call(s32[14]{0:T(128)} %concatenate.3.ids, bf16[1024,256]{1,0:T(8,128)(2,1)} %hidden_grad.1._.refs_0_, bf16[2,2,688,256]{3,2,1,0:T(8,128)(2,1)} %get-tuple-element.79.a0, bf16[2,2,688,256]{3,2,1,0:T(8,128)(2,1)} %collective-permute-done.35.ra, bf16[2,2,688,256]{3,2,1,0:T(8,128)(2,1)} %collective-permute-done.36.rb, ...), custom_call_target="tpu_custom_call" | custom-call | flops 20 | bytes 160000 | tf_op jit(solution)/shard_map/join/pallas_call | solution.py:562
  (85 shorter events, 23.4 us)
Async XLA Ops:
  0.6 16.4 %collective-permute-start.3 = (bf16[1024,256]{1,0:T(8,128)(2,1)}, bf16[1024,256]{1,0:T(8,128)(2,1)}, u32[]{:S(2)}, u32[]{:S(2)}) collective-permute-start(bf16[1024,256]{1,0:T(8,128)(2,1)} %refs_2_.1), channel_id=1, source_target_pairs={{0,2},{2,4},{4,6},{6,0},{1,3},{3,5},{5,7},{7,1},{8,10},{10,12},{12... | collective-permute-start | bytes 1572872 | tf_op jit(solution)/shard_map/ppermute | solution.py:37
  2.7 14.4 %collective-permute-start.5 = (bf16[1024,256]{1,0:T(8,128)(2,1)}, bf16[1024,256]{1,0:T(8,128)(2,1)}, u32[]{:S(2)}, u32[]{:S(2)}) collective-permute-start(bf16[1024,256]{1,0:T(8,128)(2,1)} %refs_2_.1), channel_id=1, source_target_pairs={{0,8},{8,0},{1,9},{9,1},{2,10},{10,2},{3,11},{11,3},{4,12},{12,4},... | collective-permute-start | bytes 1572872 | tf_op jit(solution)/shard_map/ppermute | solution.py:41
  4.2 14.1 %collective-permute-start.2 = (bf16[1024,256]{1,0:T(8,128)(2,1)}, bf16[1024,256]{1,0:T(8,128)(2,1)}, u32[]{:S(2)}, u32[]{:S(2)}) collective-permute-start(bf16[1024,256]{1,0:T(8,128)(2,1)} %refs_2_.1), channel_id=1, source_target_pairs={{0,1},{1,0},{2,3},{3,2},{4,5},{5,4},{6,7},{7,6},{8,9},{9,8},{10,11... | collective-permute-start | bytes 1572872 | tf_op jit(solution)/shard_map/ppermute | solution.py:41
  4.2 16.6 %collective-permute-start = (bf16[1024,256]{1,0:T(8,128)(2,1)}, bf16[1024,256]{1,0:T(8,128)(2,1)}, u32[]{:S(2)}, u32[]{:S(2)}) collective-permute-start(bf16[1024,256]{1,0:T(8,128)(2,1)} %refs_2_.1), channel_id=1, source_target_pairs={{0,6},{2,0},{4,2},{6,4},{1,7},{3,1},{5,3},{7,5},{8,14},{10,8},{12,... | collective-permute-start | bytes 1572872 | tf_op jit(solution)/shard_map/ppermute | solution.py:37
  17.1 7.3 %collective-permute-start.4 = (bf16[1024,256]{1,0:T(8,128)(2,1)}, bf16[1024,256]{1,0:T(8,128)(2,1)}, u32[]{:S(2)}, u32[]{:S(2)}) collective-permute-start(bf16[1024,256]{1,0:T(8,128)(2,1)} %collective-permute-done.3.refs_2_), channel_id=1, source_target_pairs={{0,1},{1,0},{2,3},{3,2},{4,5},{5,4},{6,7},{7,6},{8,9},{9,8},{10,11... | collective-permute-start | bytes 1572872 | tf_op jit(solution)/shard_map/ppermute | solution.py:41
  17.1 7.3 %collective-permute-start.6 = (bf16[1024,256]{1,0:T(8,128)(2,1)}, bf16[1024,256]{1,0:T(8,128)(2,1)}, u32[]{:S(2)}, u32[]{:S(2)}) collective-permute-start(bf16[1024,256]{1,0:T(8,128)(2,1)} %collective-permute-done.5.refs_4_), channel_id=1, source_target_pairs={{0,1},{1,0},{2,3},{3,2},{4,5},{5,4},{6,7},{7,6},{8,9},{9,8},{10,11... | collective-permute-start | bytes 1572872 | tf_op jit(solution)/shard_map/ppermute | solution.py:41
  17.6 16.9 %collective-permute-start.7 = (bf16[1024,256]{1,0:T(8,128)(2,1)}, bf16[1024,256]{1,0:T(8,128)(2,1)}, u32[]{:S(2)}, u32[]{:S(2)}) collective-permute-start(bf16[1024,256]{1,0:T(8,128)(2,1)} %collective-permute-done.3.refs_2_), channel_id=1, source_target_pairs={{0,2},{2,4},{4,6},{6,0},{1,3},{3,5},{5,7},{7,1},{8,10},{10,12},{12... | collective-permute-start | bytes 1572872 | tf_op jit(solution)/shard_map/ppermute | solution.py:37
  18.3 16.1 %collective-permute-start.8 = (bf16[1024,256]{1,0:T(8,128)(2,1)}, bf16[1024,256]{1,0:T(8,128)(2,1)}, u32[]{:S(2)}, u32[]{:S(2)}) collective-permute-start(bf16[1024,256]{1,0:T(8,128)(2,1)} %collective-permute-done.5.refs_4_), channel_id=1, source_target_pairs={{0,6},{2,0},{4,2},{6,4},{1,7},{3,1},{5,3},{7,5},{8,14},{10,8},{12,... | collective-permute-start | bytes 1572872 | tf_op jit(solution)/shard_map/ppermute | solution.py:37
  20.8 13.6 %collective-permute-start.9 = (bf16[1024,256]{1,0:T(8,128)(2,1)}, bf16[1024,256]{1,0:T(8,128)(2,1)}, u32[]{:S(2)}, u32[]{:S(2)}) collective-permute-start(bf16[1024,256]{1,0:T(8,128)(2,1)} %collective-permute-done.3.refs_2_), channel_id=1, source_target_pairs={{0,8},{8,0},{1,9},{9,1},{2,10},{10,2},{3,11},{11,3},{4,12},{12,4},... | collective-permute-start | bytes 1572872 | tf_op jit(solution)/shard_map/ppermute | solution.py:41
  24.4 12.1 %collective-permute-start.1 = (bf16[1024,256]{1,0:T(8,128)(2,1)}, bf16[1024,256]{1,0:T(8,128)(2,1)}, u32[]{:S(2)}, u32[]{:S(2)}) collective-permute-start(bf16[1024,256]{1,0:T(8,128)(2,1)} %collective-permute-done.refs_0_), channel_id=1, source_target_pairs={{0,1},{1,0},{2,3},{3,2},{4,5},{5,4},{6,7},{7,6},{8,9},{9,8},{10,11... | collective-permute-start | bytes 1572872 | tf_op jit(solution)/shard_map/ppermute | solution.py:41
  34.5 2.4 %collective-permute-start.10 = (bf16[1024,256]{1,0:T(8,128)(2,1)}, bf16[1024,256]{1,0:T(8,128)(2,1)}, u32[]{:S(2)}, u32[]{:S(2)}) collective-permute-start(bf16[1024,256]{1,0:T(8,128)(2,1)} %get-tuple-element.48.refs_2_), channel_id=1, source_target_pairs={{0,1},{1,0},{2,3},{3,2},{4,5},{5,4},{6,7},{7,6},{8,9},{9,8},{10,11... | collective-permute-start | bytes 1572872 | tf_op jit(solution)/shard_map/ppermute | solution.py:41
  35.0 2.6 %collective-permute-start.11 = (bf16[1024,256]{1,0:T(8,128)(2,1)}, bf16[1024,256]{1,0:T(8,128)(2,1)}, u32[]{:S(2)}, u32[]{:S(2)}) collective-permute-start(bf16[1024,256]{1,0:T(8,128)(2,1)} %get-tuple-element.49.refs_4_), channel_id=1, source_target_pairs={{0,1},{1,0},{2,3},{3,2},{4,5},{5,4},{6,7},{7,6},{8,9},{9,8},{10,11... | collective-permute-start | bytes 1572872 | tf_op jit(solution)/shard_map/ppermute | solution.py:41
  35.1 3.3 %collective-permute-start.12 = (bf16[1024,256]{1,0:T(8,128)(2,1)}, bf16[1024,256]{1,0:T(8,128)(2,1)}, u32[]{:S(2)}, u32[]{:S(2)}) collective-permute-start(bf16[1024,256]{1,0:T(8,128)(2,1)} %get-tuple-element.50.refs_6_), channel_id=1, source_target_pairs={{0,1},{1,0},{2,3},{3,2},{4,5},{5,4},{6,7},{7,6},{8,9},{9,8},{10,11... | collective-permute-start | bytes 1572872 | tf_op jit(solution)/shard_map/ppermute | solution.py:41
  35.6 15.9 %collective-permute-start.13 = (bf16[1024,256]{1,0:T(8,128)(2,1)}, bf16[1024,256]{1,0:T(8,128)(2,1)}, u32[]{:S(2)}, u32[]{:S(2)}) collective-permute-start(bf16[1024,256]{1,0:T(8,128)(2,1)} %get-tuple-element.48.refs_2_), channel_id=1, source_target_pairs={{0,8},{8,0},{1,9},{9,1},{2,10},{10,2},{3,11},{11,3},{4,12},{12,4},... | collective-permute-start | bytes 1572872 | tf_op jit(solution)/shard_map/ppermute | solution.py:41
  51.5 2.3 %collective-permute-start.14 = (bf16[1024,256]{1,0:T(8,128)(2,1)}, bf16[1024,256]{1,0:T(8,128)(2,1)}, u32[]{:S(2)}, u32[]{:S(2)}) collective-permute-start(bf16[1024,256]{1,0:T(8,128)(2,1)} %touch.3.a0), channel_id=1, source_target_pairs={{0,1},{1,0},{2,3},{3,2},{4,5},{5,4},{6,7},{7,6},{8,9},{9,8},{10,11... | collective-permute-start | bytes 1572872 | tf_op jit(solution)/shard_map/ppermute | solution.py:41
  66.1 5.7 %collective-permute-start.15 = (f32[8,1024]{1,0:T(8,128)}, f32[8,1024]{1,0:T(8,128)S(1)}, u32[]{:S(2)}, u32[]{:S(2)}) collective-permute-start(f32[8,1024]{1,0:T(8,128)} %get-tuple-element.56), channel_id=1, source_target_pairs={{0,64},{64,0},{1,65},{65,1},{2,66},{66,2},{3,67},{67,3},{4,68},{68... | collective-permute-start | bytes 98312 | tf_op jit(solution)/shard_map/ppermute | solution.py:41
  72.6 4.5 %copy-start = (f32[2,8,1024]{2,1,0:T(8,128)}, f32[2,8,1024]{2,1,0:T(8,128)S(1)}, u32[]{:S(2)}) copy-start(f32[2,8,1024]{2,1,0:T(8,128)S(1)} %pad_maximum_fusion.refs_0_) | copy-start | bytes 196612
  72.6 4.7 %collective-permute-start.16 = (f32[2,8,1024]{2,1,0:T(8,128)S(1)}, f32[2,8,1024]{2,1,0:T(8,128)S(1)}, u32[]{:S(2)}, u32[]{:S(2)}) collective-permute-start(f32[2,8,1024]{2,1,0:T(8,128)S(1)} %pad_maximum_fusion.refs_0_), channel_id=1, source_target_pairs={{0,16},{16,0},{32,48},{48,32},{1,17},{17,1},{33,49},{49,33},{2,18}... | collective-permute-start | bytes 196616 | tf_op jit(solution)/shard_map/ppermute | solution.py:41
  74.2 5.9 %collective-permute-start.17 = (f32[2,8,1024]{2,1,0:T(8,128)S(1)}, f32[2,8,1024]{2,1,0:T(8,128)S(1)}, u32[]{:S(2)}, u32[]{:S(2)}) collective-permute-start(f32[2,8,1024]{2,1,0:T(8,128)S(1)} %pad_maximum_fusion.refs_0_), channel_id=1, source_target_pairs={{0,32},{16,48},{32,0},{48,16},{1,33},{17,49},{33,1},{49,17},{2,34}... | collective-permute-start | bytes 196616 | tf_op jit(solution)/shard_map/ppermute | solution.py:41
  77.1 5.6 %collective-permute-start.18 = (f32[2,8,1024]{2,1,0:T(8,128)S(1)}, f32[2,8,1024]{2,1,0:T(8,128)}, u32[]{:S(2)}, u32[]{:S(2)}) collective-permute-start(f32[2,8,1024]{2,1,0:T(8,128)S(1)} %pad_maximum_fusion.refs_0_), channel_id=1, source_target_pairs={{0,48},{16,32},{32,16},{48,0},{1,49},{17,33},{33,17},{49,1},{2,50}... | collective-permute-start | bytes 196616 | tf_op jit(solution)/shard_map/ppermute | solution.py:41
  85.3 4.7 %collective-permute-start.19 = (f32[72,128]{1,0:T(8,128)}, f32[72,128]{1,0:T(8,128)S(1)}, u32[]{:S(2)}, u32[]{:S(2)}) collective-permute-start(f32[72,128]{1,0:T(8,128)} %get-tuple-element.58), channel_id=1, source_target_pairs={{0,2},{2,0},{4,6},{6,4},{1,3},{3,1},{5,7},{7,5},{8,10},{10,8},{12,... | collective-permute-start | bytes 110600 | tf_op jit(solution)/shard_map/ppermute | solution.py:41
  85.3 5.7 %collective-permute-start.20 = (f32[72,128]{1,0:T(8,128)}, f32[72,128]{1,0:T(8,128)S(1)}, u32[]{:S(2)}, u32[]{:S(2)}) collective-permute-start(f32[72,128]{1,0:T(8,128)} %get-tuple-element.58), channel_id=1, source_target_pairs={{0,4},{2,6},{4,0},{6,2},{1,5},{3,7},{5,1},{7,3},{8,12},{10,14},{12... | collective-permute-start | bytes 110600 | tf_op jit(solution)/shard_map/ppermute | solution.py:41
  88.2 5.4 %collective-permute-start.21 = (f32[72,128]{1,0:T(8,128)}, f32[72,128]{1,0:T(8,128)S(1)}, u32[]{:S(2)}, u32[]{:S(2)}) collective-permute-start(f32[72,128]{1,0:T(8,128)} %get-tuple-element.58), channel_id=1, source_target_pairs={{0,6},{2,4},{4,2},{6,0},{1,7},{3,5},{5,3},{7,1},{8,14},{10,12},{12... | collective-permute-start | bytes 110600 | tf_op jit(solution)/shard_map/ppermute | solution.py:41
  94.4 5.4 %copy-start.1 = (f32[72,128]{1,0:T(8,128)}, f32[72,128]{1,0:T(8,128)S(1)}, u32[]{:S(2)}) copy-start(f32[72,128]{1,0:T(8,128)S(1)} %add_add_fusion.p0) | copy-start | bytes 110596
  94.4 2.0 collective-permute-start.22
  94.5 4.0 %collective-permute-start.23 = (f32[72,128]{1,0:T(8,128)S(1)}, f32[72,128]{1,0:T(8,128)S(1)}, u32[]{:S(2)}, u32[]{:S(2)}) collective-permute-start(f32[72,128]{1,0:T(8,128)S(1)} %add_add_fusion.p0), channel_id=1, source_target_pairs={{0,8},{8,0},{1,9},{9,1},{2,10},{10,2},{3,11},{11,3},{4,12},{12,4},... | collective-permute-start | bytes 110600 | tf_op jit(solution)/shard_map/ppermute | solution.py:41
  95.7 3.4 %collective-permute-start.24 = (f32[72,128]{1,0:T(8,128)S(1)}, f32[72,128]{1,0:T(8,128)S(1)}, u32[]{:S(2)}, u32[]{:S(2)}) collective-permute-start(f32[72,128]{1,0:T(8,128)S(1)} %add_add_fusion.p0), channel_id=1, source_target_pairs={{0,9},{1,8},{8,1},{9,0},{2,11},{3,10},{10,3},{11,2},{4,13},{5,12},... | collective-permute-start | bytes 110600 | tf_op jit(solution)/shard_map/ppermute | solution.py:744
  111.1 8.2 %collective-permute-start.25 = (bf16[1,2,2,528,256]{4,3,2,1,0:T(8,128)(2,1)}, bf16[1,2,2,528,256]{4,3,2,1,0:T(8,128)(2,1)}, u32[]{:S(2)}, u32[]{:S(2)}) collective-permute-start(bf16[1,2,2,528,256]{4,3,2,1,0:T(8,128)(2,1)} %term_part.4.refs_0_), channel_id=1, source_target_pairs={{0,1},{1,0},{2,3},{3,2},{4,5},{5,4},{6,7},{7,6},{8,9},{9,8},{10,11... | collective-permute-start | bytes 3244040 | tf_op jit(solution)/shard_map/ppermute | solution.py:41
  119.0 24.0 %collective-permute-start.26 = (bf16[3,2,2,528,256]{4,3,2,1,0:T(8,128)(2,1)}, bf16[3,2,2,528,256]{4,3,2,1,0:T(8,128)(2,1)}, u32[]{:S(2)}, u32[]{:S(2)}) collective-permute-start(bf16[3,2,2,528,256]{4,3,2,1,0:T(8,128)(2,1)} %term_part.5.refs_0_), channel_id=1, source_target_pairs={{0,1},{1,0},{2,3},{3,2},{4,5},{5,4},{6,7},{7,6},{8,9},{9,8},{10,11... | collective-permute-start | bytes 9732104 | tf_op jit(solution)/shard_map/ppermute | solution.py:41
  124.4 15.9 %collective-permute-start.27 = (bf16[2,528,256]{2,1,0:T(8,128)(2,1)}, bf16[2,528,256]{2,1,0:T(8,128)(2,1)}, u32[]{:S(2)}, u32[]{:S(2)}) collective-permute-start(bf16[2,528,256]{2,1,0:T(8,128)(2,1)} %get-tuple-element.64.refs_0_), channel_id=1, source_target_pairs={{0,2},{2,4},{4,6},{6,0},{1,3},{3,5},{5,7},{7,1},{8,10},{10,12},{12... | collective-permute-start | bytes 1622024 | tf_op jit(solution)/shard_map/ppermute | solution.py:37
  124.4 18.6 %collective-permute-start.28 = (bf16[2,528,256]{2,1,0:T(8,128)(2,1)}, bf16[2,528,256]{2,1,0:T(8,128)(2,1)}, u32[]{:S(2)}, u32[]{:S(2)}) collective-permute-start(bf16[2,528,256]{2,1,0:T(8,128)(2,1)} %get-tuple-element.68), channel_id=1, source_target_pairs={{0,6},{2,0},{4,2},{6,4},{1,7},{3,1},{5,3},{7,5},{8,14},{10,8},{12,... | collective-permute-start | bytes 1622024 | tf_op jit(solution)/shard_map/ppermute | solution.py:37
  134.1 22.8 %collective-permute-start.33 = (bf16[2,688,256]{2,1,0:T(8,128)(2,1)}, bf16[2,688,256]{2,1,0:T(8,128)(2,1)}, u32[]{:S(2)}, u32[]{:S(2)}) collective-permute-start(bf16[2,688,256]{2,1,0:T(8,128)(2,1)} %get-tuple-element.67.refs_0_), channel_id=1, source_target_pairs={{0,16},{16,32},{32,48},{48,0},{1,17},{17,33},{33,49},{49,1},{2,18}... | collective-permute-start | bytes 2113544 | tf_op jit(solution)/shard_map/ppermute | solution.py:37
  134.1 22.8 %collective-permute-start.34 = (bf16[2,688,256]{2,1,0:T(8,128)(2,1)}, bf16[2,688,256]{2,1,0:T(8,128)(2,1)}, u32[]{:S(2)}, u32[]{:S(2)}) collective-permute-start(bf16[2,688,256]{2,1,0:T(8,128)(2,1)} %get-tuple-element.77), channel_id=1, source_target_pairs={{0,48},{16,0},{32,16},{48,32},{1,49},{17,1},{33,17},{49,33},{2,50}... | collective-permute-start | bytes 2113544 | tf_op jit(solution)/shard_map/ppermute | solution.py:37
  140.2 16.6 %collective-permute-start.32 = (bf16[1,2,312,256]{3,2,1,0:T(8,128)(2,1)}, bf16[1,2,312,256]{3,2,1,0:T(8,128)(2,1)}, u32[]{:S(2)}, u32[]{:S(2)}) collective-permute-start(bf16[1,2,312,256]{3,2,1,0:T(8,128)(2,1)} %get-tuple-element.76), channel_id=1, source_target_pairs={{0,64},{64,0},{1,65},{65,1},{2,66},{66,2},{3,67},{67,3},{4,68},{68... | collective-permute-start | bytes 958472 | tf_op jit(solution)/shard_map/ppermute | solution.py:41
  153.7 26.3 %collective-permute-start.29 = (bf16[2,2,528,256]{3,2,1,0:T(8,128)(2,1)}, bf16[2,2,528,256]{3,2,1,0:T(8,128)(2,1)}, u32[]{:S(2)}, u32[]{:S(2)}) collective-permute-start(bf16[2,2,528,256]{3,2,1,0:T(8,128)(2,1)} %get-tuple-element.70), channel_id=1, source_target_pairs={{0,2},{2,4},{4,6},{6,0},{1,3},{3,5},{5,7},{7,1},{8,10},{10,12},{12... | collective-permute-start | bytes 3244040 | tf_op jit(solution)/shard_map/ppermute | solution.py:37
  153.7 26.3 %collective-permute-start.30 = (bf16[2,2,528,256]{3,2,1,0:T(8,128)(2,1)}, bf16[2,2,528,256]{3,2,1,0:T(8,128)(2,1)}, u32[]{:S(2)}, u32[]{:S(2)}) collective-permute-start(bf16[2,2,528,256]{3,2,1,0:T(8,128)(2,1)} %get-tuple-element.71), channel_id=1, source_target_pairs={{0,6},{2,0},{4,2},{6,4},{1,7},{3,1},{5,3},{7,5},{8,14},{10,8},{12,... | collective-permute-start | bytes 3244040 | tf_op jit(solution)/shard_map/ppermute | solution.py:37
  166.9 24.8 %collective-permute-start.39 = (bf16[2,2,312,256]{3,2,1,0:T(8,128)(2,1)}, bf16[2,2,312,256]{3,2,1,0:T(8,128)(2,1)}, u32[]{:S(2)}, u32[]{:S(2)}) collective-permute-start(bf16[2,2,312,256]{3,2,1,0:T(8,128)(2,1)} %get-tuple-element.85), channel_id=1, source_target_pairs={{0,64},{64,0},{1,65},{65,1},{2,66},{66,2},{3,67},{67,3},{4,68},{68... | collective-permute-start | bytes 1916936 | tf_op jit(solution)/shard_map/ppermute | solution.py:41
  167.7 38.8 %collective-permute-start.35 = (bf16[2,2,688,256]{3,2,1,0:T(8,128)(2,1)}, bf16[2,2,688,256]{3,2,1,0:T(8,128)(2,1)}, u32[]{:S(2)}, u32[]{:S(2)}) collective-permute-start(bf16[2,2,688,256]{3,2,1,0:T(8,128)(2,1)} %get-tuple-element.78.refs_0_), channel_id=1, source_target_pairs={{0,16},{16,32},{32,48},{48,0},{1,17},{17,33},{33,49},{49,1},{2,18}... | collective-permute-start | bytes 4227080 | tf_op jit(solution)/shard_map/ppermute | solution.py:37
  167.7 40.5 %collective-permute-start.36 = (bf16[2,2,688,256]{3,2,1,0:T(8,128)(2,1)}, bf16[2,2,688,256]{3,2,1,0:T(8,128)(2,1)}, u32[]{:S(2)}, u32[]{:S(2)}) collective-permute-start(bf16[2,2,688,256]{3,2,1,0:T(8,128)(2,1)} %get-tuple-element.80), channel_id=1, source_target_pairs={{0,48},{16,0},{32,16},{48,32},{1,49},{17,1},{33,17},{49,33},{2,50}... | collective-permute-start | bytes 4227080 | tf_op jit(solution)/shard_map/ppermute | solution.py:37
  190.0 12.3 %collective-permute-start.38 = (bf16[1,2,312,256]{3,2,1,0:T(8,128)(2,1)}, bf16[1,2,312,256]{3,2,1,0:T(8,128)(2,1)}, u32[]{:S(2)}, u32[]{:S(2)}) collective-permute-start(bf16[1,2,312,256]{3,2,1,0:T(8,128)(2,1)} %get-tuple-element.82), channel_id=1, source_target_pairs={{0,64},{64,0},{1,65},{65,1},{2,66},{66,2},{3,67},{67,3},{4,68},{68... | collective-permute-start | bytes 958472 | tf_op jit(solution)/shard_map/ppermute | solution.py:41
  190.8 20.8 %collective-permute-start.31 = (bf16[2,528,256]{2,1,0:T(8,128)(2,1)}, bf16[2,528,256]{2,1,0:T(8,128)(2,1)}, u32[]{:S(2)}, u32[]{:S(2)}) collective-permute-start(bf16[2,528,256]{2,1,0:T(8,128)(2,1)} %get-tuple-element.73), channel_id=1, source_target_pairs={{0,8},{8,0},{1,9},{9,1},{2,10},{10,2},{3,11},{11,3},{4,12},{12,4},... | collective-permute-start | bytes 1622024 | tf_op jit(solution)/shard_map/ppermute | solution.py:41
  204.8 12.8 %collective-permute-start.40 = (bf16[2,328,256]{2,1,0:T(8,128)(2,1)}, bf16[2,328,256]{2,1,0:T(8,128)(2,1)}, u32[]{:S(2)}, u32[]{:S(2)}) collective-permute-start(bf16[2,328,256]{2,1,0:T(8,128)(2,1)} %get-tuple-element.87), channel_id=1, source_target_pairs={{0,16},{16,32},{32,48},{48,0},{1,17},{17,33},{33,49},{49,1},{2,18}... | collective-permute-start | bytes 1007624 | tf_op jit(solution)/shard_map/ppermute | solution.py:37
  204.8 12.8 %collective-permute-start.41 = (bf16[2,328,256]{2,1,0:T(8,128)(2,1)}, bf16[2,328,256]{2,1,0:T(8,128)(2,1)}, u32[]{:S(2)}, u32[]{:S(2)}) collective-permute-start(bf16[2,328,256]{2,1,0:T(8,128)(2,1)} %get-tuple-element.88), channel_id=1, source_target_pairs={{0,32},{16,48},{32,0},{48,16},{1,33},{17,49},{33,1},{49,17},{2,34}... | collective-permute-start | bytes 1007624 | tf_op jit(solution)/shard_map/ppermute | solution.py:37
  206.5 11.7 %collective-permute-start.42 = (bf16[2,328,256]{2,1,0:T(8,128)(2,1)}, bf16[2,328,256]{2,1,0:T(8,128)(2,1)}, u32[]{:S(2)}, u32[]{:S(2)}) collective-permute-start(bf16[2,328,256]{2,1,0:T(8,128)(2,1)} %get-tuple-element.89), channel_id=1, source_target_pairs={{0,48},{16,0},{32,16},{48,32},{1,49},{17,1},{33,17},{49,33},{2,50}... | collective-permute-start | bytes 1007624 | tf_op jit(solution)/shard_map/ppermute | solution.py:37
  210.7 17.0 %collective-permute-start.37 = (bf16[2,688,256]{2,1,0:T(8,128)(2,1)}, bf16[2,688,256]{2,1,0:T(8,128)(2,1)}, u32[]{:S(2)}, u32[]{:S(2)}) collective-permute-start(bf16[2,688,256]{2,1,0:T(8,128)(2,1)} %fusion), channel_id=1, source_target_pairs={{0,64},{64,0},{1,65},{65,1},{2,66},{66,2},{3,67},{67,3},{4,68},{68... | collective-permute-start | bytes 2113544 | tf_op jit(solution)/shard_map/ppermute | solution.py:41
  219.6 6.6 %collective-permute-start.43 = (f32[8,256]{1,0:T(8,128)}, f32[8,256]{1,0:T(8,128)S(1)}, u32[]{:S(2)}, u32[]{:S(2)}) collective-permute-start(f32[8,256]{1,0:T(8,128)} %gain_along_y.1), channel_id=1, source_target_pairs={{0,64},{64,0},{1,65},{65,1},{2,66},{66,2},{3,67},{67,3},{4,68},{68... | collective-permute-start | bytes 24584 | tf_op jit(solution)/shard_map/ppermute | solution.py:41
  220.4 5.8 %collective-permute-start.44 = (f32[8,256]{1,0:T(8,128)}, f32[8,256]{1,0:T(8,128)S(1)}, u32[]{:S(2)}, u32[]{:S(2)}) collective-permute-start(f32[8,256]{1,0:T(8,128)} %gain_along_y.1), channel_id=1, source_target_pairs={{0,8},{8,0},{1,9},{9,1},{2,10},{10,2},{3,11},{11,3},{4,12},{12,4},... | collective-permute-start | bytes 24584 | tf_op jit(solution)/shard_map/ppermute | solution.py:41
  221.4 5.1 %collective-permute-start.45 = (f32[8,256]{1,0:T(8,128)}, f32[8,256]{1,0:T(8,128)S(1)}, u32[]{:S(2)}, u32[]{:S(2)}) collective-permute-start(f32[8,256]{1,0:T(8,128)} %gain_along_y.1), channel_id=1, source_target_pairs={{0,72},{8,64},{64,8},{72,0},{1,73},{9,65},{65,9},{73,1},{2,74},{10... | collective-permute-start | bytes 24584 | tf_op jit(solution)/shard_map/ppermute | solution.py:770
  (5 other events, 7.6 us)

commit v5 on v4

--- a/solution.py
+++ b/solution.py
@@ -19,7 +19,7 @@
 LEN = 128
 TERMS = 1000
 BLK = 256
-ROWS_A = 688
+ROWS_A = 752
 ROWS_B = TERMS - ROWS_A
 HALF = TOK // 2
 PER = 2

time: 233 us -> 239 us (1.026)
  waiting for transfers between devices: 56.5 us -> 59.9 us
  starting transfers between devices: 54.7 us -> 57.6 us
    ppermute x15, waiting for transfers between devices: 26.6 us -> 40.4 us  [shift(): return lax.ppermute(x, axis, [(i, (i + step) % n) for i in range(n)])]
    ppermute x29, waiting for transfers between devices: 29.1 us -> 17.4 us  [swap(): return lax.ppermute(x, axis, [(i, i ^ bits) for i in range(SIZES[axis])])]
  transfers between devices with their start and end apart: 46 -> 46, of which waited for: 19 -> 19; matrix products, arithmetic and copies ran while one was open for 3% -> 3% of each run, Pallas kernels for 34% -> 33%
where the time goes in v5:
time: 239 us; the launch traced here: 238 us
  Pallas kernels  110 us (46%)
  waiting for transfers between devices  59.9 us (25%)
  starting transfers between devices  57.6 us (24%)
  other arithmetic  5.39 us (2%)
  local copies, waits for them, and re-layouts  4.49 us (2%)
    ppermute x15, waiting for transfers between devices, shift(): return lax.ppermute(x, axis, [(i, (i + step) % n) for i in range(n)])  40.4 us
    ppermute x29, starting transfers between devices, swap(): return lax.ppermute(x, axis, [(i, i ^ bits) for i in range(SIZES[axis])])  29.8 us
    pallas_call x4, Pallas kernels, term_part(): pl.pallas_call(later(len(after), functools.partial(term_kernel, count, sp...  28.2 us
    ppermute x15, starting transfers between devices, shift(): return lax.ppermute(x, axis, [(i, (i + step) % n) for i in range(n)])  24.9 us
    pallas_call x2, Pallas kernels, forward(): pl.pallas_call(functools.partial(forward_kernel, places, not state), out_...  23.1 us
    pallas_call x3, Pallas kernels, head_part(): pl.pallas_call(later(len(after), functools.partial(head_kernel, steps, sp...  22.9 us
    ppermute x29, waiting for transfers between devices, swap(): return lax.ppermute(x, axis, [(i, i ^ bits) for i in range(SIZES[axis])])  17.4 us
    pallas_call x1, Pallas kernels, forward_last(): pl.pallas_call(functools.partial(forward_last_kernel, place), out_shape=[...  12.2 us
  transfers between devices with their start and end apart: 46, of which 19 were waited for; matrix products, arithmetic and copies ran while one was open for 3% of the time, Pallas kernels for 33%

profile of v5, /device:TPU:0, one launch (start us, length us, event | category | flops | bytes accessed | tf_op | source)
XLA Modules:
  0.0 238.2 jit_solution(12673740135262054421)
XLA Ops:
  0.6 2.1 collective-permute-start.3
  2.7 1.5 collective-permute-start.5
  4.2 2.2 collective-permute-start
  6.4 10.7 %collective-permute-done.3.refs_2_ = bf16[1024,256]{1,0:T(8,128)(2,1)} collective-permute-done((bf16[1024,256]{1,0:T(8,128)(2,1)}, bf16[1024,256]{1,0:T(8,128)(2,1)}, u32[]{:S(2)}, u32[]{:S(2)}) %collective-permute-start.3) | collective-permute-done | bytes 524320 | tf_op jit(solution)/shard_map/ppermute | solution.py:37
  18.3 2.5 %collective-permute-start.8 = (bf16[1024,256]{1,0:T(8,128)(2,1)}, bf16[1024,256]{1,0:T(8,128)(2,1)}, u32[]{:S(2)}, u32[]{:S(2)}) collective-permute-start(bf16[1024,256]{1,0:T(8,128)(2,1)} %collective-permute-done.5.refs_4_), channel_id=1, source_target_pairs={{0,6},{2,0},{4,2},{6,4},{1,7},{3,1},{5,3},{7,5},{8,14},{10,8},{12,... | collective-permute-start | bytes 1572872 | tf_op jit(solution)/shard_map/ppermute | solution.py:37
  20.8 1.5 collective-permute-start.9
  24.4 10.1 %forward_part.2 = (f32[1024,1000]{1,0:T(8,128)}, f32[1024,128]{1,0:T(8,128)}, bf16[8,2,1024,256]{3,2,1,0:T(8,128)(2,1)}) custom-call(s32[14]{0:T(128)} %concatenate.3.ids, bf16[1024,256]{1,0:T(8,128)(2,1)} %refs_2_.1, bf16[1024,256]{1,0:T(8,128)(2,1)} %collective-permute-done.2.refs_1_, bf16[1024,256]{1,0:T(8,128)(2,1)} %collective-permute-done.3.refs_2_, ...), custom_call_target="tpu_custom_call" | custom-call | flops 62914560 | bytes 340000 | tf_op jit(solution)/shard_map/forward_part/pallas_call | solution.py:168
  38.4 13.1 %forward_part.3 = (f32[1024,1000]{1,0:T(8,128)}, f32[1024,128]{1,0:T(8,128)}, bf16[8,2,1024,256]{3,2,1,0:T(8,128)(2,1)}) custom-call(s32[14]{0:T(128)} %concatenate.3.ids, bf16[1024,256]{1,0:T(8,128)(2,1)} %collective-permute-done.refs_0_, ...), custom_call_target="tpu_custom_call", output_to_operand_aliasing={{0}: (11, {}), {1}: (12, {}), {2}: (13, {})} | custom-call | flops 83886080 | bytes 400000 | tf_op jit(solution)/shard_map/forward_part/pallas_call | solution.py:168
  52.0 1.9 collective-permute-done.14.a1
  53.9 12.2 %forward_last.1 = (bf16[1024,1000]{1,0:T(8,128)(2,1)}, bf16[8,2,1024,256]{3,2,1,0:T(8,128)(2,1)}, f32[1024,1]{1,0:T(8,128)}, bf16[1024,1000]{1,0:T(8,128)(2,1)}, f32[8,1024]{1,0:T(8,128)}) custom-call(s32[14]{0:T(128)} %concatenate.3.ids, s32[8]{0:T(128)} %lengths.1, bf16[1024,256]{1,0:T(8,128)(2,1)} %touch.3.a0, ...), custom_call_target="tpu_custom_call", output_to_operand_aliasing={{1}: (9, {})} | custom-call | flops 20971520 | bytes 400000 | tf_op jit(solution)/shard_map/forward_last/pallas_call | solution.py:221
  66.1 2.8 %collective-permute-start.15 = (f32[8,1024]{1,0:T(8,128)}, f32[8,1024]{1,0:T(8,128)S(1)}, u32[]{:S(2)}, u32[]{:S(2)}) collective-permute-start(f32[8,1024]{1,0:T(8,128)} %get-tuple-element.56), channel_id=1, source_target_pairs={{0,64},{64,0},{1,65},{65,1},{2,66},{66,2},{3,67},{67,3},{4,68},{68... | collective-permute-start | bytes 98312 | tf_op jit(solution)/shard_map/ppermute | solution.py:41
  68.9 2.9 %collective-permute-done.15 = f32[8,1024]{1,0:T(8,128)S(1)} collective-permute-done((f32[8,1024]{1,0:T(8,128)}, f32[8,1024]{1,0:T(8,128)S(1)}, u32[]{:S(2)}, u32[]{:S(2)}) %collective-permute-start.15) | collective-permute-done | bytes 32800 | tf_op jit(solution)/shard_map/ppermute | solution.py:41
  72.6 1.6 collective-permute-start.16
  74.1 2.9 %collective-permute-start.17 = (f32[2,8,1024]{2,1,0:T(8,128)S(1)}, f32[2,8,1024]{2,1,0:T(8,128)S(1)}, u32[]{:S(2)}, u32[]{:S(2)}) collective-permute-start(f32[2,8,1024]{2,1,0:T(8,128)S(1)} %pad_maximum_fusion.refs_0_), channel_id=1, source_target_pairs={{0,32},{16,48},{32,0},{48,16},{1,33},{17,49},{33,1},{49,17},{2,34}... | collective-permute-start | bytes 196616 | tf_op jit(solution)/shard_map/ppermute | solution.py:41
  77.3 2.8 %collective-permute-done.17.refs_2_ = f32[2,8,1024]{2,1,0:T(8,128)S(1)} collective-permute-done((f32[2,8,1024]{2,1,0:T(8,128)S(1)}, f32[2,8,1024]{2,1,0:T(8,128)S(1)}, u32[]{:S(2)}, u32[]{:S(2)}) %collective-permute-start.17) | collective-permute-done | bytes 65568 | tf_op jit(solution)/shard_map/ppermute | solution.py:41
  80.7 2.0 collective-permute-done.18.refs_3_
  82.7 2.6 %gram.1 = (f32[64,1024]{1,0:T(8,128)}, f32[72,128]{1,0:T(8,128)}) custom-call(s32[14]{0:T(128)} %concatenate.3.ids, f32[2,8,1024]{2,1,0:T(8,128)} %copy-done, f32[2,8,1024]{2,1,0:T(8,128)} %copy-done.2, f32[2,8,1024]{2,1,0:T(8,128)} %copy-done.3, f32[2,8,1024]{2,1,0:T(8,128)} %collective-permute-done.18.refs_3_), custom_call_target="tpu_custom_call" | custom-call | tf_op jit(solution)/shard_map/gram/pallas_call | solution.py:291
  85.3 2.9 %collective-permute-start.20 = (f32[72,128]{1,0:T(8,128)}, f32[72,128]{1,0:T(8,128)S(1)}, u32[]{:S(2)}, u32[]{:S(2)}) collective-permute-start(f32[72,128]{1,0:T(8,128)} %get-tuple-element.58), channel_id=1, source_target_pairs={{0,4},{2,6},{4,0},{6,2},{1,5},{3,7},{5,1},{7,3},{8,12},{10,14},{12... | collective-permute-start | bytes 110600 | tf_op jit(solution)/shard_map/ppermute | solution.py:41
  88.2 1.8 collective-permute-start.21
  90.9 2.6 %collective-permute-done.21 = f32[72,128]{1,0:T(8,128)S(1)} collective-permute-done((f32[72,128]{1,0:T(8,128)}, f32[72,128]{1,0:T(8,128)S(1)}, u32[]{:S(2)}, u32[]{:S(2)}) %collective-permute-start.21) | collective-permute-done | bytes 36896 | tf_op jit(solution)/shard_map/ppermute | solution.py:41
  96.3 2.2 collective-permute-done.23.p2
  99.8 6.5 %logit_grad.1 = (bf16[1024,1000]{1,0:T(8,128)(2,1)}, bf16[1000,1024]{1,0:T(8,128)(2,1)}, f32[16,256]{1,0:T(8,128)}, f32[8,128]{1,0:T(8,128)}) custom-call(s32[14]{0:T(128)} %concatenate.3.ids, f32[64,1024]{1,0:T(8,128)} %get-tuple-element.57.every, f32[72,128]{1,0:T(8,128)} %copy-done.1, f32[72,128]{1,0:T(8,128)} %copy-done.4, f32[72,128]{1,0:T(8,128)} %copy-done.5, ...), custom_call_target="tpu_custom_call" | custom-call | flops 409600 | bytes 240000 | tf_op jit(solution)/shard_map/logit_grad/pallas_call | solution.py:388
  106.3 4.8 %term_part.4.refs_0_ = bf16[1,2,2,528,256]{4,3,2,1,0:T(8,128)(2,1)} custom-call(s32[14]{0:T(128)} %concatenate.3.ids, bf16[1024,1000]{1,0:T(8,128)(2,1)} %get-tuple-element.62.refs_0_.refs_1_, bf16[1000,4096]{1,0:T(8,128)(2,1)} %bitcast.19, bf16[1000,4096]{1,0:T(8,128)(2,1)} %bitcast.20, f32[16,256]{1,0:T(8,128)} %get-tuple-element.63.refs_3_.refs_4_), custom_call_target="tpu_custom_call" | custom-call | flops 20971520 | bytes 103383 | tf_op jit(solution)/shard_map/term_part/pallas_call | solution.py:625
  111.2 7.7 %term_part.5.refs_0_ = bf16[3,2,2,528,256]{4,3,2,1,0:T(8,128)(2,1)} custom-call(s32[14]{0:T(128)} %concatenate.3.ids, bf16[1,2,2,528,256]{4,3,2,1,0:T(8,128)(2,1)} %term_part.4.refs_0_, bf16[1024,1000]{1,0:T(8,128)(2,1)} %get-tuple-element.62.refs_0_.refs_1_, bf16[1000,4096]{1,0:T(8,128)(2,1)} %bitcast.21, bf16[1000,4096]{1,0:T(8,128)(2,1)} %bitcast.22, ...), custom_call_target="tpu_custom_call" | custom-call | flops 62914560000 | bytes 228229120 | tf_op jit(solution)/shard_map/term_part/pallas_call | solution.py:625
  119.3 5.1 %term_part.6 = (bf16[2,528,256]{2,1,0:T(8,128)(2,1)}, bf16[2,528,256]{2,1,0:T(8,128)(2,1)}) custom-call(s32[14]{0:T(128)} %concatenate.3.ids, bf16[3,2,2,528,256]{4,3,2,1,0:T(8,128)(2,1)} %term_part.5.refs_0_, bf16[1024,1000]{1,0:T(8,128)(2,1)} %get-tuple-element.62.refs_0_.refs_1_, bf16[1000,4096]{1,0:T(8,128)(2,1)} %bitcast.23, ...), custom_call_target="tpu_custom_call" | custom-call | flops 20971520 | bytes 103383 | tf_op jit(solution)/shard_map/term_part/pallas_call | solution.py:625
  124.4 3.2 %collective-permute-start.28 = (bf16[2,528,256]{2,1,0:T(8,128)(2,1)}, bf16[2,528,256]{2,1,0:T(8,128)(2,1)}, u32[]{:S(2)}, u32[]{:S(2)}) collective-permute-start(bf16[2,528,256]{2,1,0:T(8,128)(2,1)} %get-tuple-element.68), channel_id=1, source_target_pairs={{0,6},{2,0},{4,2},{6,4},{1,7},{3,1},{5,3},{7,5},{8,14},{10,8},{12,... | collective-permute-start | bytes 1622024 | tf_op jit(solution)/shard_map/ppermute | solution.py:37
  127.6 6.4 %head_part.3 = (bf16[2,752,256]{2,1,0:T(8,128)(2,1)}, bf16[2,752,256]{2,1,0:T(8,128)(2,1)}, bf16[1,2,248,256]{3,2,1,0:T(8,128)(2,1)}, bf16[1,2,248,256]{3,2,1,0:T(8,128)(2,1)}) custom-call(s32[14]{0:T(128)} %concatenate.3.ids, bf16[2,528,256]{2,1,0:T(8,128)(2,1)} %get-tuple-element.64.refs_0_, bf16[1000,1024]{1,0:T(8,128)(2,1)} %get-tuple-element.65.refs_1_.refs_2_, ...), custom_call_target="tpu_custom_call" | custom-call | flops 41943040000 | bytes 123863040 | tf_op jit(solution)/shard_map/head_part/pallas_call | solution.py:475
  134.0 3.2 %collective-permute-start.34 = (bf16[2,752,256]{2,1,0:T(8,128)(2,1)}, bf16[2,752,256]{2,1,0:T(8,128)(2,1)}, u32[]{:S(2)}, u32[]{:S(2)}) collective-permute-start(bf16[2,752,256]{2,1,0:T(8,128)(2,1)} %get-tuple-element.77), channel_id=1, source_target_pairs={{0,48},{16,0},{32,16},{48,32},{1,49},{17,1},{33,17},{49,33},{2,50}... | collective-permute-start | bytes 2310152 | tf_op jit(solution)/shard_map/ppermute | solution.py:37
  137.2 3.0 %collective-permute-done.27.refs_6_ = bf16[2,528,256]{2,1,0:T(8,128)(2,1)} collective-permute-done((bf16[2,528,256]{2,1,0:T(8,128)(2,1)}, bf16[2,528,256]{2,1,0:T(8,128)(2,1)}, u32[]{:S(2)}, u32[]{:S(2)}) %collective-permute-start.27) | collective-permute-done | bytes 540704 | tf_op jit(solution)/shard_map/ppermute | solution.py:37
  140.2 2.7 %collective-permute-start.32 = (bf16[1,2,248,256]{3,2,1,0:T(8,128)(2,1)}, bf16[1,2,248,256]{3,2,1,0:T(8,128)(2,1)}, u32[]{:S(2)}, u32[]{:S(2)}) collective-permute-start(bf16[1,2,248,256]{3,2,1,0:T(8,128)(2,1)} %get-tuple-element.76), channel_id=1, source_target_pairs={{0,64},{64,0},{1,65},{65,1},{2,66},{66,2},{3,67},{67,3},{4,68},{68... | collective-permute-start | bytes 761864 | tf_op jit(solution)/shard_map/ppermute | solution.py:41
  143.0 10.6 %term_part.7 = (bf16[2,2,528,256]{3,2,1,0:T(8,128)(2,1)}, bf16[2,2,528,256]{3,2,1,0:T(8,128)(2,1)}, bf16[2,2,528,256]{3,2,1,0:T(8,128)(2,1)}) custom-call(s32[14]{0:T(128)} %concatenate.3.ids, bf16[2,752,256]{2,1,0:T(8,128)(2,1)} %get-tuple-element.67.refs_0_, bf16[1024,1000]{1,0:T(8,128)(2,1)} %get-tuple-element.62.refs_0_.refs_1_, ...), custom_call_target="tpu_custom_call" | custom-call | flops 62914560000 | bytes 228229120 | tf_op jit(solution)/shard_map/term_part/pallas_call | solution.py:625
  153.6 3.2 %collective-permute-start.30 = (bf16[2,2,528,256]{3,2,1,0:T(8,128)(2,1)}, bf16[2,2,528,256]{3,2,1,0:T(8,128)(2,1)}, u32[]{:S(2)}, u32[]{:S(2)}) collective-permute-start(bf16[2,2,528,256]{3,2,1,0:T(8,128)(2,1)} %get-tuple-element.71), channel_id=1, source_target_pairs={{0,6},{2,0},{4,2},{6,4},{1,7},{3,1},{5,3},{7,5},{8,14},{10,8},{12,... | collective-permute-start | bytes 3244040 | tf_op jit(solution)/shard_map/ppermute | solution.py:37
  156.9 10.1 %head_part.4 = (bf16[2,2,752,256]{3,2,1,0:T(8,128)(2,1)}, bf16[2,2,752,256]{3,2,1,0:T(8,128)(2,1)}, bf16[2,2,248,256]{3,2,1,0:T(8,128)(2,1)}, bf16[2,2,248,256]{3,2,1,0:T(8,128)(2,1)}) custom-call(s32[14]{0:T(128)} %concatenate.3.ids, bf16[2,2,528,256]{3,2,1,0:T(8,128)(2,1)} %get-tuple-element.69.refs_0_, ...), custom_call_target="tpu_custom_call" | custom-call | flops 83886080000 | bytes 206766080 | tf_op jit(solution)/shard_map/head_part/pallas_call | solution.py:475
  167.7 3.2 %collective-permute-start.36 = (bf16[2,2,752,256]{3,2,1,0:T(8,128)(2,1)}, bf16[2,2,752,256]{3,2,1,0:T(8,128)(2,1)}, u32[]{:S(2)}, u32[]{:S(2)}) collective-permute-start(bf16[2,2,752,256]{3,2,1,0:T(8,128)(2,1)} %get-tuple-element.80), channel_id=1, source_target_pairs={{0,48},{16,0},{32,16},{48,32},{1,49},{17,1},{33,17},{49,33},{2,50}... | collective-permute-start | bytes 4620296 | tf_op jit(solution)/shard_map/ppermute | solution.py:37
  170.9 9.0 %collective-permute-done.29.refs_1_ = bf16[2,2,528,256]{3,2,1,0:T(8,128)(2,1)} collective-permute-done((bf16[2,2,528,256]{3,2,1,0:T(8,128)(2,1)}, bf16[2,2,528,256]{3,2,1,0:T(8,128)(2,1)}, u32[]{:S(2)}, u32[]{:S(2)}) %collective-permute-start.29) | collective-permute-done | bytes 1081376 | tf_op jit(solution)/shard_map/ppermute | solution.py:37
  179.9 3.6 %term_sum.1 = (bf16[1024,256]{1,0:T(8,128)(2,1)}, bf16[2,528,256]{2,1,0:T(8,128)(2,1)}, f32[16,256]{1,0:T(8,128)}, f32[2,256]{1,0:T(2,128)}) custom-call(bf16[2,2,528,256]{3,2,1,0:T(8,128)(2,1)} %get-tuple-element.69.refs_0_, bf16[2,2,528,256]{3,2,1,0:T(8,128)(2,1)} %collective-permute-done.29.refs_1_, ...), custom_call_target="tpu_custom_call" | custom-call | flops 20000 | bytes 100000 | tf_op jit(solution)/shard_map/term_sum/pallas_call | solution.py:671
  183.5 6.4 %head_part.5 = (bf16[2,2,752,256]{3,2,1,0:T(8,128)(2,1)}, bf16[1,2,248,256]{3,2,1,0:T(8,128)(2,1)}, bf16[1,2,248,256]{3,2,1,0:T(8,128)(2,1)}) custom-call(s32[14]{0:T(128)} %concatenate.3.ids, bf16[2,2,752,256]{3,2,1,0:T(8,128)(2,1)} %get-tuple-element.78.refs_0_, bf16[1024,256]{1,0:T(8,128)(2,1)} %get-tuple-element.72.refs_0_.refs_1_, ...), custom_call_target="tpu_custom_call" | custom-call | flops 41943040000 | bytes 123863040 | tf_op jit(solution)/shard_map/head_part/pallas_call | solution.py:475
  191.7 11.3 %collective-permute-done.35.ra = bf16[2,2,752,256]{3,2,1,0:T(8,128)(2,1)} collective-permute-done((bf16[2,2,752,256]{3,2,1,0:T(8,128)(2,1)}, bf16[2,2,752,256]{3,2,1,0:T(8,128)(2,1)}, u32[]{:S(2)}, u32[]{:S(2)}) %collective-permute-start.35) | collective-permute-done | bytes 1540128 | tf_op jit(solution)/shard_map/ppermute | solution.py:37
  203.0 2.6 %fusion = bf16[2,752,256]{2,1,0:T(8,128)(2,1)} fusion(bf16[2,2,752,256]{3,2,1,0:T(8,128)(2,1)} %collective-permute-done.36.rb, bf16[2,2,752,256]{3,2,1,0:T(8,128)(2,1)} %collective-permute-done.35.ra, bf16[2,2,752,256]{3,2,1,0:T(8,128)(2,1)} %get-tuple-element.79.a0), kind=kLoop, calls=%fused_computation.1 | loop fusion | flops 770048 | bytes 3080192 | tf_op jit(solution)/shard_map/add | solution.py:765
  205.6 2.7 %collective-permute-start.37 = (bf16[2,752,256]{2,1,0:T(8,128)(2,1)}, bf16[2,752,256]{2,1,0:T(8,128)(2,1)}, u32[]{:S(2)}, u32[]{:S(2)}) collective-permute-start(bf16[2,752,256]{2,1,0:T(8,128)(2,1)} %fusion), channel_id=1, source_target_pairs={{0,64},{64,0},{1,65},{65,1},{2,66},{66,2},{3,67},{67,3},{4,68},{68... | collective-permute-start | bytes 2310152 | tf_op jit(solution)/shard_map/ppermute | solution.py:41
  208.4 2.3 low_sum.1
  210.7 4.4 %collective-permute-start.41 = (bf16[2,264,256]{2,1,0:T(8,128)(2,1)}, bf16[2,264,256]{2,1,0:T(8,128)(2,1)}, u32[]{:S(2)}, u32[]{:S(2)}) collective-permute-start(bf16[2,264,256]{2,1,0:T(8,128)(2,1)} %get-tuple-element.88), channel_id=1, source_target_pairs={{0,32},{16,48},{32,0},{48,16},{1,33},{17,49},{33,1},{49,17},{2,34}... | collective-permute-start | bytes 811016 | tf_op jit(solution)/shard_map/ppermute | solution.py:37
  215.1 2.8 %hidden_grad.1._.refs_0_ = bf16[1024,256]{1,0:T(8,128)(2,1)} custom-call(s32[14]{0:T(128)} %concatenate.3.ids, bf16[1024,256]{1,0:T(8,128)(2,1)} %get-tuple-element.72.refs_0_.refs_1_, bf16[2,528,256]{2,1,0:T(8,128)(2,1)} %collective-permute-done.31.refs_1_, bf16[1024,256]{1,0:T(8,128)(2,1)} %refs_2_.1, f32[1,4096]{1,0:T(1,128)} %bitcast.34, ...), custom_call_target="tpu_custom_call" | custom-call | flops 20000 | bytes 40000 | tf_op jit(solution)/shard_map/hidden_grad/pallas_call | solution.py:703
  217.9 3.5 %collective-permute-done.40.b1.refs_3_ = bf16[2,264,256]{2,1,0:T(8,128)(2,1)} collective-permute-done((bf16[2,264,256]{2,1,0:T(8,128)(2,1)}, bf16[2,264,256]{2,1,0:T(8,128)(2,1)}, u32[]{:S(2)}, u32[]{:S(2)}) %collective-permute-start.40) | collective-permute-done | bytes 270368 | tf_op jit(solution)/shard_map/ppermute | solution.py:37
  221.4 2.9 %collective-permute-done.41.b2.refs_4_ = bf16[2,264,256]{2,1,0:T(8,128)(2,1)} collective-permute-done((bf16[2,264,256]{2,1,0:T(8,128)(2,1)}, bf16[2,264,256]{2,1,0:T(8,128)(2,1)}, u32[]{:S(2)}, u32[]{:S(2)}) %collective-permute-start.41) | collective-permute-done | bytes 270368 | tf_op jit(solution)/shard_map/ppermute | solution.py:37
  227.5 2.3 collective-permute-start.45
  231.1 1.5 collective-permute-done.45
  233.8 4.4 %join.1 = bf16[1000,512]{1,0:T(8,128)(2,1)} custom-call(s32[14]{0:T(128)} %concatenate.3.ids, bf16[1024,256]{1,0:T(8,128)(2,1)} %hidden_grad.1._.refs_0_, bf16[2,2,752,256]{3,2,1,0:T(8,128)(2,1)} %get-tuple-element.79.a0, bf16[2,2,752,256]{3,2,1,0:T(8,128)(2,1)} %collective-permute-done.35.ra, bf16[2,2,752,256]{3,2,1,0:T(8,128)(2,1)} %collective-permute-done.36.rb, ...), custom_call_target="tpu_custom_call" | custom-call | flops 20 | bytes 160000 | tf_op jit(solution)/shard_map/join/pallas_call | solution.py:562
  (85 shorter events, 23.2 us)
Async XLA Ops:
  0.6 16.4 %collective-permute-start.3 = (bf16[1024,256]{1,0:T(8,128)(2,1)}, bf16[1024,256]{1,0:T(8,128)(2,1)}, u32[]{:S(2)}, u32[]{:S(2)}) collective-permute-start(bf16[1024,256]{1,0:T(8,128)(2,1)} %refs_2_.1), channel_id=1, source_target_pairs={{0,2},{2,4},{4,6},{6,0},{1,3},{3,5},{5,7},{7,1},{8,10},{10,12},{12... | collective-permute-start | bytes 1572872 | tf_op jit(solution)/shard_map/ppermute | solution.py:37
  2.7 14.4 %collective-permute-start.5 = (bf16[1024,256]{1,0:T(8,128)(2,1)}, bf16[1024,256]{1,0:T(8,128)(2,1)}, u32[]{:S(2)}, u32[]{:S(2)}) collective-permute-start(bf16[1024,256]{1,0:T(8,128)(2,1)} %refs_2_.1), channel_id=1, source_target_pairs={{0,8},{8,0},{1,9},{9,1},{2,10},{10,2},{3,11},{11,3},{4,12},{12,4},... | collective-permute-start | bytes 1572872 | tf_op jit(solution)/shard_map/ppermute | solution.py:41
  4.2 14.1 %collective-permute-start.2 = (bf16[1024,256]{1,0:T(8,128)(2,1)}, bf16[1024,256]{1,0:T(8,128)(2,1)}, u32[]{:S(2)}, u32[]{:S(2)}) collective-permute-start(bf16[1024,256]{1,0:T(8,128)(2,1)} %refs_2_.1), channel_id=1, source_target_pairs={{0,1},{1,0},{2,3},{3,2},{4,5},{5,4},{6,7},{7,6},{8,9},{9,8},{10,11... | collective-permute-start | bytes 1572872 | tf_op jit(solution)/shard_map/ppermute | solution.py:41
  4.2 16.6 %collective-permute-start = (bf16[1024,256]{1,0:T(8,128)(2,1)}, bf16[1024,256]{1,0:T(8,128)(2,1)}, u32[]{:S(2)}, u32[]{:S(2)}) collective-permute-start(bf16[1024,256]{1,0:T(8,128)(2,1)} %refs_2_.1), channel_id=1, source_target_pairs={{0,6},{2,0},{4,2},{6,4},{1,7},{3,1},{5,3},{7,5},{8,14},{10,8},{12,... | collective-permute-start | bytes 1572872 | tf_op jit(solution)/shard_map/ppermute | solution.py:37
  17.1 7.3 %collective-permute-start.4 = (bf16[1024,256]{1,0:T(8,128)(2,1)}, bf16[1024,256]{1,0:T(8,128)(2,1)}, u32[]{:S(2)}, u32[]{:S(2)}) collective-permute-start(bf16[1024,256]{1,0:T(8,128)(2,1)} %collective-permute-done.3.refs_2_), channel_id=1, source_target_pairs={{0,1},{1,0},{2,3},{3,2},{4,5},{5,4},{6,7},{7,6},{8,9},{9,8},{10,11... | collective-permute-start | bytes 1572872 | tf_op jit(solution)/shard_map/ppermute | solution.py:41
  17.1 7.3 %collective-permute-start.6 = (bf16[1024,256]{1,0:T(8,128)(2,1)}, bf16[1024,256]{1,0:T(8,128)(2,1)}, u32[]{:S(2)}, u32[]{:S(2)}) collective-permute-start(bf16[1024,256]{1,0:T(8,128)(2,1)} %collective-permute-done.5.refs_4_), channel_id=1, source_target_pairs={{0,1},{1,0},{2,3},{3,2},{4,5},{5,4},{6,7},{7,6},{8,9},{9,8},{10,11... | collective-permute-start | bytes 1572872 | tf_op jit(solution)/shard_map/ppermute | solution.py:41
  17.6 16.9 %collective-permute-start.7 = (bf16[1024,256]{1,0:T(8,128)(2,1)}, bf16[1024,256]{1,0:T(8,128)(2,1)}, u32[]{:S(2)}, u32[]{:S(2)}) collective-permute-start(bf16[1024,256]{1,0:T(8,128)(2,1)} %collective-permute-done.3.refs_2_), channel_id=1, source_target_pairs={{0,2},{2,4},{4,6},{6,0},{1,3},{3,5},{5,7},{7,1},{8,10},{10,12},{12... | collective-permute-start | bytes 1572872 | tf_op jit(solution)/shard_map/ppermute | solution.py:37
  18.3 16.1 %collective-permute-start.8 = (bf16[1024,256]{1,0:T(8,128)(2,1)}, bf16[1024,256]{1,0:T(8,128)(2,1)}, u32[]{:S(2)}, u32[]{:S(2)}) collective-permute-start(bf16[1024,256]{1,0:T(8,128)(2,1)} %collective-permute-done.5.refs_4_), channel_id=1, source_target_pairs={{0,6},{2,0},{4,2},{6,4},{1,7},{3,1},{5,3},{7,5},{8,14},{10,8},{12,... | collective-permute-start | bytes 1572872 | tf_op jit(solution)/shard_map/ppermute | solution.py:37
  20.8 13.6 %collective-permute-start.9 = (bf16[1024,256]{1,0:T(8,128)(2,1)}, bf16[1024,256]{1,0:T(8,128)(2,1)}, u32[]{:S(2)}, u32[]{:S(2)}) collective-permute-start(bf16[1024,256]{1,0:T(8,128)(2,1)} %collective-permute-done.3.refs_2_), channel_id=1, source_target_pairs={{0,8},{8,0},{1,9},{9,1},{2,10},{10,2},{3,11},{11,3},{4,12},{12,4},... | collective-permute-start | bytes 1572872 | tf_op jit(solution)/shard_map/ppermute | solution.py:41
  24.4 12.1 %collective-permute-start.1 = (bf16[1024,256]{1,0:T(8,128)(2,1)}, bf16[1024,256]{1,0:T(8,128)(2,1)}, u32[]{:S(2)}, u32[]{:S(2)}) collective-permute-start(bf16[1024,256]{1,0:T(8,128)(2,1)} %collective-permute-done.refs_0_), channel_id=1, source_target_pairs={{0,1},{1,0},{2,3},{3,2},{4,5},{5,4},{6,7},{7,6},{8,9},{9,8},{10,11... | collective-permute-start | bytes 1572872 | tf_op jit(solution)/shard_map/ppermute | solution.py:41
  34.5 2.4 %collective-permute-start.10 = (bf16[1024,256]{1,0:T(8,128)(2,1)}, bf16[1024,256]{1,0:T(8,128)(2,1)}, u32[]{:S(2)}, u32[]{:S(2)}) collective-permute-start(bf16[1024,256]{1,0:T(8,128)(2,1)} %get-tuple-element.48.refs_2_), channel_id=1, source_target_pairs={{0,1},{1,0},{2,3},{3,2},{4,5},{5,4},{6,7},{7,6},{8,9},{9,8},{10,11... | collective-permute-start | bytes 1572872 | tf_op jit(solution)/shard_map/ppermute | solution.py:41
  35.0 2.6 %collective-permute-start.11 = (bf16[1024,256]{1,0:T(8,128)(2,1)}, bf16[1024,256]{1,0:T(8,128)(2,1)}, u32[]{:S(2)}, u32[]{:S(2)}) collective-permute-start(bf16[1024,256]{1,0:T(8,128)(2,1)} %get-tuple-element.49.refs_4_), channel_id=1, source_target_pairs={{0,1},{1,0},{2,3},{3,2},{4,5},{5,4},{6,7},{7,6},{8,9},{9,8},{10,11... | collective-permute-start | bytes 1572872 | tf_op jit(solution)/shard_map/ppermute | solution.py:41
  35.1 3.3 %collective-permute-start.12 = (bf16[1024,256]{1,0:T(8,128)(2,1)}, bf16[1024,256]{1,0:T(8,128)(2,1)}, u32[]{:S(2)}, u32[]{:S(2)}) collective-permute-start(bf16[1024,256]{1,0:T(8,128)(2,1)} %get-tuple-element.50.refs_6_), channel_id=1, source_target_pairs={{0,1},{1,0},{2,3},{3,2},{4,5},{5,4},{6,7},{7,6},{8,9},{9,8},{10,11... | collective-permute-start | bytes 1572872 | tf_op jit(solution)/shard_map/ppermute | solution.py:41
  35.6 15.9 %collective-permute-start.13 = (bf16[1024,256]{1,0:T(8,128)(2,1)}, bf16[1024,256]{1,0:T(8,128)(2,1)}, u32[]{:S(2)}, u32[]{:S(2)}) collective-permute-start(bf16[1024,256]{1,0:T(8,128)(2,1)} %get-tuple-element.48.refs_2_), channel_id=1, source_target_pairs={{0,8},{8,0},{1,9},{9,1},{2,10},{10,2},{3,11},{11,3},{4,12},{12,4},... | collective-permute-start | bytes 1572872 | tf_op jit(solution)/shard_map/ppermute | solution.py:41
  51.5 2.3 collective-permute-start.14
  66.1 5.7 %collective-permute-start.15 = (f32[8,1024]{1,0:T(8,128)}, f32[8,1024]{1,0:T(8,128)S(1)}, u32[]{:S(2)}, u32[]{:S(2)}) collective-permute-start(f32[8,1024]{1,0:T(8,128)} %get-tuple-element.56), channel_id=1, source_target_pairs={{0,64},{64,0},{1,65},{65,1},{2,66},{66,2},{3,67},{67,3},{4,68},{68... | collective-permute-start | bytes 98312 | tf_op jit(solution)/shard_map/ppermute | solution.py:41
  72.6 4.5 %copy-start = (f32[2,8,1024]{2,1,0:T(8,128)}, f32[2,8,1024]{2,1,0:T(8,128)S(1)}, u32[]{:S(2)}) copy-start(f32[2,8,1024]{2,1,0:T(8,128)S(1)} %pad_maximum_fusion.refs_0_) | copy-start | bytes 196612
  72.6 4.7 %collective-permute-start.16 = (f32[2,8,1024]{2,1,0:T(8,128)S(1)}, f32[2,8,1024]{2,1,0:T(8,128)S(1)}, u32[]{:S(2)}, u32[]{:S(2)}) collective-permute-start(f32[2,8,1024]{2,1,0:T(8,128)S(1)} %pad_maximum_fusion.refs_0_), channel_id=1, source_target_pairs={{0,16},{16,0},{32,48},{48,32},{1,17},{17,1},{33,49},{49,33},{2,18}... | collective-permute-start | bytes 196616 | tf_op jit(solution)/shard_map/ppermute | solution.py:41
  74.1 5.9 %collective-permute-start.17 = (f32[2,8,1024]{2,1,0:T(8,128)S(1)}, f32[2,8,1024]{2,1,0:T(8,128)S(1)}, u32[]{:S(2)}, u32[]{:S(2)}) collective-permute-start(f32[2,8,1024]{2,1,0:T(8,128)S(1)} %pad_maximum_fusion.refs_0_), channel_id=1, source_target_pairs={{0,32},{16,48},{32,0},{48,16},{1,33},{17,49},{33,1},{49,17},{2,34}... | collective-permute-start | bytes 196616 | tf_op jit(solution)/shard_map/ppermute | solution.py:41
  77.1 5.6 %collective-permute-start.18 = (f32[2,8,1024]{2,1,0:T(8,128)S(1)}, f32[2,8,1024]{2,1,0:T(8,128)}, u32[]{:S(2)}, u32[]{:S(2)}) collective-permute-start(f32[2,8,1024]{2,1,0:T(8,128)S(1)} %pad_maximum_fusion.refs_0_), channel_id=1, source_target_pairs={{0,48},{16,32},{32,16},{48,0},{1,49},{17,33},{33,17},{49,1},{2,50}... | collective-permute-start | bytes 196616 | tf_op jit(solution)/shard_map/ppermute | solution.py:41
  85.3 4.7 %collective-permute-start.19 = (f32[72,128]{1,0:T(8,128)}, f32[72,128]{1,0:T(8,128)S(1)}, u32[]{:S(2)}, u32[]{:S(2)}) collective-permute-start(f32[72,128]{1,0:T(8,128)} %get-tuple-element.58), channel_id=1, source_target_pairs={{0,2},{2,0},{4,6},{6,4},{1,3},{3,1},{5,7},{7,5},{8,10},{10,8},{12,... | collective-permute-start | bytes 110600 | tf_op jit(solution)/shard_map/ppermute | solution.py:41
  85.3 5.7 %collective-permute-start.20 = (f32[72,128]{1,0:T(8,128)}, f32[72,128]{1,0:T(8,128)S(1)}, u32[]{:S(2)}, u32[]{:S(2)}) collective-permute-start(f32[72,128]{1,0:T(8,128)} %get-tuple-element.58), channel_id=1, source_target_pairs={{0,4},{2,6},{4,0},{6,2},{1,5},{3,7},{5,1},{7,3},{8,12},{10,14},{12... | collective-permute-start | bytes 110600 | tf_op jit(solution)/shard_map/ppermute | solution.py:41
  88.2 5.4 %collective-permute-start.21 = (f32[72,128]{1,0:T(8,128)}, f32[72,128]{1,0:T(8,128)S(1)}, u32[]{:S(2)}, u32[]{:S(2)}) collective-permute-start(f32[72,128]{1,0:T(8,128)} %get-tuple-element.58), channel_id=1, source_target_pairs={{0,6},{2,4},{4,2},{6,0},{1,7},{3,5},{5,3},{7,1},{8,14},{10,12},{12... | collective-permute-start | bytes 110600 | tf_op jit(solution)/shard_map/ppermute | solution.py:41
  94.3 5.4 %copy-start.1 = (f32[72,128]{1,0:T(8,128)}, f32[72,128]{1,0:T(8,128)S(1)}, u32[]{:S(2)}) copy-start(f32[72,128]{1,0:T(8,128)S(1)} %add_add_fusion.p0) | copy-start | bytes 110596
  94.3 2.0 collective-permute-start.22
  94.4 4.0 %collective-permute-start.23 = (f32[72,128]{1,0:T(8,128)S(1)}, f32[72,128]{1,0:T(8,128)S(1)}, u32[]{:S(2)}, u32[]{:S(2)}) collective-permute-start(f32[72,128]{1,0:T(8,128)S(1)} %add_add_fusion.p0), channel_id=1, source_target_pairs={{0,8},{8,0},{1,9},{9,1},{2,10},{10,2},{3,11},{11,3},{4,12},{12,4},... | collective-permute-start | bytes 110600 | tf_op jit(solution)/shard_map/ppermute | solution.py:41
  95.7 3.4 %collective-permute-start.24 = (f32[72,128]{1,0:T(8,128)S(1)}, f32[72,128]{1,0:T(8,128)S(1)}, u32[]{:S(2)}, u32[]{:S(2)}) collective-permute-start(f32[72,128]{1,0:T(8,128)S(1)} %add_add_fusion.p0), channel_id=1, source_target_pairs={{0,9},{1,8},{8,1},{9,0},{2,11},{3,10},{10,3},{11,2},{4,13},{5,12},... | collective-permute-start | bytes 110600 | tf_op jit(solution)/shard_map/ppermute | solution.py:744
  111.0 8.3 %collective-permute-start.25 = (bf16[1,2,2,528,256]{4,3,2,1,0:T(8,128)(2,1)}, bf16[1,2,2,528,256]{4,3,2,1,0:T(8,128)(2,1)}, u32[]{:S(2)}, u32[]{:S(2)}) collective-permute-start(bf16[1,2,2,528,256]{4,3,2,1,0:T(8,128)(2,1)} %term_part.4.refs_0_), channel_id=1, source_target_pairs={{0,1},{1,0},{2,3},{3,2},{4,5},{5,4},{6,7},{7,6},{8,9},{9,8},{10,11... | collective-permute-start | bytes 3244040 | tf_op jit(solution)/shard_map/ppermute | solution.py:41
  118.9 24.0 %collective-permute-start.26 = (bf16[3,2,2,528,256]{4,3,2,1,0:T(8,128)(2,1)}, bf16[3,2,2,528,256]{4,3,2,1,0:T(8,128)(2,1)}, u32[]{:S(2)}, u32[]{:S(2)}) collective-permute-start(bf16[3,2,2,528,256]{4,3,2,1,0:T(8,128)(2,1)} %term_part.5.refs_0_), channel_id=1, source_target_pairs={{0,1},{1,0},{2,3},{3,2},{4,5},{5,4},{6,7},{7,6},{8,9},{9,8},{10,11... | collective-permute-start | bytes 9732104 | tf_op jit(solution)/shard_map/ppermute | solution.py:41
  124.4 15.9 %collective-permute-start.27 = (bf16[2,528,256]{2,1,0:T(8,128)(2,1)}, bf16[2,528,256]{2,1,0:T(8,128)(2,1)}, u32[]{:S(2)}, u32[]{:S(2)}) collective-permute-start(bf16[2,528,256]{2,1,0:T(8,128)(2,1)} %get-tuple-element.64.refs_0_), channel_id=1, source_target_pairs={{0,2},{2,4},{4,6},{6,0},{1,3},{3,5},{5,7},{7,1},{8,10},{10,12},{12... | collective-permute-start | bytes 1622024 | tf_op jit(solution)/shard_map/ppermute | solution.py:37
  124.4 18.6 %collective-permute-start.28 = (bf16[2,528,256]{2,1,0:T(8,128)(2,1)}, bf16[2,528,256]{2,1,0:T(8,128)(2,1)}, u32[]{:S(2)}, u32[]{:S(2)}) collective-permute-start(bf16[2,528,256]{2,1,0:T(8,128)(2,1)} %get-tuple-element.68), channel_id=1, source_target_pairs={{0,6},{2,0},{4,2},{6,4},{1,7},{3,1},{5,3},{7,5},{8,14},{10,8},{12,... | collective-permute-start | bytes 1622024 | tf_op jit(solution)/shard_map/ppermute | solution.py:37
  134.0 22.8 %collective-permute-start.33 = (bf16[2,752,256]{2,1,0:T(8,128)(2,1)}, bf16[2,752,256]{2,1,0:T(8,128)(2,1)}, u32[]{:S(2)}, u32[]{:S(2)}) collective-permute-start(bf16[2,752,256]{2,1,0:T(8,128)(2,1)} %get-tuple-element.67.refs_0_), channel_id=1, source_target_pairs={{0,16},{16,32},{32,48},{48,0},{1,17},{17,33},{33,49},{49,1},{2,18}... | collective-permute-start | bytes 2310152 | tf_op jit(solution)/shard_map/ppermute | solution.py:37
  134.0 22.8 %collective-permute-start.34 = (bf16[2,752,256]{2,1,0:T(8,128)(2,1)}, bf16[2,752,256]{2,1,0:T(8,128)(2,1)}, u32[]{:S(2)}, u32[]{:S(2)}) collective-permute-start(bf16[2,752,256]{2,1,0:T(8,128)(2,1)} %get-tuple-element.77), channel_id=1, source_target_pairs={{0,48},{16,0},{32,16},{48,32},{1,49},{17,1},{33,17},{49,33},{2,50}... | collective-permute-start | bytes 2310152 | tf_op jit(solution)/shard_map/ppermute | solution.py:37
  140.2 16.6 %collective-permute-start.32 = (bf16[1,2,248,256]{3,2,1,0:T(8,128)(2,1)}, bf16[1,2,248,256]{3,2,1,0:T(8,128)(2,1)}, u32[]{:S(2)}, u32[]{:S(2)}) collective-permute-start(bf16[1,2,248,256]{3,2,1,0:T(8,128)(2,1)} %get-tuple-element.76), channel_id=1, source_target_pairs={{0,64},{64,0},{1,65},{65,1},{2,66},{66,2},{3,67},{67,3},{4,68},{68... | collective-permute-start | bytes 761864 | tf_op jit(solution)/shard_map/ppermute | solution.py:41
  153.6 26.3 %collective-permute-start.29 = (bf16[2,2,528,256]{3,2,1,0:T(8,128)(2,1)}, bf16[2,2,528,256]{3,2,1,0:T(8,128)(2,1)}, u32[]{:S(2)}, u32[]{:S(2)}) collective-permute-start(bf16[2,2,528,256]{3,2,1,0:T(8,128)(2,1)} %get-tuple-element.70), channel_id=1, source_target_pairs={{0,2},{2,4},{4,6},{6,0},{1,3},{3,5},{5,7},{7,1},{8,10},{10,12},{12... | collective-permute-start | bytes 3244040 | tf_op jit(solution)/shard_map/ppermute | solution.py:37
  153.6 26.3 %collective-permute-start.30 = (bf16[2,2,528,256]{3,2,1,0:T(8,128)(2,1)}, bf16[2,2,528,256]{3,2,1,0:T(8,128)(2,1)}, u32[]{:S(2)}, u32[]{:S(2)}) collective-permute-start(bf16[2,2,528,256]{3,2,1,0:T(8,128)(2,1)} %get-tuple-element.71), channel_id=1, source_target_pairs={{0,6},{2,0},{4,2},{6,4},{1,7},{3,1},{5,3},{7,5},{8,14},{10,8},{12,... | collective-permute-start | bytes 3244040 | tf_op jit(solution)/shard_map/ppermute | solution.py:37
  166.9 41.4 %collective-permute-start.39 = (bf16[2,2,248,256]{3,2,1,0:T(8,128)(2,1)}, bf16[2,2,248,256]{3,2,1,0:T(8,128)(2,1)}, u32[]{:S(2)}, u32[]{:S(2)}) collective-permute-start(bf16[2,2,248,256]{3,2,1,0:T(8,128)(2,1)} %get-tuple-element.85), channel_id=1, source_target_pairs={{0,64},{64,0},{1,65},{65,1},{2,66},{66,2},{3,67},{67,3},{4,68},{68... | collective-permute-start | bytes 1523720 | tf_op jit(solution)/shard_map/ppermute | solution.py:41
  167.7 35.3 %collective-permute-start.35 = (bf16[2,2,752,256]{3,2,1,0:T(8,128)(2,1)}, bf16[2,2,752,256]{3,2,1,0:T(8,128)(2,1)}, u32[]{:S(2)}, u32[]{:S(2)}) collective-permute-start(bf16[2,2,752,256]{3,2,1,0:T(8,128)(2,1)} %get-tuple-element.78.refs_0_), channel_id=1, source_target_pairs={{0,16},{16,32},{32,48},{48,0},{1,17},{17,33},{33,49},{49,1},{2,18}... | collective-permute-start | bytes 4620296 | tf_op jit(solution)/shard_map/ppermute | solution.py:37
  167.7 35.3 %collective-permute-start.36 = (bf16[2,2,752,256]{3,2,1,0:T(8,128)(2,1)}, bf16[2,2,752,256]{3,2,1,0:T(8,128)(2,1)}, u32[]{:S(2)}, u32[]{:S(2)}) collective-permute-start(bf16[2,2,752,256]{3,2,1,0:T(8,128)(2,1)} %get-tuple-element.80), channel_id=1, source_target_pairs={{0,48},{16,0},{32,16},{48,32},{1,49},{17,1},{33,17},{49,33},{2,50}... | collective-permute-start | bytes 4620296 | tf_op jit(solution)/shard_map/ppermute | solution.py:37
  189.9 18.4 %collective-permute-start.38 = (bf16[1,2,248,256]{3,2,1,0:T(8,128)(2,1)}, bf16[1,2,248,256]{3,2,1,0:T(8,128)(2,1)}, u32[]{:S(2)}, u32[]{:S(2)}) collective-permute-start(bf16[1,2,248,256]{3,2,1,0:T(8,128)(2,1)} %get-tuple-element.82), channel_id=1, source_target_pairs={{0,64},{64,0},{1,65},{65,1},{2,66},{66,2},{3,67},{67,3},{4,68},{68... | collective-permute-start | bytes 761864 | tf_op jit(solution)/shard_map/ppermute | solution.py:41
  190.7 24.4 %collective-permute-start.31 = (bf16[2,528,256]{2,1,0:T(8,128)(2,1)}, bf16[2,528,256]{2,1,0:T(8,128)(2,1)}, u32[]{:S(2)}, u32[]{:S(2)}) collective-permute-start(bf16[2,528,256]{2,1,0:T(8,128)(2,1)} %get-tuple-element.73), channel_id=1, source_target_pairs={{0,8},{8,0},{1,9},{9,1},{2,10},{10,2},{3,11},{11,3},{4,12},{12,4},... | collective-permute-start | bytes 1622024 | tf_op jit(solution)/shard_map/ppermute | solution.py:41
  205.6 28.2 %collective-permute-start.37 = (bf16[2,752,256]{2,1,0:T(8,128)(2,1)}, bf16[2,752,256]{2,1,0:T(8,128)(2,1)}, u32[]{:S(2)}, u32[]{:S(2)}) collective-permute-start(bf16[2,752,256]{2,1,0:T(8,128)(2,1)} %fusion), channel_id=1, source_target_pairs={{0,64},{64,0},{1,65},{65,1},{2,66},{66,2},{3,67},{67,3},{4,68},{68... | collective-permute-start | bytes 2310152 | tf_op jit(solution)/shard_map/ppermute | solution.py:41
  210.7 10.7 %collective-permute-start.40 = (bf16[2,264,256]{2,1,0:T(8,128)(2,1)}, bf16[2,264,256]{2,1,0:T(8,128)(2,1)}, u32[]{:S(2)}, u32[]{:S(2)}) collective-permute-start(bf16[2,264,256]{2,1,0:T(8,128)(2,1)} %get-tuple-element.87), channel_id=1, source_target_pairs={{0,16},{16,32},{32,48},{48,0},{1,17},{17,33},{33,49},{49,1},{2,18}... | collective-permute-start | bytes 811016 | tf_op jit(solution)/shard_map/ppermute | solution.py:37
  210.7 13.6 %collective-permute-start.41 = (bf16[2,264,256]{2,1,0:T(8,128)(2,1)}, bf16[2,264,256]{2,1,0:T(8,128)(2,1)}, u32[]{:S(2)}, u32[]{:S(2)}) collective-permute-start(bf16[2,264,256]{2,1,0:T(8,128)(2,1)} %get-tuple-element.88), channel_id=1, source_target_pairs={{0,32},{16,48},{32,0},{48,16},{1,33},{17,49},{33,1},{49,17},{2,34}... | collective-permute-start | bytes 811016 | tf_op jit(solution)/shard_map/ppermute | solution.py:37
  215.1 9.2 %collective-permute-start.42 = (bf16[2,264,256]{2,1,0:T(8,128)(2,1)}, bf16[2,264,256]{2,1,0:T(8,128)(2,1)}, u32[]{:S(2)}, u32[]{:S(2)}) collective-permute-start(bf16[2,264,256]{2,1,0:T(8,128)(2,1)} %get-tuple-element.89), channel_id=1, source_target_pairs={{0,48},{16,0},{32,16},{48,32},{1,49},{17,1},{33,17},{49,33},{2,50}... | collective-permute-start | bytes 811016 | tf_op jit(solution)/shard_map/ppermute | solution.py:37
  225.7 5.4 %collective-permute-start.43 = (f32[8,256]{1,0:T(8,128)}, f32[8,256]{1,0:T(8,128)S(1)}, u32[]{:S(2)}, u32[]{:S(2)}) collective-permute-start(f32[8,256]{1,0:T(8,128)} %gain_along_y.1), channel_id=1, source_target_pairs={{0,64},{64,0},{1,65},{65,1},{2,66},{66,2},{3,67},{67,3},{4,68},{68... | collective-permute-start | bytes 24584 | tf_op jit(solution)/shard_map/ppermute | solution.py:41
  226.5 4.6 %collective-permute-start.44 = (f32[8,256]{1,0:T(8,128)}, f32[8,256]{1,0:T(8,128)S(1)}, u32[]{:S(2)}, u32[]{:S(2)}) collective-permute-start(f32[8,256]{1,0:T(8,128)} %gain_along_y.1), channel_id=1, source_target_pairs={{0,8},{8,0},{1,9},{9,1},{2,10},{10,2},{3,11},{11,3},{4,12},{12,4},... | collective-permute-start | bytes 24584 | tf_op jit(solution)/shard_map/ppermute | solution.py:41
  227.5 5.1 %collective-permute-start.45 = (f32[8,256]{1,0:T(8,128)}, f32[8,256]{1,0:T(8,128)S(1)}, u32[]{:S(2)}, u32[]{:S(2)}) collective-permute-start(f32[8,256]{1,0:T(8,128)} %gain_along_y.1), channel_id=1, source_target_pairs={{0,72},{8,64},{64,8},{72,0},{1,73},{9,65},{65,9},{73,1},{2,74},{10... | collective-permute-start | bytes 24584 | tf_op jit(solution)/shard_map/ppermute | solution.py:770
  (5 other events, 7.6 us)
